TPU v7x, 256 devices: a whole 4x4x8 slice. The times are simulated.
256 devices in a mesh: section: 8 (over x_hi, y), dp: 32 (over x_lo, z, core).
Axes of the slice: x: 4 (x_hi: 2, x_lo: 2; x = x_hi * 2 + x_lo), y: 4, z: 8, core: 2. Of those that a mesh axis runs over, the one named last changes fastest.
Arguments:
- section_rows: bfloat16 [8, 8192, 2048], P('section', 'dp'), may hold values from -160 to 160
- kv_weight: bfloat16 [8, 2048, 4096], P('section', 'dp'), may hold values from -0.125 to 0.125
- cotangent: bfloat16 [8, 8192, 2048], P('section', 'dp'), may hold values from -6 to 6
- gain: float32 [2048], replicated, may hold values from 0.1 to 1.9
- section_map: int32 [8], replicated, may hold values from 0 to 31, as said below
Outputs:
- section_out: bfloat16 [8, 8192, 2048], P('section', 'dp')
- section_grad: bfloat16 [8, 8192, 2048], P('section', 'dp')
- gain_grad: float32 [2048], replicated
Inputs may be any that keep to these rules, and one draw needn't show every extreme that they name: `section_map`: the entries are distinct; exactly one is 0 and marks the section of the encoder's last layer, every other section holds one decoder layer.
All inputs are finite; a program needn't handle non-finite values.
Results may differ from a plain program's by a relative error of at most 0.01.
The roundings to bfloat16 on the way count: a program that leaves them out, or rounds other values in their place, can miss the bound.
Values may be sent and summed in bfloat16 or wider, within the bound.
No kernel may reach another device: no remote copies, remote signals or barrier semaphores. Data moves between devices by JAX's collectives and lax.ppermute only.
A program may use at most 128 MiB of HBM per device.

v0:
```python
import functools
import math

import jax
import jax.numpy as jnp
from jax import lax
from jax.experimental import pallas as pl
from jax.experimental.pallas import tpu as pltpu
from jax.sharding import PartitionSpec as P

HEAD = 256
LEN = 256
D = 2048
HALF = 4
F = HALF * HEAD
QUARTER = LEN // 4
PIECE = LEN // 2

eps = 1e-06
bf16 = jnp.bfloat16
f32 = jnp.float32

SLOTS = (
    (0, 0), (0, 1), (0, -1), (1, 0), (0, 2), (0, -2), (1, 1), (0, 3),
    (0, -3), (1, -2), (0, 4), (1, 2), (1, -3), (1, 3), (1, -1), (1, 4),
)
N_SLOT = len(SLOTS)
SLOT = D // N_SLOT

ANY = pl.BlockSpec(memory_space=pl.ANY)
VMEM = pl.BlockSpec(memory_space=pltpu.VMEM)
SMEM = pl.BlockSpec(memory_space=pltpu.SMEM)
MIB = 1024 * 1024


def dp_swap(x, move):
    pairs = []
    for index in range(32):
        column, place, core = index // 16, (index // 2) % 8, index % 2
        column, place, core = move(column, place, core)
        pairs.append((index, (column % 2) * 16 + (place % 8) * 2 + core % 2))
    return lax.ppermute(x, "dp", pairs)


def section_swap(x, move):
    pairs = []
    for index in range(8):
        high, y = move(index // 4, index % 4)
        pairs.append((index, (high % 2) * 4 + y % 4))
    return lax.ppermute(x, "section", pairs)


def other_core(x):
    return dp_swap(x, lambda c, z, k: (c, z, k + 1))


def other_column(x):
    return dp_swap(x, lambda c, z, k: (c + 1, z, k))


def from_above(x):
    return dp_swap(x, lambda c, z, k: (c, z - 1, k))


def from_below(x):
    return dp_swap(x, lambda c, z, k: (c, z + 1, k))


def other_high(x):
    return section_swap(x, lambda h, y: (h + 1, y))


def other_y(x, bits):
    return section_swap(x, lambda h, y: (h, y ^ bits))


def join_kernel(*refs):
    del refs


class Order:
    def __init__(self, token):
        self.token = token

    def take(self, *arrays):
        arrays = arrays + (self.token,)
        count = len(arrays)
        *arrays, self.token = pl.pallas_call(
            join_kernel,
            in_specs=[ANY] * count,
            out_specs=[ANY] * count,
            out_shape=[jax.ShapeDtypeStruct(x.shape, x.dtype) for x in arrays],
            input_output_aliases={i: i for i in range(count)},
            compiler_params=pltpu.CompilerParams(vmem_limit_bytes=MIB),
            cost_estimate=pl.CostEstimate(flops=0, bytes_accessed=1024, transcendentals=0),
            name="join",
        )(*arrays)
        return arrays[0] if count == 2 else arrays


def core_index():
    return lax.axis_index("dp") % 2


def y_index():
    return lax.axis_index("section") % 4


def root_of(map_ref):
    root = jnp.int32(0)
    for index in range(8):
        root = jnp.where(map_ref[index] == 0, index, root)
    return root


def is_encoder(map_ref):
    return root_of(map_ref) == lax.axis_index("section")


def row_block(index, size):
    return pl.ds(pl.multiple_of(index * size, size), size)


def copy_all(pairs, sems):
    copies = [pltpu.make_async_copy(source, target, sems.at[i]) for i, (source, target) in enumerate(pairs)]
    for copy in copies:
        copy.start()
    for copy in copies:
        copy.wait()


def columns_kernel(w_ref, keep_ref, give_ref, token_ref, sems):
    core = core_index()
    token_ref[...] = jnp.zeros_like(token_ref)
    copy_all([
        (w_ref.at[:, row_block(side * 2 + which, F)], ref.at[:, pl.ds(side * F, F)])
        for ref, which in ((give_ref, 1 - core), (keep_ref, core))
        for side in range(2)
    ], sems)


def unit_kernel(keep_ref, got_ref, unit_ref, sems):
    core = core_index()
    copy_all([
        (keep_ref, unit_ref.at[row_block(core, SLOT // 2), :]),
        (got_ref, unit_ref.at[row_block(1 - core, SLOT // 2), :]),
    ], sems)


def half_kernel(rows_ref, half_ref, sems):
    copy_all([(rows_ref.at[row_block((y_index() // 2) ^ 1, 2 * QUARTER), :], half_ref)], sems)


def give_kernel(rows_ref, cot_ref, token_ref, give_ref, sems):
    del token_ref
    cols = row_block(1 - core_index(), F)
    copy_all([
        (rows_ref.at[:, cols], give_ref.at[:, pl.ds(0, F)]),
        (cot_ref.at[:, cols], give_ref.at[:, pl.ds(F, F)]),
    ], sems)


def select_kernel(step, map_ref, own_ref, got_ref, *outs):
    y, root = y_index(), root_of(map_ref)
    if step == 0:
        mine = y // 2 == root % 4 // 2
        keep_ref, send_ref = outs
        for ref, quarter in ((keep_ref, y), (send_ref, y ^ 1)):
            ref[...] = jnp.where(mine, own_ref[row_block(quarter, QUARTER), :], got_ref[row_block(quarter % 2, QUARTER), :])
    elif step == 1:
        outs[0][...] = jnp.where(y % 2 == root % 2, own_ref[...], got_ref[...])
    else:
        outs[0][...] = jnp.where(lax.axis_index("section") // 4 == root // 4, own_ref[...], got_ref[...])


def stack_kernel(*refs):
    *parts, out_ref = refs
    rows = out_ref.shape[0] // len(parts)
    for index, part in enumerate(parts):
        out_ref[index * rows:(index + 1) * rows, :] = part[...]


def add_kernel(a_ref, b_ref, out_ref):
    out_ref[...] = a_ref[...] + b_ref[...]


def slot_column(column, offset):
    dp = lax.axis_index("dp")
    column = (dp // 16 + column) % 2
    place = ((dp // 2) % 8 + offset + 8) % 8
    return pl.multiple_of((column * 8 + place) * SLOT, SLOT)


def norm_block(ref, gain_ref, enc_ref, inv_ref):
    @pl.loop(0, PIECE // QUARTER)
    def _(block):
        rows = row_block(block, QUARTER)
        hidden = ref[rows, :].astype(f32)
        inv = lax.rsqrt(jnp.mean(hidden * hidden, axis=1, keepdims=True) + eps)
        inv_ref[rows, :] = jnp.broadcast_to(inv, (QUARTER, 128))
        for slot in range(N_SLOT):
            cols = pl.ds(slot_column(*SLOTS[slot]), SLOT)
            part = ref[rows, cols].astype(f32)
            enc_ref[rows, slot * SLOT:(slot + 1) * SLOT] = (part * inv * gain_ref[:, cols]).astype(bf16)


def norm_kernel(gain_ref, *refs):
    count = len(refs) // 3
    for index in range(count):
        norm_block(refs[index], gain_ref, refs[count + 2 * index], refs[count + 2 * index + 1])


def encoder_kernel(map_ref, gain_ref, cot_ref, a_ref, b_ref, dh_ref, gp_ref, full_ref):
    @pl.when(is_encoder(map_ref))
    def _():
        y = y_index()
        gain = gain_ref[...]
        gp_ref[...] = jnp.zeros_like(gp_ref)
        for index, ref in enumerate((a_ref, b_ref)):

            @pl.loop(0, PIECE // QUARTER)
            def _(block):
                quarter = index * (PIECE // QUARTER) + block
                rows = row_block(quarter, QUARTER)
                place = row_block(y ^ quarter, QUARTER)
                g = cot_ref[place, :].astype(f32)
                hidden = ref[row_block(block, QUARTER), :].astype(f32)
                inv = lax.rsqrt(jnp.mean(hidden * hidden, axis=1, keepdims=True) + eps)
                full_ref[place, :] = (hidden * inv * gain).astype(bf16)
                mean = jnp.mean(hidden * gain * g, axis=1, keepdims=True)
                dh_ref[rows, :] = (inv * gain * g - hidden * (inv * inv * inv * mean)).astype(bf16)
                gp_ref[...] += jnp.sum(g * hidden * inv, axis=0, keepdims=True)


NT = (((1,), (1,)), ((), ()))
TN = (((0,), (0,)), ((), ()))
SCALE = 1.0 / math.sqrt(HEAD)


def main_kernel(*refs):
    units = refs[:N_SLOT]
    encs, hids, invs = refs[N_SLOT:N_SLOT + 4], refs[N_SLOT + 4:N_SLOT + 8], refs[N_SLOT + 8:N_SLOT + 12]
    (map_ref, rows_ref, cot_ref, qg_oth, gain_ref, dh_enc, gp_enc,
     own_out, oth_out, dh_own, dh_oth, gp_ref, dkv, mean_ref) = refs[N_SLOT + 12:]
    mean_ref[...] = jnp.zeros_like(mean_ref)

    @pl.loop(0, HALF)
    def _(head):
        cols, vcols = row_block(head, HEAD), row_block(HALF + head, HEAD)
        mine = row_block(core_index() * HALF + head, HEAD)
        both = []
        for at in (cols, vcols):
            w = jnp.concatenate([unit[:, at] for unit in units], axis=0)
            enc = jnp.concatenate([ref[...] for ref in encs], axis=0)
            both.append(jnp.dot(enc, w, preferred_element_type=f32).astype(bf16))
        rows = (slice(0, LEN), slice(LEN, 2 * LEN))
        k = [both[0][at] for at in rows]
        v = [both[1][at] for at in rows]
        q = (rows_ref[:, mine], qg_oth[:, cols])
        g = (cot_ref[:, mine], qg_oth[:, vcols])
        two = range(2)
        scores = [lax.dot_general(k[i], q[i], NT, preferred_element_type=f32) * SCALE for i in two]
        dprobs = [lax.dot_general(v[i], g[i], NT, preferred_element_type=f32) for i in two]
        e = [jnp.exp(x - jnp.max(x, axis=0, keepdims=True)) for x in scores]
        probs = [x * (1.0 / jnp.sum(x, axis=0, keepdims=True)) for x in e]
        rounded = [x.astype(bf16) for x in probs]
        delta = [jnp.sum(rounded[i].astype(f32) * dprobs[i], axis=0, keepdims=True) for i in two]
        dscores = [(probs[i] * (dprobs[i] - delta[i])).astype(bf16) for i in two]
        context = [lax.dot_general(rounded[i], v[i], TN, preferred_element_type=f32) for i in two]
        dv = [jnp.dot(rounded[i], g[i], preferred_element_type=f32).astype(bf16) for i in two]
        dk = [(jnp.dot(dscores[i], q[i], preferred_element_type=f32) * SCALE).astype(bf16) for i in two]
        dq = [lax.dot_general(dscores[i], k[i], TN, preferred_element_type=f32) * SCALE for i in two]
        for i, out in enumerate((own_out, oth_out)):
            out[:, cols] = context[i].astype(bf16)
            out[:, vcols] = dq[i].astype(bf16)
            dkv[rows[i], cols] = dk[i]
            dkv[rows[i], vcols] = dv[i]
            term = dk[i].astype(f32) * k[i].astype(f32) + dv[i].astype(f32) * v[i].astype(f32)
            mean_ref[rows[i], :] += term[:, :128] + term[:, 128:]

    inv = jnp.concatenate([ref[:, :1] for ref in invs], axis=0)
    factor = inv * inv * (jnp.sum(mean_ref[...], axis=1, keepdims=True) * (1.0 / D))

    @pl.when(jnp.logical_not(is_encoder(map_ref)))
    def _():
        for block in range(N_SLOT // 2):
            w = jnp.concatenate([units[2 * block][...], units[2 * block + 1][...]], axis=0)
            denc = lax.dot_general(dkv[...], w, NT, preferred_element_type=f32)
            for side in range(2):
                cols = pl.ds(slot_column(*SLOTS[2 * block + side]), SLOT)
                total = jnp.zeros((1, SLOT), f32)
                for index, hid in enumerate(hids):
                    rows = slice(index * PIECE, (index + 1) * PIECE)
                    at = slice(index % 2 * PIECE, (index % 2 + 1) * PIECE)
                    out = (dh_own, dh_oth)[index // 2]
                    hidden = hid[:, cols].astype(f32)
                    scaled = inv[rows] * denc[rows, side * SLOT:(side + 1) * SLOT]
                    out[at, cols] = (gain_ref[:, cols] * scaled - hidden * factor[rows]).astype(bf16)
                    total = total + jnp.sum(scaled * hidden, axis=0, keepdims=True)
                gp_ref[:, cols] = total

    @pl.when(is_encoder(map_ref))
    def _():
        dh_oth[...] = jnp.zeros_like(dh_oth)
        dh_own[...] = dh_enc[...]
        gp_ref[...] = gp_enc[...]

    dh_oth[LEN:, :] = two_rows(gp_ref[...])


def two_rows(x):
    high = x.astype(bf16).astype(f32)
    index = lax.broadcasted_iota(jnp.int32, (16, x.shape[1]), 0)
    rows = jnp.where(index == 0, high, jnp.where(index == 1, x - high, 0.0))
    return rows.astype(bf16)


def one_row(rows):
    return rows[0:1, :].astype(f32) + rows[1:2, :].astype(f32)


def attend(units, pieces, where, *args):
    whole = jax.ShapeDtypeStruct((LEN, D), bf16)
    return pl.pallas_call(
        main_kernel,
        in_specs=[VMEM] * (N_SLOT + 12) + [SMEM] + [VMEM] * 6,
        out_specs=[VMEM] * 5,
        out_shape=[
            whole, whole, whole, jax.ShapeDtypeStruct((LEN + 16, D), bf16), jax.ShapeDtypeStruct((1, D), f32)
        ],
        scratch_shapes=[
            pltpu.VMEM((2 * LEN, 2 * F), bf16),
            pltpu.VMEM((2 * LEN, 128), f32),
        ],
        compiler_params=pltpu.CompilerParams(vmem_limit_bytes=16 * MIB),
        cost_estimate=pl.CostEstimate(flops=10_000_000_000, bytes_accessed=20_000_000, transcendentals=600_000),
        name="attend",
    )(*units, *pieces, where, *args)


def small_call(kernel, out_shape, args, name, limit=6, where=None):
    first = () if where is None else (where,)
    return pl.pallas_call(
        kernel,
        in_specs=[SMEM] * len(first) + [VMEM] * len(args),
        out_specs=jax.tree.map(lambda _: VMEM, out_shape),
        out_shape=out_shape,
        compiler_params=pltpu.CompilerParams(vmem_limit_bytes=limit * MIB),
        cost_estimate=pl.CostEstimate(flops=0, bytes_accessed=1024, transcendentals=0),
        name=name,
    )(*first, *args)


def copy_call(kernel, out_shape, args, name, count):
    return pl.pallas_call(
        kernel,
        in_specs=[ANY] * len(args),
        out_specs=jax.tree.map(lambda x: VMEM if x.dtype == f32 else ANY, out_shape),
        out_shape=out_shape,
        scratch_shapes=[pltpu.SemaphoreType.DMA((count,))],
        compiler_params=pltpu.CompilerParams(vmem_limit_bytes=MIB),
        cost_estimate=pl.CostEstimate(flops=0, bytes_accessed=1024, transcendentals=0),
        name=name,
    )(*args)


def bf16_rows(rows):
    return jax.ShapeDtypeStruct((rows, D), bf16)


ROWS32 = jax.ShapeDtypeStruct((QUARTER, D), f32)
LINE = jax.ShapeDtypeStruct((1, D), f32)


def split_kernel(own_ref, gp_ref, got_ref, kept_ref, gain_ref, *sent):
    gain_ref[...] = one_row(two_rows(gp_ref[...])) + one_row(got_ref[LEN:, :])
    for step in range(4):
        at = slice(step * QUARTER, (step + 1) * QUARTER)
        part = own_ref[at, :].astype(f32) + got_ref[at, :].astype(f32)
        if step == 0:
            kept_ref[...] = part
        else:
            sent[step - 1][...] = part.astype(bf16)


def sum_kernel(kept_ref, gain_ref, a_ref, b_ref, c_ref, sum_ref, sent_ref, gain_out):
    total = kept_ref[...] + (a_ref[...].astype(f32) + b_ref[...].astype(f32) + c_ref[...].astype(f32))
    sum_ref[...] = total
    sent_ref[...] = total.astype(bf16)
    gain_out[...] = gain_ref[...]


def last_kernel(sum_ref, got_ref, gain_ref, dh_ref, gain_out):
    gain_out[...] = gain_ref[...]
    dh_ref[...] = (sum_ref[...] + got_ref[...].astype(f32)).astype(bf16)


def out_kernel(offset, map_ref, own_ref, oth_ref, *refs):
    *parts, out_ref, sems = refs
    core, y = core_index(), y_index()
    rows = LEN // len(parts)

    @pl.when(jnp.logical_not(is_encoder(map_ref)))
    def _():
        copies = [
            pltpu.make_async_copy(
                ref.at[:, pl.ds(offset, F)],
                out_ref.at[:, pl.ds(pl.multiple_of(place * F, F), F)],
                sems.at[index],
            )
            for index, (ref, place) in enumerate(((own_ref, core), (oth_ref, 1 - core)))
        ]
        for copy in copies:
            copy.start()
        for copy in copies:
            copy.wait()

    @pl.when(is_encoder(map_ref))
    def _():
        copies = []
        for index, part in enumerate(parts):
            start = 0 if len(parts) == 1 else pl.multiple_of((y ^ index) * rows, rows)
            copies.append(
                pltpu.make_async_copy(part, out_ref.at[pl.ds(start, rows), :], sems.at[index])
            )
        for copy in copies:
            copy.start()
        for copy in copies:
            copy.wait()


def put_out(offset, where, own, oth, parts, name):
    return pl.pallas_call(
        functools.partial(out_kernel, offset),
        in_specs=[SMEM] + [ANY] * (2 + len(parts)),
        out_specs=ANY,
        out_shape=jax.ShapeDtypeStruct((LEN, D), bf16),
        scratch_shapes=[pltpu.SemaphoreType.DMA((4,))],
        compiler_params=pltpu.CompilerParams(vmem_limit_bytes=MIB),
        cost_estimate=pl.CostEstimate(flops=0, bytes_accessed=2_000_000, transcendentals=0),
        name=name,
    )(where, own, oth, *parts)


def on_device(section_rows, kv_weight, cotangent, gain, section_map):
    rows, cot, weight, gain = section_rows[0], cotangent[0], kv_weight[0], gain[None]
    quarter = bf16_rows(QUARTER)

    def select(step, own, got):
        outs = [quarter, quarter] if step == 0 else quarter
        kernel = functools.partial(select_kernel, step)
        return small_call(kernel, outs, (own, got), "select", limit=3, where=section_map)

    keep, give, token = copy_call(
        columns_kernel,
        [bf16_rows(SLOT // 2), bf16_rows(SLOT // 2), jax.ShapeDtypeStruct((8, 128), f32)],
        (weight,), "columns", 4,
    )
    order = Order(token)
    got = other_core(give)
    hidden = other_y(copy_call(half_kernel, bf16_rows(2 * QUARTER), (rows,), "half", 1), 2)
    a, b = {0: copy_call(unit_kernel, bf16_rows(SLOT), (keep, got), "unit", 2)}, {}
    up, down, across = from_above(a[0]), from_below(a[0]), other_column(a[0])
    qg_oth = other_core(copy_call(give_kernel, bf16_rows(LEN), (rows, cot, a[0]), "give", 2))

    hidden = order.take(hidden)
    mine, send = select(0, rows, hidden)
    hidden = other_y(send, 1)

    a[1] = order.take(up)
    up, across_1 = from_above(a[1]), other_column(a[1])
    a[-1] = order.take(down)
    down = from_below(a[-1])
    b[0], qg_oth = order.take(across, qg_oth)
    hidden = order.take(hidden)
    mine = select(1, mine, hidden)
    hidden = other_high(mine)

    a[2] = order.take(up)
    up = from_above(a[2])
    a[-2] = order.take(down)
    down, across_2 = from_below(a[-2]), other_column(a[-2])
    b[1] = order.take(across_1)
    hidden = order.take(hidden)
    mine = select(2, mine, hidden)
    hidden = other_y(mine, 1)

    a[3] = order.take(up)
    up = from_above(b[1])
    a[-3] = order.take(down)
    down, across_3 = from_below(a[-3]), other_column(a[-3])
    hidden = order.take(hidden)
    own_a = small_call(stack_kernel, bf16_rows(PIECE), (mine, hidden), "stack", limit=3)
    hidden, oth_a = other_y(own_a, 2), other_core(own_a)
    b[-2] = order.take(across_2)

    a[4] = order.take(down)
    down, across_4 = from_below(b[0]), other_column(a[4])
    b[2] = order.take(up)
    up = from_above(b[2])
    b[-3], oth_a = order.take(across_3, oth_a)
    own_b = order.take(hidden)
    oth_b = other_core(own_b)
    b[3] = order.take(up)
    b[-1] = order.take(down)
    b[4] = order.take(across_4)
    oth_b = order.take(oth_b)
    units = [(a, b)[column][offset] for column, offset in SLOTS]

    def normalise(*pieces):
        outs = [bf16_rows(PIECE), jax.ShapeDtypeStruct((PIECE, 128), f32)] * len(pieces)
        return small_call(norm_kernel, outs, (gain, *pieces), "norm")

    enc_0, inv_0, enc_2, inv_2 = normalise(own_a, oth_a)
    enc_1, inv_1 = normalise(own_b)
    enc_3, inv_3 = normalise(oth_b)
    dh_enc, gp_enc, enc_out = small_call(
        encoder_kernel, [bf16_rows(LEN), LINE, bf16_rows(LEN)], (gain, cot, own_a, own_b), "encoder",
        where=section_map,
    )
    pieces = (enc_0, enc_1, enc_2, enc_3, own_a, own_b, oth_a, oth_b, inv_0, inv_1, inv_2, inv_3)
    own_out, oth_out, dh_own, dh_oth, gp = attend(
        units, pieces, section_map, rows, cot, qg_oth, gain, dh_enc, gp_enc
    )

    def add_from(part, *moves):
        for move in moves:
            part = small_call(add_kernel, LINE, (part, move(part)), "add", limit=1)
        return part

    def z_move(bits):
        return lambda v: dp_swap(v, lambda c, z, k: (c, z ^ bits, k))

    kept, gain_part, *parts = small_call(
        split_kernel, [ROWS32, LINE, quarter, quarter, quarter], (dh_own, gp, other_core(dh_oth)), "split"
    )
    far, near, other = other_y(parts[1], 2), other_y(parts[0], 1), other_y(parts[2], 3)
    gain_part = add_from(gain_part, z_move(1), z_move(2))
    near, far, other, gain_part, got_out = order.take(near, far, other, gain_part, other_core(oth_out))
    kept, sent, gain_part = small_call(
        sum_kernel, [ROWS32, quarter, LINE], (kept, gain_part, near, far, other), "sum"
    )
    crossed = other_high(sent)
    gain_part = add_from(gain_part, lambda v: other_y(v, 1), lambda v: other_y(v, 2))
    dh, gain_part = small_call(last_kernel, [quarter, LINE], (kept, crossed, gain_part), "last")
    far, near, other = other_y(dh, 2), other_y(dh, 1), other_y(dh, 3)
    gain_part = add_from(gain_part, z_move(4), other_column, other_high)
    dhs = [dh, near, far, other]
    section_out = put_out(0, section_map, own_out, got_out, [enc_out], "rows")
    section_grad = put_out(F, section_map, own_out, got_out, dhs, "grads")
    return (section_out[None], section_grad[None], gain_part.reshape(D))


def solution(mesh):
    return jax.shard_map(
        on_device,
        mesh=mesh,
        in_specs=(
            P("section", "dp", None),
            P("section", "dp", None),
            P("section", "dp", None),
            P(),
            P(),
        ),
        out_specs=(P("section", "dp", None), P("section", "dp", None), P()),
        check_vma=False,
    )
```

profile of v0, /device:TPU:6, one launch (start us, length us, event | category | flops | bytes accessed | tf_op | source)
XLA Modules:
  0.0 156.1 jit_solution(9094435041095684450)
XLA Ops:
  0.6 1.0 copy-done.3
  1.9 1.2 copy-done
  3.2 3.3 %collective-permute-start.2 = (bf16[128,2048]{1,0:T(8,128)(2,1)S(1)}, bf16[128,2048]{1,0:T(8,128)(2,1)S(1)}, u32[]{:S(2)}, u32[]{:S(2)}) collective-permute-start(bf16[128,2048]{1,0:T(8,128)(2,1)S(1)} %half.1), channel_id=1, source_target_pairs={{0,64},{32,96},{64,0},{96,32},{128,192},{160,224},{192,128},{224,1... | collective-permute-start | bytes 1572872 | tf_op jit(solution)/shard_map/ppermute | solution.py:50
  6.7 0.3 collective-permute-start.5
  7.0 5.9 %collective-permute-start.1 = (bf16[128,2048]{1,0:T(8,128)(2,1)S(1)}, bf16[128,2048]{1,0:T(8,128)(2,1)S(1)}, u32[]{:S(2)}, u32[]{:S(2)}) collective-permute-start(bf16[128,2048]{1,0:T(8,128)(2,1)S(1)} %unit.1.token_ref.refs_0_), channel_id=1, source_target_pairs={{0,14},{1,15},{2,0},{3,1},{4,2},{5,3},{6,4},{7,5},{8,6},{9,7},{10,... | collective-permute-start | bytes 1572872 | tf_op jit(solution)/shard_map/ppermute | solution.py:42
  12.9 0.8 collective-permute-start.4
  13.7 5.4 %collective-permute-done.2.refs_0_ = bf16[128,2048]{1,0:T(8,128)(2,1)S(1)} collective-permute-done((bf16[128,2048]{1,0:T(8,128)(2,1)S(1)}, bf16[128,2048]{1,0:T(8,128)(2,1)S(1)}, u32[]{:S(2)}, u32[]{:S(2)}) %collective-permute-start.2) | collective-permute-done | bytes 524320 | tf_op jit(solution)/shard_map/ppermute | solution.py:50
  19.1 5.4 %collective-permute-done.1.refs_0_ = bf16[128,2048]{1,0:T(8,128)(2,1)S(1)} collective-permute-done((bf16[128,2048]{1,0:T(8,128)(2,1)S(1)}, bf16[128,2048]{1,0:T(8,128)(2,1)S(1)}, u32[]{:S(2)}, u32[]{:S(2)}) %collective-permute-start.1) | collective-permute-done | bytes 524320 | tf_op jit(solution)/shard_map/ppermute | solution.py:42
  24.5 3.7 %collective-permute-start.6 = (bf16[128,2048]{1,0:T(8,128)(2,1)S(1)}, bf16[128,2048]{1,0:T(8,128)(2,1)S(1)}, u32[]{:S(2)}, u32[]{:S(2)}) collective-permute-start(bf16[128,2048]{1,0:T(8,128)(2,1)S(1)} %get-tuple-element.87.refs_1_), channel_id=1, source_target_pairs={{0,14},{1,15},{2,0},{3,1},{4,2},{5,3},{6,4},{7,5},{8,6},{9,7},{10,... | collective-permute-start | bytes 1572872 | tf_op jit(solution)/shard_map/ppermute | solution.py:42
  28.2 0.6 select.3
  28.9 0.8 collective-permute-start.7
  29.6 0.8 collective-permute-start.9
  30.5 5.9 %collective-permute-done.7.refs_0_ = bf16[64,2048]{1,0:T(8,128)(2,1)S(1)} collective-permute-done((bf16[64,2048]{1,0:T(8,128)(2,1)S(1)}, bf16[64,2048]{1,0:T(8,128)(2,1)S(1)}, u32[]{:S(2)}, u32[]{:S(2)}) %collective-permute-start.7) | collective-permute-done | bytes 262176 | tf_op jit(solution)/shard_map/ppermute | solution.py:50
  36.4 2.7 %collective-permute-done.6.refs_0_ = bf16[128,2048]{1,0:T(8,128)(2,1)S(1)} collective-permute-done((bf16[128,2048]{1,0:T(8,128)(2,1)S(1)}, bf16[128,2048]{1,0:T(8,128)(2,1)S(1)}, u32[]{:S(2)}, u32[]{:S(2)}) %collective-permute-start.6) | collective-permute-done | bytes 524320 | tf_op jit(solution)/shard_map/ppermute | solution.py:42
  39.0 3.7 %collective-permute-start.10 = (bf16[128,2048]{1,0:T(8,128)(2,1)S(1)}, bf16[128,2048]{1,0:T(8,128)(2,1)S(1)}, u32[]{:S(2)}, u32[]{:S(2)}) collective-permute-start(bf16[128,2048]{1,0:T(8,128)(2,1)S(1)} %get-tuple-element.96.refs_4_), channel_id=1, source_target_pairs={{0,14},{1,15},{2,0},{3,1},{4,2},{5,3},{6,4},{7,5},{8,6},{9,7},{10,... | collective-permute-start | bytes 1572872 | tf_op jit(solution)/shard_map/ppermute | solution.py:42
  42.7 0.6 select.4.own_ref
  43.3 1.5 collective-permute-start.11
  44.8 9.3 %collective-permute-done.11.refs_0_ = bf16[64,2048]{1,0:T(8,128)(2,1)S(1)} collective-permute-done((bf16[64,2048]{1,0:T(8,128)(2,1)S(1)}, bf16[64,2048]{1,0:T(8,128)(2,1)S(1)}, u32[]{:S(2)}, u32[]{:S(2)}) %collective-permute-start.11) | collective-permute-done | bytes 262176 | tf_op jit(solution)/shard_map/ppermute | solution.py:50
  54.2 0.6 select.5.refs_0_
  54.8 0.8 collective-permute-start.14
  55.5 0.5 collective-permute-done.12.refs_0_
  56.1 3.2 %collective-permute-start.16 = (bf16[128,2048]{1,0:T(8,128)(2,1)S(1)}, bf16[128,2048]{1,0:T(8,128)(2,1)S(1)}, u32[]{:S(2)}, u32[]{:S(2)}) collective-permute-start(bf16[128,2048]{1,0:T(8,128)(2,1)S(1)} %get-tuple-element.100.refs_6_), channel_id=1, source_target_pairs={{0,14},{1,15},{2,0},{3,1},{4,2},{5,3},{6,4},{7,5},{8,6},{9,7},{10,... | collective-permute-start | bytes 1572872 | tf_op jit(solution)/shard_map/ppermute | solution.py:42
  59.3 1.9 %collective-permute-done.14.refs_0_ = bf16[64,2048]{1,0:T(8,128)(2,1)S(1)} collective-permute-done((bf16[64,2048]{1,0:T(8,128)(2,1)S(1)}, bf16[64,2048]{1,0:T(8,128)(2,1)S(1)}, u32[]{:S(2)}, u32[]{:S(2)}) %collective-permute-start.14) | collective-permute-done | bytes 262176 | tf_op jit(solution)/shard_map/ppermute | solution.py:50
  61.3 0.3 collective-permute-start.18
  61.5 0.9 collective-permute-start.17
  62.5 1.1 collective-permute-start.20
  63.6 4.9 %collective-permute-done.15.refs_0_ = bf16[128,2048]{1,0:T(8,128)(2,1)S(1)} collective-permute-done((bf16[128,2048]{1,0:T(8,128)(2,1)S(1)}, bf16[128,2048]{1,0:T(8,128)(2,1)S(1)}, u32[]{:S(2)}, u32[]{:S(2)}) %collective-permute-start.15) | collective-permute-done | bytes 524320 | tf_op jit(solution)/shard_map/ppermute | solution.py:42
  68.5 3.2 %collective-permute-start.19 = (bf16[128,2048]{1,0:T(8,128)(2,1)S(1)}, bf16[128,2048]{1,0:T(8,128)(2,1)S(1)}, u32[]{:S(2)}, u32[]{:S(2)}) collective-permute-start(bf16[128,2048]{1,0:T(8,128)(2,1)S(1)} %get-tuple-element.115.refs_11_), channel_id=1, source_target_pairs={{0,14},{1,15},{2,0},{3,1},{4,2},{5,3},{6,4},{7,5},{8,6},{9,7},{10,... | collective-permute-start | bytes 1572872 | tf_op jit(solution)/shard_map/ppermute | solution.py:42
  71.7 0.8 collective-permute-start.22
  72.6 3.8 %collective-permute-done.17.refs_0_ = bf16[128,2048]{1,0:T(8,128)(2,1)S(1)} collective-permute-done((bf16[128,2048]{1,0:T(8,128)(2,1)S(1)}, bf16[128,2048]{1,0:T(8,128)(2,1)S(1)}, u32[]{:S(2)}, u32[]{:S(2)}) %collective-permute-start.17) | collective-permute-done | bytes 524320 | tf_op jit(solution)/shard_map/ppermute | solution.py:42
  76.4 1.6 %collective-permute-done.20.refs_0_ = bf16[128,2048]{1,0:T(8,128)(2,1)S(1)} collective-permute-done((bf16[128,2048]{1,0:T(8,128)(2,1)S(1)}, bf16[128,2048]{1,0:T(8,128)(2,1)S(1)}, u32[]{:S(2)}, u32[]{:S(2)}) %collective-permute-start.20) | collective-permute-done | bytes 524320 | tf_op jit(solution)/shard_map/ppermute | solution.py:50
  78.0 0.4 norm.4
  78.3 0.6 encoder.1
  78.9 0.7 norm.3
  79.6 0.3 collective-permute-done.21.refs_0_
  80.0 7.2 %collective-permute-done.22.refs_0_ = bf16[128,2048]{1,0:T(8,128)(2,1)S(1)} collective-permute-done((bf16[128,2048]{1,0:T(8,128)(2,1)S(1)}, bf16[128,2048]{1,0:T(8,128)(2,1)S(1)}, u32[]{:S(2)}, u32[]{:S(2)}) %collective-permute-start.22) | collective-permute-done | bytes 524320 | tf_op jit(solution)/shard_map/ppermute | solution.py:42
  87.1 0.4 norm.5
  87.5 14.7 %attend.1 = (bf16[256,2048]{1,0:T(8,128)(2,1)S(1)}, bf16[256,2048]{1,0:T(8,128)(2,1)S(1)}, bf16[256,2048]{1,0:T(8,128)(2,1)S(1)}, bf16[272,2048]{1,0:T(8,128)(2,1)S(1)}, f32[1,2048]{1,0:T(1,128)S(1)}) custom-call(bf16[128,2048]{1,0:T(8,128)(2,1)S(1)} %unit.1.token_ref.refs_0_, bf16[128,2048]{1,0:T(8,128)(2,1)S(1)} %get-tuple-element.87.refs_1_, ...), custom_call_target="tpu_custom_call" | custom-call | flops 10000000000 | bytes 20000000 | tf_op jit(solution)/shard_map/attend/pallas_call | solution.py:324
  102.2 0.3 collective-permute-start.24
  102.6 0.5 collective-permute-start.30
  103.1 2.2 %collective-permute-done.24.got_ref = bf16[272,2048]{1,0:T(8,128)(2,1)S(1)} collective-permute-done((bf16[272,2048]{1,0:T(8,128)(2,1)S(1)}, bf16[272,2048]{1,0:T(8,128)(2,1)S(1)}, u32[]{:S(2)}, u32[]{:S(2)}) %collective-permute-start.24) | collective-permute-done | bytes 1114144 | tf_op jit(solution)/shard_map/ppermute | solution.py:42
  105.3 0.3 split.1
  105.7 2.4 %collective-permute-start.26 = (bf16[64,2048]{1,0:T(8,128)(2,1)S(1)}, bf16[64,2048]{1,0:T(8,128)(2,1)S(1)}, u32[]{:S(2)}, u32[]{:S(2)}) collective-permute-start(bf16[64,2048]{1,0:T(8,128)(2,1)S(1)} %get-tuple-element.146), channel_id=1, source_target_pairs={{0,64},{32,96},{64,0},{96,32},{128,192},{160,224},{192,128},{224,1... | collective-permute-start | bytes 786440 | tf_op jit(solution)/shard_map/ppermute | solution.py:50
  108.1 2.3 %collective-permute-start.27 = (bf16[64,2048]{1,0:T(8,128)(2,1)S(1)}, bf16[64,2048]{1,0:T(8,128)(2,1)S(1)}, u32[]{:S(2)}, u32[]{:S(2)}) collective-permute-start(bf16[64,2048]{1,0:T(8,128)(2,1)S(1)} %get-tuple-element.147), channel_id=1, source_target_pairs={{0,96},{32,64},{64,32},{96,0},{128,224},{160,192},{192,160},{224,1... | collective-permute-start | bytes 786440 | tf_op jit(solution)/shard_map/ppermute | solution.py:50
  110.4 3.6 %collective-permute-done.28.b_ref = f32[1,2048]{1,0:T(1,128)S(1)} collective-permute-done((f32[1,2048]{1,0:T(1,128)S(1)}, f32[1,2048]{1,0:T(1,128)S(1)}, u32[]{:S(2)}, u32[]{:S(2)}) %collective-permute-start.28) | collective-permute-done | bytes 8224 | tf_op jit(solution)/shard_map/ppermute | solution.py:42
  114.0 0.9 collective-permute-start.29
  115.0 3.6 %collective-permute-done.29.b_ref = f32[1,2048]{1,0:T(1,128)S(1)} collective-permute-done((f32[1,2048]{1,0:T(1,128)S(1)}, f32[1,2048]{1,0:T(1,128)S(1)}, u32[]{:S(2)}, u32[]{:S(2)}) %collective-permute-start.29) | collective-permute-done | bytes 8224 | tf_op jit(solution)/shard_map/ppermute | solution.py:42
  118.6 1.5 collective-permute-done.26.refs_1_
  120.1 2.6 %collective-permute-done.27.refs_2_ = bf16[64,2048]{1,0:T(8,128)(2,1)S(1)} collective-permute-done((bf16[64,2048]{1,0:T(8,128)(2,1)S(1)}, bf16[64,2048]{1,0:T(8,128)(2,1)S(1)}, u32[]{:S(2)}, u32[]{:S(2)}) %collective-permute-start.27) | collective-permute-done | bytes 262176 | tf_op jit(solution)/shard_map/ppermute | solution.py:50
  122.7 0.1 sum.1
  122.8 1.5 collective-permute-start.31
  124.3 3.6 %collective-permute-done.32.b_ref = f32[1,2048]{1,0:T(1,128)S(1)} collective-permute-done((f32[1,2048]{1,0:T(1,128)S(1)}, f32[1,2048]{1,0:T(1,128)S(1)}, u32[]{:S(2)}, u32[]{:S(2)}) %collective-permute-start.32) | collective-permute-done | bytes 8224 | tf_op jit(solution)/shard_map/ppermute | solution.py:50
  128.0 1.7 %collective-permute-start.33 = (f32[1,2048]{1,0:T(1,128)S(1)}, f32[1,2048]{1,0:T(1,128)S(1)}, u32[]{:S(2)}, u32[]{:S(2)}) collective-permute-start(f32[1,2048]{1,0:T(1,128)S(1)} %add.9.a_ref), channel_id=1, source_target_pairs={{0,64},{32,96},{64,0},{96,32},{128,192},{160,224},{192,128},{224,1... | collective-permute-start | bytes 24584 | tf_op jit(solution)/shard_map/ppermute | solution.py:50
  129.7 3.4 %collective-permute-done.33.b_ref = f32[1,2048]{1,0:T(1,128)S(1)} collective-permute-done((f32[1,2048]{1,0:T(1,128)S(1)}, f32[1,2048]{1,0:T(1,128)S(1)}, u32[]{:S(2)}, u32[]{:S(2)}) %collective-permute-start.33) | collective-permute-done | bytes 8224 | tf_op jit(solution)/shard_map/ppermute | solution.py:50
  133.2 2.4 %collective-permute-start.36 = (bf16[64,2048]{1,0:T(8,128)(2,1)S(1)}, bf16[64,2048]{1,0:T(8,128)(2,1)S(1)}, u32[]{:S(2)}, u32[]{:S(2)}) collective-permute-start(bf16[64,2048]{1,0:T(8,128)(2,1)S(1)} %get-tuple-element.161.refs_0_), channel_id=1, source_target_pairs={{0,96},{32,64},{64,32},{96,0},{128,224},{160,192},{192,160},{224,1... | collective-permute-start | bytes 786440 | tf_op jit(solution)/shard_map/ppermute | solution.py:50
  135.6 1.8 %collective-permute-start.34 = (bf16[64,2048]{1,0:T(8,128)(2,1)S(1)}, bf16[64,2048]{1,0:T(8,128)(2,1)S(1)}, u32[]{:S(2)}, u32[]{:S(2)}) collective-permute-start(bf16[64,2048]{1,0:T(8,128)(2,1)S(1)} %get-tuple-element.161.refs_0_), channel_id=1, source_target_pairs={{0,32},{32,0},{64,96},{96,64},{128,160},{160,128},{192,224},{224,1... | collective-permute-start | bytes 786440 | tf_op jit(solution)/shard_map/ppermute | solution.py:50
  137.4 1.8 %collective-permute-start.37 = (f32[1,2048]{1,0:T(1,128)S(1)}, f32[1,2048]{1,0:T(1,128)S(1)}, u32[]{:S(2)}, u32[]{:S(2)}) collective-permute-start(f32[1,2048]{1,0:T(1,128)S(1)} %get-tuple-element.162.a_ref), channel_id=1, source_target_pairs={{0,8},{1,9},{2,10},{3,11},{4,12},{5,13},{6,14},{7,15},{8,0},{9,1},... | collective-permute-start | bytes 24584 | tf_op jit(solution)/shard_map/ppermute | solution.py:42
  139.2 5.7 %collective-permute-done.37.b_ref = f32[1,2048]{1,0:T(1,128)S(1)} collective-permute-done((f32[1,2048]{1,0:T(1,128)S(1)}, f32[1,2048]{1,0:T(1,128)S(1)}, u32[]{:S(2)}, u32[]{:S(2)}) %collective-permute-start.37) | collective-permute-done | bytes 8224 | tf_op jit(solution)/shard_map/ppermute | solution.py:42
  144.9 3.6 %collective-permute-done.38.b_ref = f32[1,2048]{1,0:T(1,128)S(1)} collective-permute-done((f32[1,2048]{1,0:T(1,128)S(1)}, f32[1,2048]{1,0:T(1,128)S(1)}, u32[]{:S(2)}, u32[]{:S(2)}) %collective-permute-start.38) | collective-permute-done | bytes 8224 | tf_op jit(solution)/shard_map/ppermute | solution.py:42
  148.6 2.1 %collective-permute-start.39 = (f32[1,2048]{1,0:T(1,128)S(1)}, f32[1,2048]{1,0:T(1,128)S(1)}, u32[]{:S(2)}, u32[]{:S(2)}) collective-permute-start(f32[1,2048]{1,0:T(1,128)S(1)} %add.12.a_ref), channel_id=1, source_target_pairs={{0,128},{32,160},{64,192},{96,224},{128,0},{160,32},{192,64},{224,... | collective-permute-start | bytes 24584 | tf_op jit(solution)/shard_map/ppermute | solution.py:50
  150.7 1.6 rows.1
  152.3 1.5 collective-permute-done.39.b_ref
  153.8 0.6 add.13
  154.4 1.6 %grads.1 = bf16[256,2048]{1,0:T(8,128)(2,1)} custom-call(s32[8]{0:T(128)S(1)} %copy-done.5, bf16[256,2048]{1,0:T(8,128)(2,1)S(1)} %get-tuple-element.141.own_ref, bf16[256,2048]{1,0:T(8,128)(2,1)S(1)} %get-tuple-element.151.oth_ref, bf16[64,2048]{1,0:T(8,128)(2,1)S(1)} %get-tuple-element.161.refs_0_, bf16[64,2048]{1,0:T(8,128)(2,1)S(1)} %collective-permute-done.34.refs_1_, ...), custom_call_target="tpu_custom_call" | custom-call | bytes 2000000 | tf_op jit(solution)/shard_map/grads/pallas_call | solution.py:433
  (75 shorter events, 0.8 us)
Async XLA Ops:
  0.6 1.0 copy-start.3
  1.8 4.7 %collective-permute-start = (bf16[64,2048]{1,0:T(8,128)(2,1)S(1)}, bf16[64,2048]{1,0:T(8,128)(2,1)S(1)}, u32[]{:S(2)}, u32[]{:S(2)}) collective-permute-start(bf16[64,2048]{1,0:T(8,128)(2,1)S(1)} %get-tuple-element.84), channel_id=1, source_target_pairs={{0,1},{1,0},{2,3},{3,2},{4,5},{5,4},{6,7},{7,6},{8,9},{9,8},{10,11... | collective-permute-start | bytes 786440 | tf_op jit(solution)/shard_map/ppermute | solution.py:42
  1.9 1.2 copy-start
  3.1 3.4 %copy-start.1 = (bf16[1,256,2048]{2,1,0:T(8,128)(2,1)S(1)}, bf16[1,256,2048]{2,1,0:T(8,128)(2,1)}, u32[]{:S(2)}) copy-start(bf16[1,256,2048]{2,1,0:T(8,128)(2,1)} %param.5) | copy-start | bytes 3145732
  3.1 3.4 %copy-start.2 = (bf16[1,256,2048]{2,1,0:T(8,128)(2,1)S(1)}, bf16[1,256,2048]{2,1,0:T(8,128)(2,1)}, u32[]{:S(2)}) copy-start(bf16[1,256,2048]{2,1,0:T(8,128)(2,1)} %param.7) | copy-start | bytes 3145732
  3.2 15.9 %collective-permute-start.2 = (bf16[128,2048]{1,0:T(8,128)(2,1)S(1)}, bf16[128,2048]{1,0:T(8,128)(2,1)S(1)}, u32[]{:S(2)}, u32[]{:S(2)}) collective-permute-start(bf16[128,2048]{1,0:T(8,128)(2,1)S(1)} %half.1), channel_id=1, source_target_pairs={{0,64},{32,96},{64,0},{96,32},{128,192},{160,224},{192,128},{224,1... | collective-permute-start | bytes 1572872 | tf_op jit(solution)/shard_map/ppermute | solution.py:50
  6.7 21.5 %copy-start.5 = (s32[8]{0:T(128)S(1)}, s32[8]{0:T(128)}, u32[]{:S(2)}) copy-start(s32[8]{0:T(128)} %map_ref.11) | copy-start | bytes 100
  6.7 23.7 %collective-permute-start.5 = (bf16[256,2048]{1,0:T(8,128)(2,1)S(1)}, bf16[256,2048]{1,0:T(8,128)(2,1)S(1)}, u32[]{:S(2)}, u32[]{:S(2)}) collective-permute-start(bf16[256,2048]{1,0:T(8,128)(2,1)S(1)} %give.1), channel_id=1, source_target_pairs={{0,1},{1,0},{2,3},{3,2},{4,5},{5,4},{6,7},{7,6},{8,9},{9,8},{10,11... | collective-permute-start | bytes 3145736 | tf_op jit(solution)/shard_map/ppermute | solution.py:42
  7.0 17.5 %collective-permute-start.1 = (bf16[128,2048]{1,0:T(8,128)(2,1)S(1)}, bf16[128,2048]{1,0:T(8,128)(2,1)S(1)}, u32[]{:S(2)}, u32[]{:S(2)}) collective-permute-start(bf16[128,2048]{1,0:T(8,128)(2,1)S(1)} %unit.1.token_ref.refs_0_), channel_id=1, source_target_pairs={{0,14},{1,15},{2,0},{3,1},{4,2},{5,3},{6,4},{7,5},{8,6},{9,7},{10,... | collective-permute-start | bytes 1572872 | tf_op jit(solution)/shard_map/ppermute | solution.py:42
  12.9 15.3 %collective-permute-start.3 = (bf16[128,2048]{1,0:T(8,128)(2,1)S(1)}, bf16[128,2048]{1,0:T(8,128)(2,1)S(1)}, u32[]{:S(2)}, u32[]{:S(2)}) collective-permute-start(bf16[128,2048]{1,0:T(8,128)(2,1)S(1)} %unit.1.token_ref.refs_0_), channel_id=1, source_target_pairs={{0,2},{1,3},{2,4},{3,5},{4,6},{5,7},{6,8},{7,9},{8,10},{9,11},{10,... | collective-permute-start | bytes 1572872 | tf_op jit(solution)/shard_map/ppermute | solution.py:42
  12.9 16.8 %collective-permute-start.4 = (bf16[128,2048]{1,0:T(8,128)(2,1)S(1)}, bf16[128,2048]{1,0:T(8,128)(2,1)S(1)}, u32[]{:S(2)}, u32[]{:S(2)}) collective-permute-start(bf16[128,2048]{1,0:T(8,128)(2,1)S(1)} %unit.1.token_ref.refs_0_), channel_id=1, source_target_pairs={{0,16},{1,17},{2,18},{3,19},{4,20},{5,21},{6,22},{7,23},{8,24},{9,... | collective-permute-start | bytes 1572872 | tf_op jit(solution)/shard_map/ppermute | solution.py:42
  24.5 14.5 %collective-permute-start.6 = (bf16[128,2048]{1,0:T(8,128)(2,1)S(1)}, bf16[128,2048]{1,0:T(8,128)(2,1)S(1)}, u32[]{:S(2)}, u32[]{:S(2)}) collective-permute-start(bf16[128,2048]{1,0:T(8,128)(2,1)S(1)} %get-tuple-element.87.refs_1_), channel_id=1, source_target_pairs={{0,14},{1,15},{2,0},{3,1},{4,2},{5,3},{6,4},{7,5},{8,6},{9,7},{10,... | collective-permute-start | bytes 1572872 | tf_op jit(solution)/shard_map/ppermute | solution.py:42
  28.2 14.5 %collective-permute-start.8 = (bf16[128,2048]{1,0:T(8,128)(2,1)S(1)}, bf16[128,2048]{1,0:T(8,128)(2,1)S(1)}, u32[]{:S(2)}, u32[]{:S(2)}) collective-permute-start(bf16[128,2048]{1,0:T(8,128)(2,1)S(1)} %get-tuple-element.89.refs_2_), channel_id=1, source_target_pairs={{0,2},{1,3},{2,4},{3,5},{4,6},{5,7},{6,8},{7,9},{8,10},{9,11},{10,... | collective-permute-start | bytes 1572872 | tf_op jit(solution)/shard_map/ppermute | solution.py:42
  28.9 7.5 %collective-permute-start.7 = (bf16[64,2048]{1,0:T(8,128)(2,1)S(1)}, bf16[64,2048]{1,0:T(8,128)(2,1)S(1)}, u32[]{:S(2)}, u32[]{:S(2)}) collective-permute-start(bf16[64,2048]{1,0:T(8,128)(2,1)S(1)} %get-tuple-element.93), channel_id=1, source_target_pairs={{0,32},{32,0},{64,96},{96,64},{128,160},{160,128},{192,224},{224,1... | collective-permute-start | bytes 786440 | tf_op jit(solution)/shard_map/ppermute | solution.py:50
  29.6 15.2 %collective-permute-start.9 = (bf16[128,2048]{1,0:T(8,128)(2,1)S(1)}, bf16[128,2048]{1,0:T(8,128)(2,1)S(1)}, u32[]{:S(2)}, u32[]{:S(2)}) collective-permute-start(bf16[128,2048]{1,0:T(8,128)(2,1)S(1)} %get-tuple-element.87.refs_1_), channel_id=1, source_target_pairs={{0,16},{1,17},{2,18},{3,19},{4,20},{5,21},{6,22},{7,23},{8,24},{9,... | collective-permute-start | bytes 1572872 | tf_op jit(solution)/shard_map/ppermute | solution.py:42
  39.0 16.5 %collective-permute-start.10 = (bf16[128,2048]{1,0:T(8,128)(2,1)S(1)}, bf16[128,2048]{1,0:T(8,128)(2,1)S(1)}, u32[]{:S(2)}, u32[]{:S(2)}) collective-permute-start(bf16[128,2048]{1,0:T(8,128)(2,1)S(1)} %get-tuple-element.96.refs_4_), channel_id=1, source_target_pairs={{0,14},{1,15},{2,0},{3,1},{4,2},{5,3},{6,4},{7,5},{8,6},{9,7},{10,... | collective-permute-start | bytes 1572872 | tf_op jit(solution)/shard_map/ppermute | solution.py:42
  42.7 13.3 %collective-permute-start.12 = (bf16[128,2048]{1,0:T(8,128)(2,1)S(1)}, bf16[128,2048]{1,0:T(8,128)(2,1)S(1)}, u32[]{:S(2)}, u32[]{:S(2)}) collective-permute-start(bf16[128,2048]{1,0:T(8,128)(2,1)S(1)} %get-tuple-element.98.refs_5_), channel_id=1, source_target_pairs={{0,2},{1,3},{2,4},{3,5},{4,6},{5,7},{6,8},{7,9},{8,10},{9,11},{10,... | collective-permute-start | bytes 1572872 | tf_op jit(solution)/shard_map/ppermute | solution.py:42
  43.3 10.8 %collective-permute-start.11 = (bf16[64,2048]{1,0:T(8,128)(2,1)S(1)}, bf16[64,2048]{1,0:T(8,128)(2,1)S(1)}, u32[]{:S(2)}, u32[]{:S(2)}) collective-permute-start(bf16[64,2048]{1,0:T(8,128)(2,1)S(1)} %select.4.own_ref), channel_id=1, source_target_pairs={{0,128},{32,160},{64,192},{96,224},{128,0},{160,32},{192,64},{224,... | collective-permute-start | bytes 786440 | tf_op jit(solution)/shard_map/ppermute | solution.py:50
  44.8 17.6 %collective-permute-start.13 = (bf16[128,2048]{1,0:T(8,128)(2,1)S(1)}, bf16[128,2048]{1,0:T(8,128)(2,1)S(1)}, u32[]{:S(2)}, u32[]{:S(2)}) collective-permute-start(bf16[128,2048]{1,0:T(8,128)(2,1)S(1)} %get-tuple-element.98.refs_5_), channel_id=1, source_target_pairs={{0,16},{1,17},{2,18},{3,19},{4,20},{5,21},{6,22},{7,23},{8,24},{9,... | collective-permute-start | bytes 1572872 | tf_op jit(solution)/shard_map/ppermute | solution.py:42
  54.8 6.5 %collective-permute-start.14 = (bf16[64,2048]{1,0:T(8,128)(2,1)S(1)}, bf16[64,2048]{1,0:T(8,128)(2,1)S(1)}, u32[]{:S(2)}, u32[]{:S(2)}) collective-permute-start(bf16[64,2048]{1,0:T(8,128)(2,1)S(1)} %select.5.refs_0_), channel_id=1, source_target_pairs={{0,32},{32,0},{64,96},{96,64},{128,160},{160,128},{192,224},{224,1... | collective-permute-start | bytes 786440 | tf_op jit(solution)/shard_map/ppermute | solution.py:50
  56.1 12.4 %collective-permute-start.15 = (bf16[128,2048]{1,0:T(8,128)(2,1)S(1)}, bf16[128,2048]{1,0:T(8,128)(2,1)S(1)}, u32[]{:S(2)}, u32[]{:S(2)}) collective-permute-start(bf16[128,2048]{1,0:T(8,128)(2,1)S(1)} %get-tuple-element.107.refs_8_), channel_id=1, source_target_pairs={{0,2},{1,3},{2,4},{3,5},{4,6},{5,7},{6,8},{7,9},{8,10},{9,11},{10,... | collective-permute-start | bytes 1572872 | tf_op jit(solution)/shard_map/ppermute | solution.py:42
  56.1 12.4 %collective-permute-start.16 = (bf16[128,2048]{1,0:T(8,128)(2,1)S(1)}, bf16[128,2048]{1,0:T(8,128)(2,1)S(1)}, u32[]{:S(2)}, u32[]{:S(2)}) collective-permute-start(bf16[128,2048]{1,0:T(8,128)(2,1)S(1)} %get-tuple-element.100.refs_6_), channel_id=1, source_target_pairs={{0,14},{1,15},{2,0},{3,1},{4,2},{5,3},{6,4},{7,5},{8,6},{9,7},{10,... | collective-permute-start | bytes 1572872 | tf_op jit(solution)/shard_map/ppermute | solution.py:42
  61.3 10.5 %collective-permute-start.18 = (bf16[128,2048]{1,0:T(8,128)(2,1)S(1)}, bf16[128,2048]{1,0:T(8,128)(2,1)S(1)}, u32[]{:S(2)}, u32[]{:S(2)}) collective-permute-start(bf16[128,2048]{1,0:T(8,128)(2,1)S(1)} %stack.1.refs_0_.a_ref.refs_20_), channel_id=1, source_target_pairs={{0,1},{1,0},{2,3},{3,2},{4,5},{5,4},{6,7},{7,6},{8,9},{9,8},{10,11... | collective-permute-start | bytes 1572872 | tf_op jit(solution)/shard_map/ppermute | solution.py:42
  61.5 14.8 %collective-permute-start.17 = (bf16[128,2048]{1,0:T(8,128)(2,1)S(1)}, bf16[128,2048]{1,0:T(8,128)(2,1)S(1)}, u32[]{:S(2)}, u32[]{:S(2)}) collective-permute-start(bf16[128,2048]{1,0:T(8,128)(2,1)S(1)} %get-tuple-element.107.refs_8_), channel_id=1, source_target_pairs={{0,16},{1,17},{2,18},{3,19},{4,20},{5,21},{6,22},{7,23},{8,24},{9,... | collective-permute-start | bytes 1572872 | tf_op jit(solution)/shard_map/ppermute | solution.py:42
  62.5 15.5 %collective-permute-start.20 = (bf16[128,2048]{1,0:T(8,128)(2,1)S(1)}, bf16[128,2048]{1,0:T(8,128)(2,1)S(1)}, u32[]{:S(2)}, u32[]{:S(2)}) collective-permute-start(bf16[128,2048]{1,0:T(8,128)(2,1)S(1)} %stack.1.refs_0_.a_ref.refs_20_), channel_id=1, source_target_pairs={{0,64},{32,96},{64,0},{96,32},{128,192},{160,224},{192,128},{224,1... | collective-permute-start | bytes 1572872 | tf_op jit(solution)/shard_map/ppermute | solution.py:50
  68.5 11.5 %collective-permute-start.21 = (bf16[128,2048]{1,0:T(8,128)(2,1)S(1)}, bf16[128,2048]{1,0:T(8,128)(2,1)S(1)}, u32[]{:S(2)}, u32[]{:S(2)}) collective-permute-start(bf16[128,2048]{1,0:T(8,128)(2,1)S(1)} %get-tuple-element.91.refs_3_), channel_id=1, source_target_pairs={{0,2},{1,3},{2,4},{3,5},{4,6},{5,7},{6,8},{7,9},{8,10},{9,11},{10,... | collective-permute-start | bytes 1572872 | tf_op jit(solution)/shard_map/ppermute | solution.py:42
  68.5 9.5 %copy-start.4 = (f32[2048]{0:T(1024)S(1)}, f32[2048]{0:T(1024)}, u32[]{:S(2)}) copy-start(f32[2048]{0:T(1024)} %param.8) | copy-start | bytes 24580
  68.5 11.1 %collective-permute-start.19 = (bf16[128,2048]{1,0:T(8,128)(2,1)S(1)}, bf16[128,2048]{1,0:T(8,128)(2,1)S(1)}, u32[]{:S(2)}, u32[]{:S(2)}) collective-permute-start(bf16[128,2048]{1,0:T(8,128)(2,1)S(1)} %get-tuple-element.115.refs_11_), channel_id=1, source_target_pairs={{0,14},{1,15},{2,0},{3,1},{4,2},{5,3},{6,4},{7,5},{8,6},{9,7},{10,... | collective-permute-start | bytes 1572872 | tf_op jit(solution)/shard_map/ppermute | solution.py:42
  71.7 15.4 %collective-permute-start.22 = (bf16[128,2048]{1,0:T(8,128)(2,1)S(1)}, bf16[128,2048]{1,0:T(8,128)(2,1)S(1)}, u32[]{:S(2)}, u32[]{:S(2)}) collective-permute-start(bf16[128,2048]{1,0:T(8,128)(2,1)S(1)} %get-tuple-element.113.refs_10_), channel_id=1, source_target_pairs={{0,16},{1,17},{2,18},{3,19},{4,20},{5,21},{6,22},{7,23},{8,24},{9,... | collective-permute-start | bytes 1572872 | tf_op jit(solution)/shard_map/ppermute | solution.py:42
  77.9 9.2 %collective-permute-start.23 = (bf16[128,2048]{1,0:T(8,128)(2,1)S(1)}, bf16[128,2048]{1,0:T(8,128)(2,1)S(1)}, u32[]{:S(2)}, u32[]{:S(2)}) collective-permute-start(bf16[128,2048]{1,0:T(8,128)(2,1)S(1)} %get-tuple-element.128.refs_0_.b_ref.refs_21_), channel_id=1, source_target_pairs={{0,1},{1,0},{2,3},{3,2},{4,5},{5,4},{6,7},{7,6},{8,9},{9,8},{10,11... | collective-permute-start | bytes 1572872 | tf_op jit(solution)/shard_map/ppermute | solution.py:42
  102.2 3.1 %collective-permute-start.24 = (bf16[272,2048]{1,0:T(8,128)(2,1)S(1)}, bf16[272,2048]{1,0:T(8,128)(2,1)S(1)}, u32[]{:S(2)}, u32[]{:S(2)}) collective-permute-start(bf16[272,2048]{1,0:T(8,128)(2,1)S(1)} %get-tuple-element.144), channel_id=1, source_target_pairs={{0,1},{1,0},{2,3},{3,2},{4,5},{5,4},{6,7},{7,6},{8,9},{9,8},{10,11... | collective-permute-start | bytes 3342344 | tf_op jit(solution)/shard_map/ppermute | solution.py:42
  102.6 16.0 %collective-permute-start.30 = (bf16[256,2048]{1,0:T(8,128)(2,1)S(1)}, bf16[256,2048]{1,0:T(8,128)(2,1)S(1)}, u32[]{:S(2)}, u32[]{:S(2)}) collective-permute-start(bf16[256,2048]{1,0:T(8,128)(2,1)S(1)} %get-tuple-element.149), channel_id=1, source_target_pairs={{0,1},{1,0},{2,3},{3,2},{4,5},{5,4},{6,7},{7,6},{8,9},{9,8},{10,11... | collective-permute-start | bytes 3145736 | tf_op jit(solution)/shard_map/ppermute | solution.py:42
  105.6 13.0 %collective-permute-start.25 = (bf16[64,2048]{1,0:T(8,128)(2,1)S(1)}, bf16[64,2048]{1,0:T(8,128)(2,1)S(1)}, u32[]{:S(2)}, u32[]{:S(2)}) collective-permute-start(bf16[64,2048]{1,0:T(8,128)(2,1)S(1)} %get-tuple-element.145), channel_id=1, source_target_pairs={{0,32},{32,0},{64,96},{96,64},{128,160},{160,128},{192,224},{224,1... | collective-permute-start | bytes 786440 | tf_op jit(solution)/shard_map/ppermute | solution.py:50
  105.7 14.4 %collective-permute-start.26 = (bf16[64,2048]{1,0:T(8,128)(2,1)S(1)}, bf16[64,2048]{1,0:T(8,128)(2,1)S(1)}, u32[]{:S(2)}, u32[]{:S(2)}) collective-permute-start(bf16[64,2048]{1,0:T(8,128)(2,1)S(1)} %get-tuple-element.146), channel_id=1, source_target_pairs={{0,64},{32,96},{64,0},{96,32},{128,192},{160,224},{192,128},{224,1... | collective-permute-start | bytes 786440 | tf_op jit(solution)/shard_map/ppermute | solution.py:50
  108.1 14.6 %collective-permute-start.27 = (bf16[64,2048]{1,0:T(8,128)(2,1)S(1)}, bf16[64,2048]{1,0:T(8,128)(2,1)S(1)}, u32[]{:S(2)}, u32[]{:S(2)}) collective-permute-start(bf16[64,2048]{1,0:T(8,128)(2,1)S(1)} %get-tuple-element.147), channel_id=1, source_target_pairs={{0,96},{32,64},{64,32},{96,0},{128,224},{160,192},{192,160},{224,1... | collective-permute-start | bytes 786440 | tf_op jit(solution)/shard_map/ppermute | solution.py:50
  110.4 3.7 %collective-permute-start.28 = (f32[1,2048]{1,0:T(1,128)S(1)}, f32[1,2048]{1,0:T(1,128)S(1)}, u32[]{:S(2)}, u32[]{:S(2)}) collective-permute-start(f32[1,2048]{1,0:T(1,128)S(1)} %get-tuple-element.148.a_ref), channel_id=1, source_target_pairs={{0,2},{1,3},{2,0},{3,1},{4,6},{5,7},{6,4},{7,5},{8,10},{9,11},{10,... | collective-permute-start | bytes 24584 | tf_op jit(solution)/shard_map/ppermute | solution.py:42
  114.0 4.5 %collective-permute-start.29 = (f32[1,2048]{1,0:T(1,128)S(1)}, f32[1,2048]{1,0:T(1,128)S(1)}, u32[]{:S(2)}, u32[]{:S(2)}) collective-permute-start(f32[1,2048]{1,0:T(1,128)S(1)} %add.7.a_ref), channel_id=1, source_target_pairs={{0,4},{1,5},{2,6},{3,7},{4,0},{5,1},{6,2},{7,3},{8,12},{9,13},{10,... | collective-permute-start | bytes 24584 | tf_op jit(solution)/shard_map/ppermute | solution.py:42
  122.8 10.3 %collective-permute-start.31 = (bf16[64,2048]{1,0:T(8,128)(2,1)S(1)}, bf16[64,2048]{1,0:T(8,128)(2,1)S(1)}, u32[]{:S(2)}, u32[]{:S(2)}) collective-permute-start(bf16[64,2048]{1,0:T(8,128)(2,1)S(1)} %get-tuple-element.159), channel_id=1, source_target_pairs={{0,128},{32,160},{64,192},{96,224},{128,0},{160,32},{192,64},{224,... | collective-permute-start | bytes 786440 | tf_op jit(solution)/shard_map/ppermute | solution.py:50
  124.3 3.7 %collective-permute-start.32 = (f32[1,2048]{1,0:T(1,128)S(1)}, f32[1,2048]{1,0:T(1,128)S(1)}, u32[]{:S(2)}, u32[]{:S(2)}) collective-permute-start(f32[1,2048]{1,0:T(1,128)S(1)} %get-tuple-element.160.a_ref), channel_id=1, source_target_pairs={{0,32},{32,0},{64,96},{96,64},{128,160},{160,128},{192,224},{224,1... | collective-permute-start | bytes 24584 | tf_op jit(solution)/shard_map/ppermute | solution.py:50
  128.0 5.2 %collective-permute-start.33 = (f32[1,2048]{1,0:T(1,128)S(1)}, f32[1,2048]{1,0:T(1,128)S(1)}, u32[]{:S(2)}, u32[]{:S(2)}) collective-permute-start(f32[1,2048]{1,0:T(1,128)S(1)} %add.9.a_ref), channel_id=1, source_target_pairs={{0,64},{32,96},{64,0},{96,32},{128,192},{160,224},{192,128},{224,1... | collective-permute-start | bytes 24584 | tf_op jit(solution)/shard_map/ppermute | solution.py:50
  133.2 21.2 %collective-permute-start.36 = (bf16[64,2048]{1,0:T(8,128)(2,1)S(1)}, bf16[64,2048]{1,0:T(8,128)(2,1)S(1)}, u32[]{:S(2)}, u32[]{:S(2)}) collective-permute-start(bf16[64,2048]{1,0:T(8,128)(2,1)S(1)} %get-tuple-element.161.refs_0_), channel_id=1, source_target_pairs={{0,96},{32,64},{64,32},{96,0},{128,224},{160,192},{192,160},{224,1... | collective-permute-start | bytes 786440 | tf_op jit(solution)/shard_map/ppermute | solution.py:50
  135.6 18.8 %collective-permute-start.35 = (bf16[64,2048]{1,0:T(8,128)(2,1)S(1)}, bf16[64,2048]{1,0:T(8,128)(2,1)S(1)}, u32[]{:S(2)}, u32[]{:S(2)}) collective-permute-start(bf16[64,2048]{1,0:T(8,128)(2,1)S(1)} %get-tuple-element.161.refs_0_), channel_id=1, source_target_pairs={{0,64},{32,96},{64,0},{96,32},{128,192},{160,224},{192,128},{224,1... | collective-permute-start | bytes 786440 | tf_op jit(solution)/shard_map/ppermute | solution.py:50
  135.6 18.8 %collective-permute-start.34 = (bf16[64,2048]{1,0:T(8,128)(2,1)S(1)}, bf16[64,2048]{1,0:T(8,128)(2,1)S(1)}, u32[]{:S(2)}, u32[]{:S(2)}) collective-permute-start(bf16[64,2048]{1,0:T(8,128)(2,1)S(1)} %get-tuple-element.161.refs_0_), channel_id=1, source_target_pairs={{0,32},{32,0},{64,96},{96,64},{128,160},{160,128},{192,224},{224,1... | collective-permute-start | bytes 786440 | tf_op jit(solution)/shard_map/ppermute | solution.py:50
  137.4 7.6 %collective-permute-start.37 = (f32[1,2048]{1,0:T(1,128)S(1)}, f32[1,2048]{1,0:T(1,128)S(1)}, u32[]{:S(2)}, u32[]{:S(2)}) collective-permute-start(f32[1,2048]{1,0:T(1,128)S(1)} %get-tuple-element.162.a_ref), channel_id=1, source_target_pairs={{0,8},{1,9},{2,10},{3,11},{4,12},{5,13},{6,14},{7,15},{8,0},{9,1},... | collective-permute-start | bytes 24584 | tf_op jit(solution)/shard_map/ppermute | solution.py:42
  144.9 3.7 %collective-permute-start.38 = (f32[1,2048]{1,0:T(1,128)S(1)}, f32[1,2048]{1,0:T(1,128)S(1)}, u32[]{:S(2)}, u32[]{:S(2)}) collective-permute-start(f32[1,2048]{1,0:T(1,128)S(1)} %add.11.a_ref), channel_id=1, source_target_pairs={{0,16},{1,17},{2,18},{3,19},{4,20},{5,21},{6,22},{7,23},{8,24},{9,... | collective-permute-start | bytes 24584 | tf_op jit(solution)/shard_map/ppermute | solution.py:42
  148.6 5.2 %collective-permute-start.39 = (f32[1,2048]{1,0:T(1,128)S(1)}, f32[1,2048]{1,0:T(1,128)S(1)}, u32[]{:S(2)}, u32[]{:S(2)}) collective-permute-start(f32[1,2048]{1,0:T(1,128)S(1)} %add.12.a_ref), channel_id=1, source_target_pairs={{0,128},{32,160},{64,192},{96,224},{128,0},{160,32},{192,64},{224,... | collective-permute-start | bytes 24584 | tf_op jit(solution)/shard_map/ppermute | solution.py:50
where the time goes:
time: 157 us; the launch traced here: 156 us
  waiting for transfers between devices  80.5 us (51%)
  starting transfers between devices  49.1 us (31%)
  Pallas kernels  23.1 us (15%)
  local copies, waits for them, and re-layouts  2.27 us (1%)
    ppermute x25, waiting for transfers between devices, dp_swap(): return lax.ppermute(x, 'dp', pairs)  43.7 us
    ppermute x15, waiting for transfers between devices, section_swap(): return lax.ppermute(x, 'section', pairs)  36.8 us
    ppermute x25, starting transfers between devices, dp_swap(): return lax.ppermute(x, 'dp', pairs)  27.4 us
    ppermute x15, starting transfers between devices, section_swap(): return lax.ppermute(x, 'section', pairs)  21.7 us
    pallas_call x1, Pallas kernels, attend(): pl.pallas_call(main_kernel, in_specs=[VMEM] * (N_SLOT + 12) + [SMEM] + [V...  14.7 us
    pallas_call x18, Pallas kernels, small_call(): pl.pallas_call(kernel, in_specs=[SMEM] * len(first) + [VMEM] * len(args),...  4.91 us
  transfers between devices with their start and end apart: 40, of which 22 were waited for; matrix products, arithmetic and copies ran while one was open for 0% of the time, Pallas kernels for 4%

commit v1 on v0

--- a/solution.py
+++ b/solution.py
@@ -158,6 +158,10 @@
         (rows_ref.at[:, cols], give_ref.at[:, pl.ds(0, F)]),
         (cot_ref.at[:, cols], give_ref.at[:, pl.ds(F, F)]),
     ], sems)
+
+
+def butterfly_kernel(a_ref, b_ref, c_ref, d_ref, out_ref):
+    out_ref[...] = (a_ref[...] + b_ref[...]) + (c_ref[...] + d_ref[...])
 
 
 def select_kernel(step, map_ref, own_ref, got_ref, *outs):
@@ -489,31 +493,30 @@
     up = from_above(b[1])
     a[-3] = order.take(down)
     down, across_3 = from_below(a[-3]), other_column(a[-3])
+    b[-2] = order.take(across_2)
     hidden = order.take(hidden)
     own_a = small_call(stack_kernel, bf16_rows(PIECE), (mine, hidden), "stack", limit=3)
-    hidden, oth_a = other_y(own_a, 2), other_core(own_a)
-    b[-2] = order.take(across_2)
+    hidden = other_y(own_a, 2)
 
     a[4] = order.take(down)
     down, across_4 = from_below(b[0]), other_column(a[4])
     b[2] = order.take(up)
     up = from_above(b[2])
-    b[-3], oth_a = order.take(across_3, oth_a)
+    b[-3] = order.take(across_3)
     own_b = order.take(hidden)
-    oth_b = other_core(own_b)
+    oth_a, oth_b = other_core(own_a), other_core(own_b)
     b[3] = order.take(up)
     b[-1] = order.take(down)
     b[4] = order.take(across_4)
-    oth_b = order.take(oth_b)
+    oth_a, oth_b = order.take(oth_a, oth_b)
     units = [(a, b)[column][offset] for column, offset in SLOTS]
 
     def normalise(*pieces):
         outs = [bf16_rows(PIECE), jax.ShapeDtypeStruct((PIECE, 128), f32)] * len(pieces)
         return small_call(norm_kernel, outs, (gain, *pieces), "norm")
 
-    enc_0, inv_0, enc_2, inv_2 = normalise(own_a, oth_a)
-    enc_1, inv_1 = normalise(own_b)
-    enc_3, inv_3 = normalise(oth_b)
+    enc_0, inv_0, enc_1, inv_1 = normalise(own_a, own_b)
+    enc_2, inv_2, enc_3, inv_3 = normalise(oth_a, oth_b)
     dh_enc, gp_enc, enc_out = small_call(
         encoder_kernel, [bf16_rows(LEN), LINE, bf16_rows(LEN)], (gain, cot, own_a, own_b), "encoder",
         where=section_map,
@@ -541,7 +544,9 @@
         sum_kernel, [ROWS32, quarter, LINE], (kept, gain_part, near, far, other), "sum"
     )
     crossed = other_high(sent)
-    gain_part = add_from(gain_part, lambda v: other_y(v, 1), lambda v: other_y(v, 2))
+    gain_part = small_call(
+        butterfly_kernel, LINE, (gain_part, *[other_y(gain_part, bits) for bits in (1, 2, 3)]), "add", limit=1
+    )
     dh, gain_part = small_call(last_kernel, [quarter, LINE], (kept, crossed, gain_part), "last")
     far, near, other = other_y(dh, 2), other_y(dh, 1), other_y(dh, 3)
     gain_part = add_from(gain_part, z_move(4), other_column, other_high)

time: 157 us -> 156 us (level)
  waiting for transfers between devices: 80.5 us -> 78.4 us
    ppermute x15 -> x16, waiting for transfers between devices: 36.8 us -> 29.7 us  [section_swap(): return lax.ppermute(x, 'section', pairs)]
    ppermute x25, waiting for transfers between devices: 43.7 us -> 48.7 us  [dp_swap(): return lax.ppermute(x, 'dp', pairs)]
    ppermute x15 -> x16, starting transfers between devices: 21.7 us -> 24.1 us  [section_swap(): return lax.ppermute(x, 'section', pairs)]
    ppermute x25, starting transfers between devices: 27.4 us -> 25.5 us  [dp_swap(): return lax.ppermute(x, 'dp', pairs)]
    pallas_call x18 -> x16, Pallas kernels: 4.91 us -> 4.96 us  [small_call(): pl.pallas_call(kernel, in_specs=[SMEM] * len(first) + [VMEM] * len(args),...]
  transfers between devices with their start and end apart: 40 -> 41, of which waited for: 22 -> 20; matrix products, arithmetic and copies ran while one was open for 0% -> 0% of each run, Pallas kernels for 4% -> 4%
where the time goes in v1:
time: 156 us; the launch traced here: 155 us
  waiting for transfers between devices  78.4 us (50%)
  starting transfers between devices  49.6 us (32%)
  Pallas kernels  23.2 us (15%)
  local copies, waits for them, and re-layouts  2.27 us (1%)
    ppermute x25, waiting for transfers between devices, dp_swap(): return lax.ppermute(x, 'dp', pairs)  48.7 us
    ppermute x16, waiting for transfers between devices, section_swap(): return lax.ppermute(x, 'section', pairs)  29.7 us
    ppermute x25, starting transfers between devices, dp_swap(): return lax.ppermute(x, 'dp', pairs)  25.5 us
    ppermute x16, starting transfers between devices, section_swap(): return lax.ppermute(x, 'section', pairs)  24.1 us
    pallas_call x1, Pallas kernels, attend(): pl.pallas_call(main_kernel, in_specs=[VMEM] * (N_SLOT + 12) + [SMEM] + [V...  14.7 us
    pallas_call x16, Pallas kernels, small_call(): pl.pallas_call(kernel, in_specs=[SMEM] * len(first) + [VMEM] * len(args),...  4.96 us
  transfers between devices with their start and end apart: 41, of which 20 were waited for; matrix products, arithmetic and copies ran while one was open for 0% of the time, Pallas kernels for 4%

profile of v1, /device:TPU:6, one launch (start us, length us, event | category | flops | bytes accessed | tf_op | source)
XLA Modules:
  0.0 154.5 jit_solution(12793340501753803370)
XLA Ops:
  0.6 1.0 copy-done.3
  1.7 0.1 columns.1
  1.8 0.1 collective-permute-start
  1.9 1.2 copy-done
  3.2 3.3 %collective-permute-start.2 = (bf16[128,2048]{1,0:T(8,128)(2,1)S(1)}, bf16[128,2048]{1,0:T(8,128)(2,1)S(1)}, u32[]{:S(2)}, u32[]{:S(2)}) collective-permute-start(bf16[128,2048]{1,0:T(8,128)(2,1)S(1)} %half.1), channel_id=1, source_target_pairs={{0,64},{32,96},{64,0},{96,32},{128,192},{160,224},{192,128},{224,1... | collective-permute-start | bytes 1572872 | tf_op jit(solution)/shard_map/ppermute | solution.py:50
  6.6 0.1 give.1
  6.7 0.3 collective-permute-start.5
  7.0 5.9 %collective-permute-start.1 = (bf16[128,2048]{1,0:T(8,128)(2,1)S(1)}, bf16[128,2048]{1,0:T(8,128)(2,1)S(1)}, u32[]{:S(2)}, u32[]{:S(2)}) collective-permute-start(bf16[128,2048]{1,0:T(8,128)(2,1)S(1)} %unit.1.token_ref.refs_0_), channel_id=1, source_target_pairs={{0,14},{1,15},{2,0},{3,1},{4,2},{5,3},{6,4},{7,5},{8,6},{9,7},{10,... | collective-permute-start | bytes 1572872 | tf_op jit(solution)/shard_map/ppermute | solution.py:42
  12.9 0.8 collective-permute-start.4
  13.7 5.4 %collective-permute-done.2.refs_0_ = bf16[128,2048]{1,0:T(8,128)(2,1)S(1)} collective-permute-done((bf16[128,2048]{1,0:T(8,128)(2,1)S(1)}, bf16[128,2048]{1,0:T(8,128)(2,1)S(1)}, u32[]{:S(2)}, u32[]{:S(2)}) %collective-permute-start.2) | collective-permute-done | bytes 524320 | tf_op jit(solution)/shard_map/ppermute | solution.py:50
  19.1 5.4 %collective-permute-done.1.refs_0_ = bf16[128,2048]{1,0:T(8,128)(2,1)S(1)} collective-permute-done((bf16[128,2048]{1,0:T(8,128)(2,1)S(1)}, bf16[128,2048]{1,0:T(8,128)(2,1)S(1)}, u32[]{:S(2)}, u32[]{:S(2)}) %collective-permute-start.1) | collective-permute-done | bytes 524320 | tf_op jit(solution)/shard_map/ppermute | solution.py:42
  24.5 3.7 %collective-permute-start.6 = (bf16[128,2048]{1,0:T(8,128)(2,1)S(1)}, bf16[128,2048]{1,0:T(8,128)(2,1)S(1)}, u32[]{:S(2)}, u32[]{:S(2)}) collective-permute-start(bf16[128,2048]{1,0:T(8,128)(2,1)S(1)} %get-tuple-element.87.refs_1_), channel_id=1, source_target_pairs={{0,14},{1,15},{2,0},{3,1},{4,2},{5,3},{6,4},{7,5},{8,6},{9,7},{10,... | collective-permute-start | bytes 1572872 | tf_op jit(solution)/shard_map/ppermute | solution.py:42
  28.2 0.6 select.3
  28.8 0.8 collective-permute-start.7
  29.6 0.8 collective-permute-start.9
  30.4 5.9 %collective-permute-done.7.refs_0_ = bf16[64,2048]{1,0:T(8,128)(2,1)S(1)} collective-permute-done((bf16[64,2048]{1,0:T(8,128)(2,1)S(1)}, bf16[64,2048]{1,0:T(8,128)(2,1)S(1)}, u32[]{:S(2)}, u32[]{:S(2)}) %collective-permute-start.7) | collective-permute-done | bytes 262176 | tf_op jit(solution)/shard_map/ppermute | solution.py:50
  36.3 2.7 %collective-permute-done.6.refs_0_ = bf16[128,2048]{1,0:T(8,128)(2,1)S(1)} collective-permute-done((bf16[128,2048]{1,0:T(8,128)(2,1)S(1)}, bf16[128,2048]{1,0:T(8,128)(2,1)S(1)}, u32[]{:S(2)}, u32[]{:S(2)}) %collective-permute-start.6) | collective-permute-done | bytes 524320 | tf_op jit(solution)/shard_map/ppermute | solution.py:42
  39.0 3.7 %collective-permute-start.10 = (bf16[128,2048]{1,0:T(8,128)(2,1)S(1)}, bf16[128,2048]{1,0:T(8,128)(2,1)S(1)}, u32[]{:S(2)}, u32[]{:S(2)}) collective-permute-start(bf16[128,2048]{1,0:T(8,128)(2,1)S(1)} %get-tuple-element.96.refs_4_), channel_id=1, source_target_pairs={{0,14},{1,15},{2,0},{3,1},{4,2},{5,3},{6,4},{7,5},{8,6},{9,7},{10,... | collective-permute-start | bytes 1572872 | tf_op jit(solution)/shard_map/ppermute | solution.py:42
  42.7 0.6 select.4.own_ref
  43.3 1.5 collective-permute-start.11
  44.8 9.3 %collective-permute-done.11.refs_0_ = bf16[64,2048]{1,0:T(8,128)(2,1)S(1)} collective-permute-done((bf16[64,2048]{1,0:T(8,128)(2,1)S(1)}, bf16[64,2048]{1,0:T(8,128)(2,1)S(1)}, u32[]{:S(2)}, u32[]{:S(2)}) %collective-permute-start.11) | collective-permute-done | bytes 262176 | tf_op jit(solution)/shard_map/ppermute | solution.py:50
  54.1 0.6 select.5.refs_0_
  54.7 0.8 collective-permute-start.15
  55.5 0.5 collective-permute-done.12.refs_0_
  56.0 3.2 %collective-permute-start.16 = (bf16[128,2048]{1,0:T(8,128)(2,1)S(1)}, bf16[128,2048]{1,0:T(8,128)(2,1)S(1)}, u32[]{:S(2)}, u32[]{:S(2)}) collective-permute-start(bf16[128,2048]{1,0:T(8,128)(2,1)S(1)} %get-tuple-element.100.refs_6_), channel_id=1, source_target_pairs={{0,14},{1,15},{2,0},{3,1},{4,2},{5,3},{6,4},{7,5},{8,6},{9,7},{10,... | collective-permute-start | bytes 1572872 | tf_op jit(solution)/shard_map/ppermute | solution.py:42
  59.2 0.8 collective-permute-start.17
  60.0 2.7 %collective-permute-done.13.refs_0_ = bf16[128,2048]{1,0:T(8,128)(2,1)S(1)} collective-permute-done((bf16[128,2048]{1,0:T(8,128)(2,1)S(1)}, bf16[128,2048]{1,0:T(8,128)(2,1)S(1)}, u32[]{:S(2)}, u32[]{:S(2)}) %collective-permute-start.13) | collective-permute-done | bytes 524320 | tf_op jit(solution)/shard_map/ppermute | solution.py:42
  62.8 1.3 collective-permute-start.19
  64.1 7.9 %collective-permute-done.14.refs_0_ = bf16[128,2048]{1,0:T(8,128)(2,1)S(1)} collective-permute-done((bf16[128,2048]{1,0:T(8,128)(2,1)S(1)}, bf16[128,2048]{1,0:T(8,128)(2,1)S(1)}, u32[]{:S(2)}, u32[]{:S(2)}) %collective-permute-start.14) | collective-permute-done | bytes 524320 | tf_op jit(solution)/shard_map/ppermute | solution.py:42
  72.0 0.3 collective-permute-start.18
  72.3 1.3 collective-permute-start.21
  73.7 0.7 norm.2
  74.4 0.6 encoder.1
  75.0 11.4 %collective-permute-done.18.refs_0_ = bf16[128,2048]{1,0:T(8,128)(2,1)S(1)} collective-permute-done((bf16[128,2048]{1,0:T(8,128)(2,1)S(1)}, bf16[128,2048]{1,0:T(8,128)(2,1)S(1)}, u32[]{:S(2)}, u32[]{:S(2)}) %collective-permute-start.18) | collective-permute-done | bytes 524320 | tf_op jit(solution)/shard_map/ppermute | solution.py:42
  86.5 0.7 norm.3
  87.2 14.7 %attend.1 = (bf16[256,2048]{1,0:T(8,128)(2,1)S(1)}, bf16[256,2048]{1,0:T(8,128)(2,1)S(1)}, bf16[256,2048]{1,0:T(8,128)(2,1)S(1)}, bf16[272,2048]{1,0:T(8,128)(2,1)S(1)}, f32[1,2048]{1,0:T(1,128)S(1)}) custom-call(bf16[128,2048]{1,0:T(8,128)(2,1)S(1)} %unit.1.token_ref.refs_0_, bf16[128,2048]{1,0:T(8,128)(2,1)S(1)} %get-tuple-element.87.refs_1_, ...), custom_call_target="tpu_custom_call" | custom-call | flops 10000000000 | bytes 20000000 | tf_op jit(solution)/shard_map/attend/pallas_call | solution.py:328
  102.0 0.3 collective-permute-start.24
  102.3 0.5 collective-permute-start.30
  102.8 2.2 %collective-permute-done.24.got_ref = bf16[272,2048]{1,0:T(8,128)(2,1)S(1)} collective-permute-done((bf16[272,2048]{1,0:T(8,128)(2,1)S(1)}, bf16[272,2048]{1,0:T(8,128)(2,1)S(1)}, u32[]{:S(2)}, u32[]{:S(2)}) %collective-permute-start.24) | collective-permute-done | bytes 1114144 | tf_op jit(solution)/shard_map/ppermute | solution.py:42
  105.0 0.3 split.1
  105.3 2.1 %collective-permute-start.25 = (bf16[64,2048]{1,0:T(8,128)(2,1)S(1)}, bf16[64,2048]{1,0:T(8,128)(2,1)S(1)}, u32[]{:S(2)}, u32[]{:S(2)}) collective-permute-start(bf16[64,2048]{1,0:T(8,128)(2,1)S(1)} %get-tuple-element.145), channel_id=1, source_target_pairs={{0,32},{32,0},{64,96},{96,64},{128,160},{160,128},{192,224},{224,1... | collective-permute-start | bytes 786440 | tf_op jit(solution)/shard_map/ppermute | solution.py:50
  107.4 0.3 collective-permute-start.26
  107.7 2.4 %collective-permute-start.27 = (bf16[64,2048]{1,0:T(8,128)(2,1)S(1)}, bf16[64,2048]{1,0:T(8,128)(2,1)S(1)}, u32[]{:S(2)}, u32[]{:S(2)}) collective-permute-start(bf16[64,2048]{1,0:T(8,128)(2,1)S(1)} %get-tuple-element.147), channel_id=1, source_target_pairs={{0,96},{32,64},{64,32},{96,0},{128,224},{160,192},{192,160},{224,1... | collective-permute-start | bytes 786440 | tf_op jit(solution)/shard_map/ppermute | solution.py:50
  110.2 1.6 %collective-permute-start.28 = (f32[1,2048]{1,0:T(1,128)S(1)}, f32[1,2048]{1,0:T(1,128)S(1)}, u32[]{:S(2)}, u32[]{:S(2)}) collective-permute-start(f32[1,2048]{1,0:T(1,128)S(1)} %get-tuple-element.148.a_ref), channel_id=1, source_target_pairs={{0,2},{1,3},{2,0},{3,1},{4,6},{5,7},{6,4},{7,5},{8,10},{9,11},{10,... | collective-permute-start | bytes 24584 | tf_op jit(solution)/shard_map/ppermute | solution.py:42
  111.8 2.0 %collective-permute-done.28.b_ref = f32[1,2048]{1,0:T(1,128)S(1)} collective-permute-done((f32[1,2048]{1,0:T(1,128)S(1)}, f32[1,2048]{1,0:T(1,128)S(1)}, u32[]{:S(2)}, u32[]{:S(2)}) %collective-permute-start.28) | collective-permute-done | bytes 8224 | tf_op jit(solution)/shard_map/ppermute | solution.py:42
  113.8 4.5 %collective-permute-done.29.b_ref = f32[1,2048]{1,0:T(1,128)S(1)} collective-permute-done((f32[1,2048]{1,0:T(1,128)S(1)}, f32[1,2048]{1,0:T(1,128)S(1)}, u32[]{:S(2)}, u32[]{:S(2)}) %collective-permute-start.29) | collective-permute-done | bytes 8224 | tf_op jit(solution)/shard_map/ppermute | solution.py:42
  118.4 1.4 collective-permute-done.26.refs_1_
  119.8 2.6 %collective-permute-done.27.refs_2_ = bf16[64,2048]{1,0:T(8,128)(2,1)S(1)} collective-permute-done((bf16[64,2048]{1,0:T(8,128)(2,1)S(1)}, bf16[64,2048]{1,0:T(8,128)(2,1)S(1)}, u32[]{:S(2)}, u32[]{:S(2)}) %collective-permute-start.27) | collective-permute-done | bytes 262176 | tf_op jit(solution)/shard_map/ppermute | solution.py:50
  122.4 0.1 sum.1
  122.5 0.9 collective-permute-start.31
  123.4 3.0 %collective-permute-start.34 = (f32[1,2048]{1,0:T(1,128)S(1)}, f32[1,2048]{1,0:T(1,128)S(1)}, u32[]{:S(2)}, u32[]{:S(2)}) collective-permute-start(f32[1,2048]{1,0:T(1,128)S(1)} %get-tuple-element.160.a_ref), channel_id=1, source_target_pairs={{0,96},{32,64},{64,32},{96,0},{128,224},{160,192},{192,160},{224,1... | collective-permute-start | bytes 24584 | tf_op jit(solution)/shard_map/ppermute | solution.py:50
  126.4 1.1 collective-permute-start.32
  127.5 0.8 collective-permute-done.34.d_ref
  128.3 3.2 %collective-permute-done.33.c_ref = f32[1,2048]{1,0:T(1,128)S(1)} collective-permute-done((f32[1,2048]{1,0:T(1,128)S(1)}, f32[1,2048]{1,0:T(1,128)S(1)}, u32[]{:S(2)}, u32[]{:S(2)}) %collective-permute-start.33) | collective-permute-done | bytes 8224 | tf_op jit(solution)/shard_map/ppermute | solution.py:50
  131.6 2.5 %collective-permute-start.37 = (bf16[64,2048]{1,0:T(8,128)(2,1)S(1)}, bf16[64,2048]{1,0:T(8,128)(2,1)S(1)}, u32[]{:S(2)}, u32[]{:S(2)}) collective-permute-start(bf16[64,2048]{1,0:T(8,128)(2,1)S(1)} %get-tuple-element.161.refs_0_), channel_id=1, source_target_pairs={{0,96},{32,64},{64,32},{96,0},{128,224},{160,192},{192,160},{224,1... | collective-permute-start | bytes 786440 | tf_op jit(solution)/shard_map/ppermute | solution.py:50
  134.1 1.7 %collective-permute-start.35 = (bf16[64,2048]{1,0:T(8,128)(2,1)S(1)}, bf16[64,2048]{1,0:T(8,128)(2,1)S(1)}, u32[]{:S(2)}, u32[]{:S(2)}) collective-permute-start(bf16[64,2048]{1,0:T(8,128)(2,1)S(1)} %get-tuple-element.161.refs_0_), channel_id=1, source_target_pairs={{0,32},{32,0},{64,96},{96,64},{128,160},{160,128},{192,224},{224,1... | collective-permute-start | bytes 786440 | tf_op jit(solution)/shard_map/ppermute | solution.py:50
  135.8 2.0 %collective-permute-start.38 = (f32[1,2048]{1,0:T(1,128)S(1)}, f32[1,2048]{1,0:T(1,128)S(1)}, u32[]{:S(2)}, u32[]{:S(2)}) collective-permute-start(f32[1,2048]{1,0:T(1,128)S(1)} %get-tuple-element.162.a_ref), channel_id=1, source_target_pairs={{0,8},{1,9},{2,10},{3,11},{4,12},{5,13},{6,14},{7,15},{8,0},{9,1},... | collective-permute-start | bytes 24584 | tf_op jit(solution)/shard_map/ppermute | solution.py:42
  137.8 5.5 %collective-permute-done.38.b_ref = f32[1,2048]{1,0:T(1,128)S(1)} collective-permute-done((f32[1,2048]{1,0:T(1,128)S(1)}, f32[1,2048]{1,0:T(1,128)S(1)}, u32[]{:S(2)}, u32[]{:S(2)}) %collective-permute-start.38) | collective-permute-done | bytes 8224 | tf_op jit(solution)/shard_map/ppermute | solution.py:42
  143.4 3.6 %collective-permute-done.39.b_ref = f32[1,2048]{1,0:T(1,128)S(1)} collective-permute-done((f32[1,2048]{1,0:T(1,128)S(1)}, f32[1,2048]{1,0:T(1,128)S(1)}, u32[]{:S(2)}, u32[]{:S(2)}) %collective-permute-start.39) | collective-permute-done | bytes 8224 | tf_op jit(solution)/shard_map/ppermute | solution.py:42
  147.0 2.4 %collective-permute-start.40 = (f32[1,2048]{1,0:T(1,128)S(1)}, f32[1,2048]{1,0:T(1,128)S(1)}, u32[]{:S(2)}, u32[]{:S(2)}) collective-permute-start(f32[1,2048]{1,0:T(1,128)S(1)} %add.10.a_ref), channel_id=1, source_target_pairs={{0,128},{32,160},{64,192},{96,224},{128,0},{160,32},{192,64},{224,... | collective-permute-start | bytes 24584 | tf_op jit(solution)/shard_map/ppermute | solution.py:50
  149.5 1.6 %rows.1 = bf16[256,2048]{1,0:T(8,128)(2,1)} custom-call(s32[8]{0:T(128)S(1)} %copy-done.5, bf16[256,2048]{1,0:T(8,128)(2,1)S(1)} %get-tuple-element.141.own_ref, bf16[256,2048]{1,0:T(8,128)(2,1)S(1)} %get-tuple-element.151.oth_ref, bf16[256,2048]{1,0:T(8,128)(2,1)S(1)} %get-tuple-element.152.refs_0_), custom_call_target="tpu_custom_call" | custom-call | bytes 2000000 | tf_op jit(solution)/shard_map/rows/pallas_call | solution.py:437
  151.0 1.1 collective-permute-done.40.b_ref
  152.2 0.6 add.11
  152.8 1.6 %grads.1 = bf16[256,2048]{1,0:T(8,128)(2,1)} custom-call(s32[8]{0:T(128)S(1)} %copy-done.5, bf16[256,2048]{1,0:T(8,128)(2,1)S(1)} %get-tuple-element.141.own_ref, bf16[256,2048]{1,0:T(8,128)(2,1)S(1)} %get-tuple-element.151.oth_ref, bf16[64,2048]{1,0:T(8,128)(2,1)S(1)} %get-tuple-element.161.refs_0_, bf16[64,2048]{1,0:T(8,128)(2,1)S(1)} %collective-permute-done.35.refs_1_, ...), custom_call_target="tpu_custom_call" | custom-call | bytes 2000000 | tf_op jit(solution)/shard_map/grads/pallas_call | solution.py:437
  (75 shorter events, 0.4 us)
Async XLA Ops:
  0.6 1.0 copy-start.3
  1.8 4.7 %collective-permute-start = (bf16[64,2048]{1,0:T(8,128)(2,1)S(1)}, bf16[64,2048]{1,0:T(8,128)(2,1)S(1)}, u32[]{:S(2)}, u32[]{:S(2)}) collective-permute-start(bf16[64,2048]{1,0:T(8,128)(2,1)S(1)} %get-tuple-element.84), channel_id=1, source_target_pairs={{0,1},{1,0},{2,3},{3,2},{4,5},{5,4},{6,7},{7,6},{8,9},{9,8},{10,11... | collective-permute-start | bytes 786440 | tf_op jit(solution)/shard_map/ppermute | solution.py:42
  1.9 1.2 copy-start
  3.1 3.4 %copy-start.1 = (bf16[1,256,2048]{2,1,0:T(8,128)(2,1)S(1)}, bf16[1,256,2048]{2,1,0:T(8,128)(2,1)}, u32[]{:S(2)}) copy-start(bf16[1,256,2048]{2,1,0:T(8,128)(2,1)} %param.5) | copy-start | bytes 3145732
  3.1 3.4 %copy-start.2 = (bf16[1,256,2048]{2,1,0:T(8,128)(2,1)S(1)}, bf16[1,256,2048]{2,1,0:T(8,128)(2,1)}, u32[]{:S(2)}) copy-start(bf16[1,256,2048]{2,1,0:T(8,128)(2,1)} %param.7) | copy-start | bytes 3145732
  3.2 15.9 %collective-permute-start.2 = (bf16[128,2048]{1,0:T(8,128)(2,1)S(1)}, bf16[128,2048]{1,0:T(8,128)(2,1)S(1)}, u32[]{:S(2)}, u32[]{:S(2)}) collective-permute-start(bf16[128,2048]{1,0:T(8,128)(2,1)S(1)} %half.1), channel_id=1, source_target_pairs={{0,64},{32,96},{64,0},{96,32},{128,192},{160,224},{192,128},{224,1... | collective-permute-start | bytes 1572872 | tf_op jit(solution)/shard_map/ppermute | solution.py:50
  6.7 21.5 %copy-start.5 = (s32[8]{0:T(128)S(1)}, s32[8]{0:T(128)}, u32[]{:S(2)}) copy-start(s32[8]{0:T(128)} %map_ref.11) | copy-start | bytes 100
  6.7 23.7 %collective-permute-start.5 = (bf16[256,2048]{1,0:T(8,128)(2,1)S(1)}, bf16[256,2048]{1,0:T(8,128)(2,1)S(1)}, u32[]{:S(2)}, u32[]{:S(2)}) collective-permute-start(bf16[256,2048]{1,0:T(8,128)(2,1)S(1)} %give.1), channel_id=1, source_target_pairs={{0,1},{1,0},{2,3},{3,2},{4,5},{5,4},{6,7},{7,6},{8,9},{9,8},{10,11... | collective-permute-start | bytes 3145736 | tf_op jit(solution)/shard_map/ppermute | solution.py:42
  7.0 17.5 %collective-permute-start.1 = (bf16[128,2048]{1,0:T(8,128)(2,1)S(1)}, bf16[128,2048]{1,0:T(8,128)(2,1)S(1)}, u32[]{:S(2)}, u32[]{:S(2)}) collective-permute-start(bf16[128,2048]{1,0:T(8,128)(2,1)S(1)} %unit.1.token_ref.refs_0_), channel_id=1, source_target_pairs={{0,14},{1,15},{2,0},{3,1},{4,2},{5,3},{6,4},{7,5},{8,6},{9,7},{10,... | collective-permute-start | bytes 1572872 | tf_op jit(solution)/shard_map/ppermute | solution.py:42
  12.9 15.3 %collective-permute-start.3 = (bf16[128,2048]{1,0:T(8,128)(2,1)S(1)}, bf16[128,2048]{1,0:T(8,128)(2,1)S(1)}, u32[]{:S(2)}, u32[]{:S(2)}) collective-permute-start(bf16[128,2048]{1,0:T(8,128)(2,1)S(1)} %unit.1.token_ref.refs_0_), channel_id=1, source_target_pairs={{0,2},{1,3},{2,4},{3,5},{4,6},{5,7},{6,8},{7,9},{8,10},{9,11},{10,... | collective-permute-start | bytes 1572872 | tf_op jit(solution)/shard_map/ppermute | solution.py:42
  12.9 16.7 %collective-permute-start.4 = (bf16[128,2048]{1,0:T(8,128)(2,1)S(1)}, bf16[128,2048]{1,0:T(8,128)(2,1)S(1)}, u32[]{:S(2)}, u32[]{:S(2)}) collective-permute-start(bf16[128,2048]{1,0:T(8,128)(2,1)S(1)} %unit.1.token_ref.refs_0_), channel_id=1, source_target_pairs={{0,16},{1,17},{2,18},{3,19},{4,20},{5,21},{6,22},{7,23},{8,24},{9,... | collective-permute-start | bytes 1572872 | tf_op jit(solution)/shard_map/ppermute | solution.py:42
  24.5 14.5 %collective-permute-start.6 = (bf16[128,2048]{1,0:T(8,128)(2,1)S(1)}, bf16[128,2048]{1,0:T(8,128)(2,1)S(1)}, u32[]{:S(2)}, u32[]{:S(2)}) collective-permute-start(bf16[128,2048]{1,0:T(8,128)(2,1)S(1)} %get-tuple-element.87.refs_1_), channel_id=1, source_target_pairs={{0,14},{1,15},{2,0},{3,1},{4,2},{5,3},{6,4},{7,5},{8,6},{9,7},{10,... | collective-permute-start | bytes 1572872 | tf_op jit(solution)/shard_map/ppermute | solution.py:42
  28.2 14.5 %collective-permute-start.8 = (bf16[128,2048]{1,0:T(8,128)(2,1)S(1)}, bf16[128,2048]{1,0:T(8,128)(2,1)S(1)}, u32[]{:S(2)}, u32[]{:S(2)}) collective-permute-start(bf16[128,2048]{1,0:T(8,128)(2,1)S(1)} %get-tuple-element.89.refs_2_), channel_id=1, source_target_pairs={{0,2},{1,3},{2,4},{3,5},{4,6},{5,7},{6,8},{7,9},{8,10},{9,11},{10,... | collective-permute-start | bytes 1572872 | tf_op jit(solution)/shard_map/ppermute | solution.py:42
  28.8 7.5 %collective-permute-start.7 = (bf16[64,2048]{1,0:T(8,128)(2,1)S(1)}, bf16[64,2048]{1,0:T(8,128)(2,1)S(1)}, u32[]{:S(2)}, u32[]{:S(2)}) collective-permute-start(bf16[64,2048]{1,0:T(8,128)(2,1)S(1)} %get-tuple-element.93), channel_id=1, source_target_pairs={{0,32},{32,0},{64,96},{96,64},{128,160},{160,128},{192,224},{224,1... | collective-permute-start | bytes 786440 | tf_op jit(solution)/shard_map/ppermute | solution.py:50
  29.6 15.2 %collective-permute-start.9 = (bf16[128,2048]{1,0:T(8,128)(2,1)S(1)}, bf16[128,2048]{1,0:T(8,128)(2,1)S(1)}, u32[]{:S(2)}, u32[]{:S(2)}) collective-permute-start(bf16[128,2048]{1,0:T(8,128)(2,1)S(1)} %get-tuple-element.87.refs_1_), channel_id=1, source_target_pairs={{0,16},{1,17},{2,18},{3,19},{4,20},{5,21},{6,22},{7,23},{8,24},{9,... | collective-permute-start | bytes 1572872 | tf_op jit(solution)/shard_map/ppermute | solution.py:42
  39.0 16.5 %collective-permute-start.10 = (bf16[128,2048]{1,0:T(8,128)(2,1)S(1)}, bf16[128,2048]{1,0:T(8,128)(2,1)S(1)}, u32[]{:S(2)}, u32[]{:S(2)}) collective-permute-start(bf16[128,2048]{1,0:T(8,128)(2,1)S(1)} %get-tuple-element.96.refs_4_), channel_id=1, source_target_pairs={{0,14},{1,15},{2,0},{3,1},{4,2},{5,3},{6,4},{7,5},{8,6},{9,7},{10,... | collective-permute-start | bytes 1572872 | tf_op jit(solution)/shard_map/ppermute | solution.py:42
  42.7 13.3 %collective-permute-start.12 = (bf16[128,2048]{1,0:T(8,128)(2,1)S(1)}, bf16[128,2048]{1,0:T(8,128)(2,1)S(1)}, u32[]{:S(2)}, u32[]{:S(2)}) collective-permute-start(bf16[128,2048]{1,0:T(8,128)(2,1)S(1)} %get-tuple-element.98.refs_5_), channel_id=1, source_target_pairs={{0,2},{1,3},{2,4},{3,5},{4,6},{5,7},{6,8},{7,9},{8,10},{9,11},{10,... | collective-permute-start | bytes 1572872 | tf_op jit(solution)/shard_map/ppermute | solution.py:42
  43.3 10.8 %collective-permute-start.11 = (bf16[64,2048]{1,0:T(8,128)(2,1)S(1)}, bf16[64,2048]{1,0:T(8,128)(2,1)S(1)}, u32[]{:S(2)}, u32[]{:S(2)}) collective-permute-start(bf16[64,2048]{1,0:T(8,128)(2,1)S(1)} %select.4.own_ref), channel_id=1, source_target_pairs={{0,128},{32,160},{64,192},{96,224},{128,0},{160,32},{192,64},{224,... | collective-permute-start | bytes 786440 | tf_op jit(solution)/shard_map/ppermute | solution.py:50
  44.8 18.0 %collective-permute-start.13 = (bf16[128,2048]{1,0:T(8,128)(2,1)S(1)}, bf16[128,2048]{1,0:T(8,128)(2,1)S(1)}, u32[]{:S(2)}, u32[]{:S(2)}) collective-permute-start(bf16[128,2048]{1,0:T(8,128)(2,1)S(1)} %get-tuple-element.98.refs_5_), channel_id=1, source_target_pairs={{0,16},{1,17},{2,18},{3,19},{4,20},{5,21},{6,22},{7,23},{8,24},{9,... | collective-permute-start | bytes 1572872 | tf_op jit(solution)/shard_map/ppermute | solution.py:42
  54.7 8.1 %collective-permute-start.15 = (bf16[64,2048]{1,0:T(8,128)(2,1)S(1)}, bf16[64,2048]{1,0:T(8,128)(2,1)S(1)}, u32[]{:S(2)}, u32[]{:S(2)}) collective-permute-start(bf16[64,2048]{1,0:T(8,128)(2,1)S(1)} %select.5.refs_0_), channel_id=1, source_target_pairs={{0,32},{32,0},{64,96},{96,64},{128,160},{160,128},{192,224},{224,1... | collective-permute-start | bytes 786440 | tf_op jit(solution)/shard_map/ppermute | solution.py:50
  56.0 16.1 %collective-permute-start.14 = (bf16[128,2048]{1,0:T(8,128)(2,1)S(1)}, bf16[128,2048]{1,0:T(8,128)(2,1)S(1)}, u32[]{:S(2)}, u32[]{:S(2)}) collective-permute-start(bf16[128,2048]{1,0:T(8,128)(2,1)S(1)} %get-tuple-element.107.refs_8_), channel_id=1, source_target_pairs={{0,2},{1,3},{2,4},{3,5},{4,6},{5,7},{6,8},{7,9},{8,10},{9,11},{10,... | collective-permute-start | bytes 1572872 | tf_op jit(solution)/shard_map/ppermute | solution.py:42
  56.0 16.1 %collective-permute-start.16 = (bf16[128,2048]{1,0:T(8,128)(2,1)S(1)}, bf16[128,2048]{1,0:T(8,128)(2,1)S(1)}, u32[]{:S(2)}, u32[]{:S(2)}) collective-permute-start(bf16[128,2048]{1,0:T(8,128)(2,1)S(1)} %get-tuple-element.100.refs_6_), channel_id=1, source_target_pairs={{0,14},{1,15},{2,0},{3,1},{4,2},{5,3},{6,4},{7,5},{8,6},{9,7},{10,... | collective-permute-start | bytes 1572872 | tf_op jit(solution)/shard_map/ppermute | solution.py:42
  59.2 13.1 %collective-permute-start.17 = (bf16[128,2048]{1,0:T(8,128)(2,1)S(1)}, bf16[128,2048]{1,0:T(8,128)(2,1)S(1)}, u32[]{:S(2)}, u32[]{:S(2)}) collective-permute-start(bf16[128,2048]{1,0:T(8,128)(2,1)S(1)} %get-tuple-element.107.refs_8_), channel_id=1, source_target_pairs={{0,16},{1,17},{2,18},{3,19},{4,20},{5,21},{6,22},{7,23},{8,24},{9,... | collective-permute-start | bytes 1572872 | tf_op jit(solution)/shard_map/ppermute | solution.py:42
  62.8 10.9 %copy-start.4 = (f32[2048]{0:T(1024)S(1)}, f32[2048]{0:T(1024)}, u32[]{:S(2)}) copy-start(f32[2048]{0:T(1024)} %param.8) | copy-start | bytes 24580
  62.8 10.9 %collective-permute-start.19 = (bf16[128,2048]{1,0:T(8,128)(2,1)S(1)}, bf16[128,2048]{1,0:T(8,128)(2,1)S(1)}, u32[]{:S(2)}, u32[]{:S(2)}) collective-permute-start(bf16[128,2048]{1,0:T(8,128)(2,1)S(1)} %stack.1.refs_0_.a_ref.refs_20_), channel_id=1, source_target_pairs={{0,64},{32,96},{64,0},{96,32},{128,192},{160,224},{192,128},{224,1... | collective-permute-start | bytes 1572872 | tf_op jit(solution)/shard_map/ppermute | solution.py:50
  64.1 22.3 %collective-permute-start.20 = (bf16[128,2048]{1,0:T(8,128)(2,1)S(1)}, bf16[128,2048]{1,0:T(8,128)(2,1)S(1)}, u32[]{:S(2)}, u32[]{:S(2)}) collective-permute-start(bf16[128,2048]{1,0:T(8,128)(2,1)S(1)} %get-tuple-element.91.refs_3_), channel_id=1, source_target_pairs={{0,2},{1,3},{2,4},{3,5},{4,6},{5,7},{6,8},{7,9},{8,10},{9,11},{10,... | collective-permute-start | bytes 1572872 | tf_op jit(solution)/shard_map/ppermute | solution.py:42
  72.0 14.5 %collective-permute-start.22 = (bf16[128,2048]{1,0:T(8,128)(2,1)S(1)}, bf16[128,2048]{1,0:T(8,128)(2,1)S(1)}, u32[]{:S(2)}, u32[]{:S(2)}) collective-permute-start(bf16[128,2048]{1,0:T(8,128)(2,1)S(1)} %stack.1.refs_0_.a_ref.refs_20_), channel_id=1, source_target_pairs={{0,1},{1,0},{2,3},{3,2},{4,5},{5,4},{6,7},{7,6},{8,9},{9,8},{10,11... | collective-permute-start | bytes 1572872 | tf_op jit(solution)/shard_map/ppermute | solution.py:42
  72.0 14.3 %collective-permute-start.18 = (bf16[128,2048]{1,0:T(8,128)(2,1)S(1)}, bf16[128,2048]{1,0:T(8,128)(2,1)S(1)}, u32[]{:S(2)}, u32[]{:S(2)}) collective-permute-start(bf16[128,2048]{1,0:T(8,128)(2,1)S(1)} %get-tuple-element.115.refs_11_), channel_id=1, source_target_pairs={{0,14},{1,15},{2,0},{3,1},{4,2},{5,3},{6,4},{7,5},{8,6},{9,7},{10,... | collective-permute-start | bytes 1572872 | tf_op jit(solution)/shard_map/ppermute | solution.py:42
  72.3 14.1 %collective-permute-start.21 = (bf16[128,2048]{1,0:T(8,128)(2,1)S(1)}, bf16[128,2048]{1,0:T(8,128)(2,1)S(1)}, u32[]{:S(2)}, u32[]{:S(2)}) collective-permute-start(bf16[128,2048]{1,0:T(8,128)(2,1)S(1)} %get-tuple-element.113.refs_10_), channel_id=1, source_target_pairs={{0,16},{1,17},{2,18},{3,19},{4,20},{5,21},{6,22},{7,23},{8,24},{9,... | collective-permute-start | bytes 1572872 | tf_op jit(solution)/shard_map/ppermute | solution.py:42
  73.7 12.8 %collective-permute-start.23 = (bf16[128,2048]{1,0:T(8,128)(2,1)S(1)}, bf16[128,2048]{1,0:T(8,128)(2,1)S(1)}, u32[]{:S(2)}, u32[]{:S(2)}) collective-permute-start(bf16[128,2048]{1,0:T(8,128)(2,1)S(1)} %get-tuple-element.126.refs_1_.b_ref.refs_21_), channel_id=1, source_target_pairs={{0,1},{1,0},{2,3},{3,2},{4,5},{5,4},{6,7},{7,6},{8,9},{9,8},{10,11... | collective-permute-start | bytes 1572872 | tf_op jit(solution)/shard_map/ppermute | solution.py:42
  102.0 3.1 %collective-permute-start.24 = (bf16[272,2048]{1,0:T(8,128)(2,1)S(1)}, bf16[272,2048]{1,0:T(8,128)(2,1)S(1)}, u32[]{:S(2)}, u32[]{:S(2)}) collective-permute-start(bf16[272,2048]{1,0:T(8,128)(2,1)S(1)} %get-tuple-element.144), channel_id=1, source_target_pairs={{0,1},{1,0},{2,3},{3,2},{4,5},{5,4},{6,7},{7,6},{8,9},{9,8},{10,11... | collective-permute-start | bytes 3342344 | tf_op jit(solution)/shard_map/ppermute | solution.py:42
  102.3 16.1 %collective-permute-start.30 = (bf16[256,2048]{1,0:T(8,128)(2,1)S(1)}, bf16[256,2048]{1,0:T(8,128)(2,1)S(1)}, u32[]{:S(2)}, u32[]{:S(2)}) collective-permute-start(bf16[256,2048]{1,0:T(8,128)(2,1)S(1)} %get-tuple-element.149), channel_id=1, source_target_pairs={{0,1},{1,0},{2,3},{3,2},{4,5},{5,4},{6,7},{7,6},{8,9},{9,8},{10,11... | collective-permute-start | bytes 3145736 | tf_op jit(solution)/shard_map/ppermute | solution.py:42
  105.3 13.0 %collective-permute-start.25 = (bf16[64,2048]{1,0:T(8,128)(2,1)S(1)}, bf16[64,2048]{1,0:T(8,128)(2,1)S(1)}, u32[]{:S(2)}, u32[]{:S(2)}) collective-permute-start(bf16[64,2048]{1,0:T(8,128)(2,1)S(1)} %get-tuple-element.145), channel_id=1, source_target_pairs={{0,32},{32,0},{64,96},{96,64},{128,160},{160,128},{192,224},{224,1... | collective-permute-start | bytes 786440 | tf_op jit(solution)/shard_map/ppermute | solution.py:50
  107.4 12.4 %collective-permute-start.26 = (bf16[64,2048]{1,0:T(8,128)(2,1)S(1)}, bf16[64,2048]{1,0:T(8,128)(2,1)S(1)}, u32[]{:S(2)}, u32[]{:S(2)}) collective-permute-start(bf16[64,2048]{1,0:T(8,128)(2,1)S(1)} %get-tuple-element.146), channel_id=1, source_target_pairs={{0,64},{32,96},{64,0},{96,32},{128,192},{160,224},{192,128},{224,1... | collective-permute-start | bytes 786440 | tf_op jit(solution)/shard_map/ppermute | solution.py:50
  107.7 14.6 %collective-permute-start.27 = (bf16[64,2048]{1,0:T(8,128)(2,1)S(1)}, bf16[64,2048]{1,0:T(8,128)(2,1)S(1)}, u32[]{:S(2)}, u32[]{:S(2)}) collective-permute-start(bf16[64,2048]{1,0:T(8,128)(2,1)S(1)} %get-tuple-element.147), channel_id=1, source_target_pairs={{0,96},{32,64},{64,32},{96,0},{128,224},{160,192},{192,160},{224,1... | collective-permute-start | bytes 786440 | tf_op jit(solution)/shard_map/ppermute | solution.py:50
  110.2 3.7 %collective-permute-start.28 = (f32[1,2048]{1,0:T(1,128)S(1)}, f32[1,2048]{1,0:T(1,128)S(1)}, u32[]{:S(2)}, u32[]{:S(2)}) collective-permute-start(f32[1,2048]{1,0:T(1,128)S(1)} %get-tuple-element.148.a_ref), channel_id=1, source_target_pairs={{0,2},{1,3},{2,0},{3,1},{4,6},{5,7},{6,4},{7,5},{8,10},{9,11},{10,... | collective-permute-start | bytes 24584 | tf_op jit(solution)/shard_map/ppermute | solution.py:42
  113.8 4.5 %collective-permute-start.29 = (f32[1,2048]{1,0:T(1,128)S(1)}, f32[1,2048]{1,0:T(1,128)S(1)}, u32[]{:S(2)}, u32[]{:S(2)}) collective-permute-start(f32[1,2048]{1,0:T(1,128)S(1)} %add.6.a_ref), channel_id=1, source_target_pairs={{0,4},{1,5},{2,6},{3,7},{4,0},{5,1},{6,2},{7,3},{8,12},{9,13},{10,... | collective-permute-start | bytes 24584 | tf_op jit(solution)/shard_map/ppermute | solution.py:42
  122.5 9.0 %collective-permute-start.31 = (bf16[64,2048]{1,0:T(8,128)(2,1)S(1)}, bf16[64,2048]{1,0:T(8,128)(2,1)S(1)}, u32[]{:S(2)}, u32[]{:S(2)}) collective-permute-start(bf16[64,2048]{1,0:T(8,128)(2,1)S(1)} %get-tuple-element.159), channel_id=1, source_target_pairs={{0,128},{32,160},{64,192},{96,224},{128,0},{160,32},{192,64},{224,... | collective-permute-start | bytes 786440 | tf_op jit(solution)/shard_map/ppermute | solution.py:50
  123.4 4.9 %collective-permute-start.34 = (f32[1,2048]{1,0:T(1,128)S(1)}, f32[1,2048]{1,0:T(1,128)S(1)}, u32[]{:S(2)}, u32[]{:S(2)}) collective-permute-start(f32[1,2048]{1,0:T(1,128)S(1)} %get-tuple-element.160.a_ref), channel_id=1, source_target_pairs={{0,96},{32,64},{64,32},{96,0},{128,224},{160,192},{192,160},{224,1... | collective-permute-start | bytes 24584 | tf_op jit(solution)/shard_map/ppermute | solution.py:50
  126.4 5.2 %collective-permute-start.33 = (f32[1,2048]{1,0:T(1,128)S(1)}, f32[1,2048]{1,0:T(1,128)S(1)}, u32[]{:S(2)}, u32[]{:S(2)}) collective-permute-start(f32[1,2048]{1,0:T(1,128)S(1)} %get-tuple-element.160.a_ref), channel_id=1, source_target_pairs={{0,64},{32,96},{64,0},{96,32},{128,192},{160,224},{192,128},{224,1... | collective-permute-start | bytes 24584 | tf_op jit(solution)/shard_map/ppermute | solution.py:50
  126.4 5.2 %collective-permute-start.32 = (f32[1,2048]{1,0:T(1,128)S(1)}, f32[1,2048]{1,0:T(1,128)S(1)}, u32[]{:S(2)}, u32[]{:S(2)}) collective-permute-start(f32[1,2048]{1,0:T(1,128)S(1)} %get-tuple-element.160.a_ref), channel_id=1, source_target_pairs={{0,32},{32,0},{64,96},{96,64},{128,160},{160,128},{192,224},{224,1... | collective-permute-start | bytes 24584 | tf_op jit(solution)/shard_map/ppermute | solution.py:50
  131.6 21.2 %collective-permute-start.37 = (bf16[64,2048]{1,0:T(8,128)(2,1)S(1)}, bf16[64,2048]{1,0:T(8,128)(2,1)S(1)}, u32[]{:S(2)}, u32[]{:S(2)}) collective-permute-start(bf16[64,2048]{1,0:T(8,128)(2,1)S(1)} %get-tuple-element.161.refs_0_), channel_id=1, source_target_pairs={{0,96},{32,64},{64,32},{96,0},{128,224},{160,192},{192,160},{224,1... | collective-permute-start | bytes 786440 | tf_op jit(solution)/shard_map/ppermute | solution.py:50
  134.1 18.6 %collective-permute-start.36 = (bf16[64,2048]{1,0:T(8,128)(2,1)S(1)}, bf16[64,2048]{1,0:T(8,128)(2,1)S(1)}, u32[]{:S(2)}, u32[]{:S(2)}) collective-permute-start(bf16[64,2048]{1,0:T(8,128)(2,1)S(1)} %get-tuple-element.161.refs_0_), channel_id=1, source_target_pairs={{0,64},{32,96},{64,0},{96,32},{128,192},{160,224},{192,128},{224,1... | collective-permute-start | bytes 786440 | tf_op jit(solution)/shard_map/ppermute | solution.py:50
  134.1 18.6 %collective-permute-start.35 = (bf16[64,2048]{1,0:T(8,128)(2,1)S(1)}, bf16[64,2048]{1,0:T(8,128)(2,1)S(1)}, u32[]{:S(2)}, u32[]{:S(2)}) collective-permute-start(bf16[64,2048]{1,0:T(8,128)(2,1)S(1)} %get-tuple-element.161.refs_0_), channel_id=1, source_target_pairs={{0,32},{32,0},{64,96},{96,64},{128,160},{160,128},{192,224},{224,1... | collective-permute-start | bytes 786440 | tf_op jit(solution)/shard_map/ppermute | solution.py:50
  135.8 7.6 %collective-permute-start.38 = (f32[1,2048]{1,0:T(1,128)S(1)}, f32[1,2048]{1,0:T(1,128)S(1)}, u32[]{:S(2)}, u32[]{:S(2)}) collective-permute-start(f32[1,2048]{1,0:T(1,128)S(1)} %get-tuple-element.162.a_ref), channel_id=1, source_target_pairs={{0,8},{1,9},{2,10},{3,11},{4,12},{5,13},{6,14},{7,15},{8,0},{9,1},... | collective-permute-start | bytes 24584 | tf_op jit(solution)/shard_map/ppermute | solution.py:42
  143.4 3.7 %collective-permute-start.39 = (f32[1,2048]{1,0:T(1,128)S(1)}, f32[1,2048]{1,0:T(1,128)S(1)}, u32[]{:S(2)}, u32[]{:S(2)}) collective-permute-start(f32[1,2048]{1,0:T(1,128)S(1)} %add.9.a_ref), channel_id=1, source_target_pairs={{0,16},{1,17},{2,18},{3,19},{4,20},{5,21},{6,22},{7,23},{8,24},{9,... | collective-permute-start | bytes 24584 | tf_op jit(solution)/shard_map/ppermute | solution.py:42
  147.0 5.2 %collective-permute-start.40 = (f32[1,2048]{1,0:T(1,128)S(1)}, f32[1,2048]{1,0:T(1,128)S(1)}, u32[]{:S(2)}, u32[]{:S(2)}) collective-permute-start(f32[1,2048]{1,0:T(1,128)S(1)} %add.10.a_ref), channel_id=1, source_target_pairs={{0,128},{32,160},{64,192},{96,224},{128,0},{160,32},{192,64},{224,... | collective-permute-start | bytes 24584 | tf_op jit(solution)/shard_map/ppermute | solution.py:50

commit v2 on v1

--- a/solution.py
+++ b/solution.py
@@ -182,6 +182,11 @@
     rows = out_ref.shape[0] // len(parts)
     for index, part in enumerate(parts):
         out_ref[index * rows:(index + 1) * rows, :] = part[...]
+
+
+def late_kernel(a_ref, token_ref, out_ref):
+    del token_ref
+    out_ref[...] = a_ref[...]
 
 
 def add_kernel(a_ref, b_ref, out_ref):
@@ -504,7 +509,8 @@
     up = from_above(b[2])
     b[-3] = order.take(across_3)
     own_b = order.take(hidden)
-    oth_a, oth_b = other_core(own_a), other_core(own_b)
+    late_a = small_call(late_kernel, bf16_rows(PIECE), (own_a, order.token), "late", limit=3)
+    oth_a, oth_b = other_core(late_a), other_core(own_b)
     b[3] = order.take(up)
     b[-1] = order.take(down)
     b[4] = order.take(across_4)
@@ -531,6 +537,9 @@
             part = small_call(add_kernel, LINE, (part, move(part)), "add", limit=1)
         return part
 
+    def butterfly(part, *moves):
+        return small_call(butterfly_kernel, LINE, (part, *[move(part) for move in moves]), "add", limit=1)
+
     def z_move(bits):
         return lambda v: dp_swap(v, lambda c, z, k: (c, z ^ bits, k))
 
@@ -538,18 +547,19 @@
         split_kernel, [ROWS32, LINE, quarter, quarter, quarter], (dh_own, gp, other_core(dh_oth)), "split"
     )
     far, near, other = other_y(parts[1], 2), other_y(parts[0], 1), other_y(parts[2], 3)
-    gain_part = add_from(gain_part, z_move(1), z_move(2))
-    near, far, other, gain_part, got_out = order.take(near, far, other, gain_part, other_core(oth_out))
+    gain_part, got_out = order.take(gain_part, other_core(oth_out))
+    gain_part = butterfly(gain_part, *[z_move(bits) for bits in (1, 2, 3)])
+    gain_part = add_from(gain_part, z_move(4))
+    near, far, other, gain_part = order.take(near, far, other, gain_part)
     kept, sent, gain_part = small_call(
         sum_kernel, [ROWS32, quarter, LINE], (kept, gain_part, near, far, other), "sum"
     )
     crossed = other_high(sent)
-    gain_part = small_call(
-        butterfly_kernel, LINE, (gain_part, *[other_y(gain_part, bits) for bits in (1, 2, 3)]), "add", limit=1
-    )
+    gain_part = butterfly(gain_part, *[lambda v, bits=bits: other_y(v, bits) for bits in (1, 2, 3)])
     dh, gain_part = small_call(last_kernel, [quarter, LINE], (kept, crossed, gain_part), "last")
     far, near, other = other_y(dh, 2), other_y(dh, 1), other_y(dh, 3)
-    gain_part = add_from(gain_part, z_move(4), other_column, other_high)
+    gain_part = add_from(gain_part, other_column)
+    gain_part = add_from(gain_part, other_high)
     dhs = [dh, near, far, other]
     section_out = put_out(0, section_map, own_out, got_out, [enc_out], "rows")
     section_grad = put_out(F, section_map, own_out, got_out, dhs, "grads")

time: 156 us -> 150 us (0.962)
  waiting for transfers between devices: 78.4 us -> 71.8 us
    ppermute x25 -> x26, waiting for transfers between devices: 48.7 us -> 44.8 us  [dp_swap(): return lax.ppermute(x, 'dp', pairs)]
    ppermute x16, waiting for transfers between devices: 29.7 us -> 27 us  [section_swap(): return lax.ppermute(x, 'section', pairs)]
    ppermute x25 -> x26, starting transfers between devices: 25.5 us -> 26.7 us  [dp_swap(): return lax.ppermute(x, 'dp', pairs)]
  transfers between devices with their start and end apart: 41 -> 42, of which waited for: 20 -> 20; matrix products, arithmetic and copies ran while one was open for 0% -> 0% of each run, Pallas kernels for 4% -> 4%
where the time goes in v2:
time: 150 us; the launch traced here: 149 us
  waiting for transfers between devices  71.8 us (48%)
  starting transfers between devices  50.3 us (34%)
  Pallas kernels  23.2 us (15%)
  local copies, waits for them, and re-layouts  2.27 us (2%)
    ppermute x26, waiting for transfers between devices, dp_swap(): return lax.ppermute(x, 'dp', pairs)  44.8 us
    ppermute x16, waiting for transfers between devices, section_swap(): return lax.ppermute(x, 'section', pairs)  27 us
    ppermute x26, starting transfers between devices, dp_swap(): return lax.ppermute(x, 'dp', pairs)  26.7 us
    ppermute x16, starting transfers between devices, section_swap(): return lax.ppermute(x, 'section', pairs)  23.6 us
    pallas_call x1, Pallas kernels, attend(): pl.pallas_call(main_kernel, in_specs=[VMEM] * (N_SLOT + 12) + [SMEM] + [V...  14.8 us
    pallas_call x16, Pallas kernels, small_call(): pl.pallas_call(kernel, in_specs=[SMEM] * len(first) + [VMEM] * len(args),...  4.99 us
    pallas_call x2, Pallas kernels, put_out(): pl.pallas_call(functools.partial(out_kernel, offset), in_specs=[SMEM] + [...  3.12 us
  transfers between devices with their start and end apart: 42, of which 20 were waited for; matrix products, arithmetic and copies ran while one was open for 0% of the time, Pallas kernels for 4%

profile of v2, /device:TPU:6, one launch (start us, length us, event | category | flops | bytes accessed | tf_op | source)
XLA Modules:
  0.0 148.7 jit_solution(12382471458852649459)
XLA Ops:
  0.6 1.0 copy-done.3
  1.9 1.2 copy-done
  3.2 3.3 %collective-permute-start.2 = (bf16[128,2048]{1,0:T(8,128)(2,1)S(1)}, bf16[128,2048]{1,0:T(8,128)(2,1)S(1)}, u32[]{:S(2)}, u32[]{:S(2)}) collective-permute-start(bf16[128,2048]{1,0:T(8,128)(2,1)S(1)} %half.1), channel_id=1, source_target_pairs={{0,64},{32,96},{64,0},{96,32},{128,192},{160,224},{192,128},{224,1... | collective-permute-start | bytes 1572872 | tf_op jit(solution)/shard_map/ppermute | solution.py:50
  6.7 0.3 collective-permute-start.5
  7.0 5.9 %collective-permute-start.1 = (bf16[128,2048]{1,0:T(8,128)(2,1)S(1)}, bf16[128,2048]{1,0:T(8,128)(2,1)S(1)}, u32[]{:S(2)}, u32[]{:S(2)}) collective-permute-start(bf16[128,2048]{1,0:T(8,128)(2,1)S(1)} %unit.1.token_ref.refs_0_), channel_id=1, source_target_pairs={{0,14},{1,15},{2,0},{3,1},{4,2},{5,3},{6,4},{7,5},{8,6},{9,7},{10,... | collective-permute-start | bytes 1572872 | tf_op jit(solution)/shard_map/ppermute | solution.py:42
  12.9 0.8 collective-permute-start.4
  13.7 5.4 %collective-permute-done.2.refs_0_ = bf16[128,2048]{1,0:T(8,128)(2,1)S(1)} collective-permute-done((bf16[128,2048]{1,0:T(8,128)(2,1)S(1)}, bf16[128,2048]{1,0:T(8,128)(2,1)S(1)}, u32[]{:S(2)}, u32[]{:S(2)}) %collective-permute-start.2) | collective-permute-done | bytes 524320 | tf_op jit(solution)/shard_map/ppermute | solution.py:50
  19.1 5.4 %collective-permute-done.1.refs_0_ = bf16[128,2048]{1,0:T(8,128)(2,1)S(1)} collective-permute-done((bf16[128,2048]{1,0:T(8,128)(2,1)S(1)}, bf16[128,2048]{1,0:T(8,128)(2,1)S(1)}, u32[]{:S(2)}, u32[]{:S(2)}) %collective-permute-start.1) | collective-permute-done | bytes 524320 | tf_op jit(solution)/shard_map/ppermute | solution.py:42
  24.5 3.7 %collective-permute-start.6 = (bf16[128,2048]{1,0:T(8,128)(2,1)S(1)}, bf16[128,2048]{1,0:T(8,128)(2,1)S(1)}, u32[]{:S(2)}, u32[]{:S(2)}) collective-permute-start(bf16[128,2048]{1,0:T(8,128)(2,1)S(1)} %get-tuple-element.89.refs_1_), channel_id=1, source_target_pairs={{0,14},{1,15},{2,0},{3,1},{4,2},{5,3},{6,4},{7,5},{8,6},{9,7},{10,... | collective-permute-start | bytes 1572872 | tf_op jit(solution)/shard_map/ppermute | solution.py:42
  28.2 0.6 select.3
  28.8 0.8 collective-permute-start.7
  29.6 0.8 collective-permute-start.9
  30.4 5.9 %collective-permute-done.7.refs_0_ = bf16[64,2048]{1,0:T(8,128)(2,1)S(1)} collective-permute-done((bf16[64,2048]{1,0:T(8,128)(2,1)S(1)}, bf16[64,2048]{1,0:T(8,128)(2,1)S(1)}, u32[]{:S(2)}, u32[]{:S(2)}) %collective-permute-start.7) | collective-permute-done | bytes 262176 | tf_op jit(solution)/shard_map/ppermute | solution.py:50
  36.3 2.7 %collective-permute-done.6.refs_0_ = bf16[128,2048]{1,0:T(8,128)(2,1)S(1)} collective-permute-done((bf16[128,2048]{1,0:T(8,128)(2,1)S(1)}, bf16[128,2048]{1,0:T(8,128)(2,1)S(1)}, u32[]{:S(2)}, u32[]{:S(2)}) %collective-permute-start.6) | collective-permute-done | bytes 524320 | tf_op jit(solution)/shard_map/ppermute | solution.py:42
  39.0 3.7 %collective-permute-start.10 = (bf16[128,2048]{1,0:T(8,128)(2,1)S(1)}, bf16[128,2048]{1,0:T(8,128)(2,1)S(1)}, u32[]{:S(2)}, u32[]{:S(2)}) collective-permute-start(bf16[128,2048]{1,0:T(8,128)(2,1)S(1)} %get-tuple-element.98.refs_4_), channel_id=1, source_target_pairs={{0,14},{1,15},{2,0},{3,1},{4,2},{5,3},{6,4},{7,5},{8,6},{9,7},{10,... | collective-permute-start | bytes 1572872 | tf_op jit(solution)/shard_map/ppermute | solution.py:42
  42.7 0.6 select.4.own_ref
  43.3 1.5 %collective-permute-start.11 = (bf16[64,2048]{1,0:T(8,128)(2,1)S(1)}, bf16[64,2048]{1,0:T(8,128)(2,1)S(1)}, u32[]{:S(2)}, u32[]{:S(2)}) collective-permute-start(bf16[64,2048]{1,0:T(8,128)(2,1)S(1)} %select.4.own_ref), channel_id=1, source_target_pairs={{0,128},{32,160},{64,192},{96,224},{128,0},{160,32},{192,64},{224,... | collective-permute-start | bytes 786440 | tf_op jit(solution)/shard_map/ppermute | solution.py:50
  44.8 9.3 %collective-permute-done.11.refs_0_ = bf16[64,2048]{1,0:T(8,128)(2,1)S(1)} collective-permute-done((bf16[64,2048]{1,0:T(8,128)(2,1)S(1)}, bf16[64,2048]{1,0:T(8,128)(2,1)S(1)}, u32[]{:S(2)}, u32[]{:S(2)}) %collective-permute-start.11) | collective-permute-done | bytes 262176 | tf_op jit(solution)/shard_map/ppermute | solution.py:50
  54.1 0.6 select.5.refs_0_
  54.7 0.8 collective-permute-start.15
  55.5 0.5 collective-permute-done.12.refs_0_
  56.0 3.2 %collective-permute-start.16 = (bf16[128,2048]{1,0:T(8,128)(2,1)S(1)}, bf16[128,2048]{1,0:T(8,128)(2,1)S(1)}, u32[]{:S(2)}, u32[]{:S(2)}) collective-permute-start(bf16[128,2048]{1,0:T(8,128)(2,1)S(1)} %get-tuple-element.102.refs_6_), channel_id=1, source_target_pairs={{0,14},{1,15},{2,0},{3,1},{4,2},{5,3},{6,4},{7,5},{8,6},{9,7},{10,... | collective-permute-start | bytes 1572872 | tf_op jit(solution)/shard_map/ppermute | solution.py:42
  59.2 0.8 collective-permute-start.17
  60.0 2.7 %collective-permute-done.13.refs_0_ = bf16[128,2048]{1,0:T(8,128)(2,1)S(1)} collective-permute-done((bf16[128,2048]{1,0:T(8,128)(2,1)S(1)}, bf16[128,2048]{1,0:T(8,128)(2,1)S(1)}, u32[]{:S(2)}, u32[]{:S(2)}) %collective-permute-start.13) | collective-permute-done | bytes 524320 | tf_op jit(solution)/shard_map/ppermute | solution.py:42
  62.8 1.3 collective-permute-start.19
  64.1 7.9 %collective-permute-done.14.refs_0_ = bf16[128,2048]{1,0:T(8,128)(2,1)S(1)} collective-permute-done((bf16[128,2048]{1,0:T(8,128)(2,1)S(1)}, bf16[128,2048]{1,0:T(8,128)(2,1)S(1)}, u32[]{:S(2)}, u32[]{:S(2)}) %collective-permute-start.14) | collective-permute-done | bytes 524320 | tf_op jit(solution)/shard_map/ppermute | solution.py:42
  72.0 0.3 collective-permute-start.18
  72.3 0.7 collective-permute-start.21
  73.0 1.0 collective-permute-done.17.refs_0_
  74.1 0.5 collective-permute-start.23
  74.6 0.7 norm.2
  75.4 0.6 encoder.1
  75.9 5.4 %collective-permute-done.18.refs_0_ = bf16[128,2048]{1,0:T(8,128)(2,1)S(1)} collective-permute-done((bf16[128,2048]{1,0:T(8,128)(2,1)S(1)}, bf16[128,2048]{1,0:T(8,128)(2,1)S(1)}, u32[]{:S(2)}, u32[]{:S(2)}) %collective-permute-start.18) | collective-permute-done | bytes 524320 | tf_op jit(solution)/shard_map/ppermute | solution.py:42
  81.3 1.5 %collective-permute-done.21.refs_0_ = bf16[128,2048]{1,0:T(8,128)(2,1)S(1)} collective-permute-done((bf16[128,2048]{1,0:T(8,128)(2,1)S(1)}, bf16[128,2048]{1,0:T(8,128)(2,1)S(1)}, u32[]{:S(2)}, u32[]{:S(2)}) %collective-permute-start.21) | collective-permute-done | bytes 524320 | tf_op jit(solution)/shard_map/ppermute | solution.py:42
  82.8 0.7 norm.3
  83.6 14.8 %attend.1 = (bf16[256,2048]{1,0:T(8,128)(2,1)S(1)}, bf16[256,2048]{1,0:T(8,128)(2,1)S(1)}, bf16[256,2048]{1,0:T(8,128)(2,1)S(1)}, bf16[272,2048]{1,0:T(8,128)(2,1)S(1)}, f32[1,2048]{1,0:T(1,128)S(1)}) custom-call(bf16[128,2048]{1,0:T(8,128)(2,1)S(1)} %unit.1.token_ref.refs_0_, bf16[128,2048]{1,0:T(8,128)(2,1)S(1)} %get-tuple-element.89.refs_1_, ...), custom_call_target="tpu_custom_call" | custom-call | flops 10000000000 | bytes 20000000 | tf_op jit(solution)/shard_map/attend/pallas_call | solution.py:333
  98.3 0.3 collective-permute-start.24
  98.6 0.5 collective-permute-start.25
  99.1 2.2 %collective-permute-done.24.got_ref = bf16[272,2048]{1,0:T(8,128)(2,1)S(1)} collective-permute-done((bf16[272,2048]{1,0:T(8,128)(2,1)S(1)}, bf16[272,2048]{1,0:T(8,128)(2,1)S(1)}, u32[]{:S(2)}, u32[]{:S(2)}) %collective-permute-start.24) | collective-permute-done | bytes 1114144 | tf_op jit(solution)/shard_map/ppermute | solution.py:42
  101.4 0.3 split.1
  101.7 0.9 collective-permute-start.26
  102.6 1.5 %collective-permute-start.27 = (bf16[64,2048]{1,0:T(8,128)(2,1)S(1)}, bf16[64,2048]{1,0:T(8,128)(2,1)S(1)}, u32[]{:S(2)}, u32[]{:S(2)}) collective-permute-start(bf16[64,2048]{1,0:T(8,128)(2,1)S(1)} %get-tuple-element.154), channel_id=1, source_target_pairs={{0,64},{32,96},{64,0},{96,32},{128,192},{160,224},{192,128},{224,1... | collective-permute-start | bytes 786440 | tf_op jit(solution)/shard_map/ppermute | solution.py:50
  104.1 2.4 %collective-permute-start.28 = (bf16[64,2048]{1,0:T(8,128)(2,1)S(1)}, bf16[64,2048]{1,0:T(8,128)(2,1)S(1)}, u32[]{:S(2)}, u32[]{:S(2)}) collective-permute-start(bf16[64,2048]{1,0:T(8,128)(2,1)S(1)} %get-tuple-element.155), channel_id=1, source_target_pairs={{0,96},{32,64},{64,32},{96,0},{128,224},{160,192},{192,160},{224,1... | collective-permute-start | bytes 786440 | tf_op jit(solution)/shard_map/ppermute | solution.py:50
  106.5 2.3 %collective-permute-start.31 = (f32[1,2048]{1,0:T(1,128)S(1)}, f32[1,2048]{1,0:T(1,128)S(1)}, u32[]{:S(2)}, u32[]{:S(2)}) collective-permute-start(f32[1,2048]{1,0:T(1,128)S(1)} %get-tuple-element.156.a_ref), channel_id=1, source_target_pairs={{0,6},{1,7},{2,4},{3,5},{4,2},{5,3},{6,0},{7,1},{8,14},{9,15},{10,... | collective-permute-start | bytes 24584 | tf_op jit(solution)/shard_map/ppermute | solution.py:42
  108.8 3.1 %collective-permute-done.31.d_ref = f32[1,2048]{1,0:T(1,128)S(1)} collective-permute-done((f32[1,2048]{1,0:T(1,128)S(1)}, f32[1,2048]{1,0:T(1,128)S(1)}, u32[]{:S(2)}, u32[]{:S(2)}) %collective-permute-start.31) | collective-permute-done | bytes 8224 | tf_op jit(solution)/shard_map/ppermute | solution.py:42
  111.9 1.4 collective-permute-done.30.c_ref
  113.4 2.2 %collective-permute-done.29.b_ref = f32[1,2048]{1,0:T(1,128)S(1)} collective-permute-done((f32[1,2048]{1,0:T(1,128)S(1)}, f32[1,2048]{1,0:T(1,128)S(1)}, u32[]{:S(2)}, u32[]{:S(2)}) %collective-permute-start.29) | collective-permute-done | bytes 8224 | tf_op jit(solution)/shard_map/ppermute | solution.py:42
  115.6 2.4 %collective-permute-start.32 = (f32[1,2048]{1,0:T(1,128)S(1)}, f32[1,2048]{1,0:T(1,128)S(1)}, u32[]{:S(2)}, u32[]{:S(2)}) collective-permute-start(f32[1,2048]{1,0:T(1,128)S(1)} %add.5.a_ref), channel_id=1, source_target_pairs={{0,8},{1,9},{2,10},{3,11},{4,12},{5,13},{6,14},{7,15},{8,0},{9,1},... | collective-permute-start | bytes 24584 | tf_op jit(solution)/shard_map/ppermute | solution.py:42
  118.0 5.2 %collective-permute-done.32.b_ref = f32[1,2048]{1,0:T(1,128)S(1)} collective-permute-done((f32[1,2048]{1,0:T(1,128)S(1)}, f32[1,2048]{1,0:T(1,128)S(1)}, u32[]{:S(2)}, u32[]{:S(2)}) %collective-permute-start.32) | collective-permute-done | bytes 8224 | tf_op jit(solution)/shard_map/ppermute | solution.py:42
  123.3 2.5 %collective-permute-start.33 = (bf16[64,2048]{1,0:T(8,128)(2,1)S(1)}, bf16[64,2048]{1,0:T(8,128)(2,1)S(1)}, u32[]{:S(2)}, u32[]{:S(2)}) collective-permute-start(bf16[64,2048]{1,0:T(8,128)(2,1)S(1)} %get-tuple-element.163), channel_id=1, source_target_pairs={{0,128},{32,160},{64,192},{96,224},{128,0},{160,32},{192,64},{224,... | collective-permute-start | bytes 786440 | tf_op jit(solution)/shard_map/ppermute | solution.py:50
  125.8 2.1 %collective-permute-start.36 = (f32[1,2048]{1,0:T(1,128)S(1)}, f32[1,2048]{1,0:T(1,128)S(1)}, u32[]{:S(2)}, u32[]{:S(2)}) collective-permute-start(f32[1,2048]{1,0:T(1,128)S(1)} %get-tuple-element.164.a_ref), channel_id=1, source_target_pairs={{0,96},{32,64},{64,32},{96,0},{128,224},{160,192},{192,160},{224,1... | collective-permute-start | bytes 24584 | tf_op jit(solution)/shard_map/ppermute | solution.py:50
  127.9 0.7 collective-permute-start.35
  128.6 1.3 collective-permute-start.34
  129.9 0.8 collective-permute-done.36.d_ref
  130.7 2.6 %collective-permute-done.35.c_ref = f32[1,2048]{1,0:T(1,128)S(1)} collective-permute-done((f32[1,2048]{1,0:T(1,128)S(1)}, f32[1,2048]{1,0:T(1,128)S(1)}, u32[]{:S(2)}, u32[]{:S(2)}) %collective-permute-start.35) | collective-permute-done | bytes 8224 | tf_op jit(solution)/shard_map/ppermute | solution.py:50
  133.3 1.2 collective-permute-start.39
  134.5 1.3 collective-permute-start.38
  135.8 1.7 %collective-permute-start.37 = (bf16[64,2048]{1,0:T(8,128)(2,1)S(1)}, bf16[64,2048]{1,0:T(8,128)(2,1)S(1)}, u32[]{:S(2)}, u32[]{:S(2)}) collective-permute-start(bf16[64,2048]{1,0:T(8,128)(2,1)S(1)} %get-tuple-element.165.refs_0_), channel_id=1, source_target_pairs={{0,32},{32,0},{64,96},{96,64},{128,160},{160,128},{192,224},{224,1... | collective-permute-start | bytes 786440 | tf_op jit(solution)/shard_map/ppermute | solution.py:50
  137.6 3.5 %collective-permute-done.40.b_ref = f32[1,2048]{1,0:T(1,128)S(1)} collective-permute-done((f32[1,2048]{1,0:T(1,128)S(1)}, f32[1,2048]{1,0:T(1,128)S(1)}, u32[]{:S(2)}, u32[]{:S(2)}) %collective-permute-start.40) | collective-permute-done | bytes 8224 | tf_op jit(solution)/shard_map/ppermute | solution.py:42
  141.1 0.5 collective-permute-start.41
  141.7 1.6 %rows.1 = bf16[256,2048]{1,0:T(8,128)(2,1)} custom-call(s32[8]{0:T(128)S(1)} %copy-done.5, bf16[256,2048]{1,0:T(8,128)(2,1)S(1)} %get-tuple-element.143.own_ref, bf16[256,2048]{1,0:T(8,128)(2,1)S(1)} %get-tuple-element.150.oth_ref, bf16[256,2048]{1,0:T(8,128)(2,1)S(1)} %get-tuple-element.151.refs_0_), custom_call_target="tpu_custom_call" | custom-call | bytes 2000000 | tf_op jit(solution)/shard_map/rows/pallas_call | solution.py:442
  143.2 3.1 %collective-permute-done.41.b_ref = f32[1,2048]{1,0:T(1,128)S(1)} collective-permute-done((f32[1,2048]{1,0:T(1,128)S(1)}, f32[1,2048]{1,0:T(1,128)S(1)}, u32[]{:S(2)}, u32[]{:S(2)}) %collective-permute-start.41) | collective-permute-done | bytes 8224 | tf_op jit(solution)/shard_map/ppermute | solution.py:50
  146.3 0.6 add.9
  146.9 1.6 %grads.1 = bf16[256,2048]{1,0:T(8,128)(2,1)} custom-call(s32[8]{0:T(128)S(1)} %copy-done.5, bf16[256,2048]{1,0:T(8,128)(2,1)S(1)} %get-tuple-element.143.own_ref, bf16[256,2048]{1,0:T(8,128)(2,1)S(1)} %get-tuple-element.150.oth_ref, bf16[64,2048]{1,0:T(8,128)(2,1)S(1)} %get-tuple-element.165.refs_0_, bf16[64,2048]{1,0:T(8,128)(2,1)S(1)} %collective-permute-done.37.refs_1_, ...), custom_call_target="tpu_custom_call" | custom-call | bytes 2000000 | tf_op jit(solution)/shard_map/grads/pallas_call | solution.py:442
  (78 shorter events, 1.0 us)
Async XLA Ops:
  0.6 1.0 copy-start.3
  1.8 4.7 %collective-permute-start = (bf16[64,2048]{1,0:T(8,128)(2,1)S(1)}, bf16[64,2048]{1,0:T(8,128)(2,1)S(1)}, u32[]{:S(2)}, u32[]{:S(2)}) collective-permute-start(bf16[64,2048]{1,0:T(8,128)(2,1)S(1)} %get-tuple-element.86), channel_id=1, source_target_pairs={{0,1},{1,0},{2,3},{3,2},{4,5},{5,4},{6,7},{7,6},{8,9},{9,8},{10,11... | collective-permute-start | bytes 786440 | tf_op jit(solution)/shard_map/ppermute | solution.py:42
  1.9 1.2 copy-start
  3.1 3.4 %copy-start.1 = (bf16[1,256,2048]{2,1,0:T(8,128)(2,1)S(1)}, bf16[1,256,2048]{2,1,0:T(8,128)(2,1)}, u32[]{:S(2)}) copy-start(bf16[1,256,2048]{2,1,0:T(8,128)(2,1)} %param.5) | copy-start | bytes 3145732
  3.1 3.4 %copy-start.2 = (bf16[1,256,2048]{2,1,0:T(8,128)(2,1)S(1)}, bf16[1,256,2048]{2,1,0:T(8,128)(2,1)}, u32[]{:S(2)}) copy-start(bf16[1,256,2048]{2,1,0:T(8,128)(2,1)} %param.7) | copy-start | bytes 3145732
  3.2 15.9 %collective-permute-start.2 = (bf16[128,2048]{1,0:T(8,128)(2,1)S(1)}, bf16[128,2048]{1,0:T(8,128)(2,1)S(1)}, u32[]{:S(2)}, u32[]{:S(2)}) collective-permute-start(bf16[128,2048]{1,0:T(8,128)(2,1)S(1)} %half.1), channel_id=1, source_target_pairs={{0,64},{32,96},{64,0},{96,32},{128,192},{160,224},{192,128},{224,1... | collective-permute-start | bytes 1572872 | tf_op jit(solution)/shard_map/ppermute | solution.py:50
  6.7 21.5 %copy-start.5 = (s32[8]{0:T(128)S(1)}, s32[8]{0:T(128)}, u32[]{:S(2)}) copy-start(s32[8]{0:T(128)} %map_ref.11) | copy-start | bytes 100
  6.7 23.7 %collective-permute-start.5 = (bf16[256,2048]{1,0:T(8,128)(2,1)S(1)}, bf16[256,2048]{1,0:T(8,128)(2,1)S(1)}, u32[]{:S(2)}, u32[]{:S(2)}) collective-permute-start(bf16[256,2048]{1,0:T(8,128)(2,1)S(1)} %give.1), channel_id=1, source_target_pairs={{0,1},{1,0},{2,3},{3,2},{4,5},{5,4},{6,7},{7,6},{8,9},{9,8},{10,11... | collective-permute-start | bytes 3145736 | tf_op jit(solution)/shard_map/ppermute | solution.py:42
  7.0 17.5 %collective-permute-start.1 = (bf16[128,2048]{1,0:T(8,128)(2,1)S(1)}, bf16[128,2048]{1,0:T(8,128)(2,1)S(1)}, u32[]{:S(2)}, u32[]{:S(2)}) collective-permute-start(bf16[128,2048]{1,0:T(8,128)(2,1)S(1)} %unit.1.token_ref.refs_0_), channel_id=1, source_target_pairs={{0,14},{1,15},{2,0},{3,1},{4,2},{5,3},{6,4},{7,5},{8,6},{9,7},{10,... | collective-permute-start | bytes 1572872 | tf_op jit(solution)/shard_map/ppermute | solution.py:42
  12.9 15.3 %collective-permute-start.3 = (bf16[128,2048]{1,0:T(8,128)(2,1)S(1)}, bf16[128,2048]{1,0:T(8,128)(2,1)S(1)}, u32[]{:S(2)}, u32[]{:S(2)}) collective-permute-start(bf16[128,2048]{1,0:T(8,128)(2,1)S(1)} %unit.1.token_ref.refs_0_), channel_id=1, source_target_pairs={{0,2},{1,3},{2,4},{3,5},{4,6},{5,7},{6,8},{7,9},{8,10},{9,11},{10,... | collective-permute-start | bytes 1572872 | tf_op jit(solution)/shard_map/ppermute | solution.py:42
  12.9 16.7 %collective-permute-start.4 = (bf16[128,2048]{1,0:T(8,128)(2,1)S(1)}, bf16[128,2048]{1,0:T(8,128)(2,1)S(1)}, u32[]{:S(2)}, u32[]{:S(2)}) collective-permute-start(bf16[128,2048]{1,0:T(8,128)(2,1)S(1)} %unit.1.token_ref.refs_0_), channel_id=1, source_target_pairs={{0,16},{1,17},{2,18},{3,19},{4,20},{5,21},{6,22},{7,23},{8,24},{9,... | collective-permute-start | bytes 1572872 | tf_op jit(solution)/shard_map/ppermute | solution.py:42
  24.5 14.5 %collective-permute-start.6 = (bf16[128,2048]{1,0:T(8,128)(2,1)S(1)}, bf16[128,2048]{1,0:T(8,128)(2,1)S(1)}, u32[]{:S(2)}, u32[]{:S(2)}) collective-permute-start(bf16[128,2048]{1,0:T(8,128)(2,1)S(1)} %get-tuple-element.89.refs_1_), channel_id=1, source_target_pairs={{0,14},{1,15},{2,0},{3,1},{4,2},{5,3},{6,4},{7,5},{8,6},{9,7},{10,... | collective-permute-start | bytes 1572872 | tf_op jit(solution)/shard_map/ppermute | solution.py:42
  28.2 14.5 %collective-permute-start.8 = (bf16[128,2048]{1,0:T(8,128)(2,1)S(1)}, bf16[128,2048]{1,0:T(8,128)(2,1)S(1)}, u32[]{:S(2)}, u32[]{:S(2)}) collective-permute-start(bf16[128,2048]{1,0:T(8,128)(2,1)S(1)} %get-tuple-element.91.refs_2_), channel_id=1, source_target_pairs={{0,2},{1,3},{2,4},{3,5},{4,6},{5,7},{6,8},{7,9},{8,10},{9,11},{10,... | collective-permute-start | bytes 1572872 | tf_op jit(solution)/shard_map/ppermute | solution.py:42
  28.8 7.5 %collective-permute-start.7 = (bf16[64,2048]{1,0:T(8,128)(2,1)S(1)}, bf16[64,2048]{1,0:T(8,128)(2,1)S(1)}, u32[]{:S(2)}, u32[]{:S(2)}) collective-permute-start(bf16[64,2048]{1,0:T(8,128)(2,1)S(1)} %get-tuple-element.95), channel_id=1, source_target_pairs={{0,32},{32,0},{64,96},{96,64},{128,160},{160,128},{192,224},{224,1... | collective-permute-start | bytes 786440 | tf_op jit(solution)/shard_map/ppermute | solution.py:50
  29.6 15.2 %collective-permute-start.9 = (bf16[128,2048]{1,0:T(8,128)(2,1)S(1)}, bf16[128,2048]{1,0:T(8,128)(2,1)S(1)}, u32[]{:S(2)}, u32[]{:S(2)}) collective-permute-start(bf16[128,2048]{1,0:T(8,128)(2,1)S(1)} %get-tuple-element.89.refs_1_), channel_id=1, source_target_pairs={{0,16},{1,17},{2,18},{3,19},{4,20},{5,21},{6,22},{7,23},{8,24},{9,... | collective-permute-start | bytes 1572872 | tf_op jit(solution)/shard_map/ppermute | solution.py:42
  39.0 16.5 %collective-permute-start.10 = (bf16[128,2048]{1,0:T(8,128)(2,1)S(1)}, bf16[128,2048]{1,0:T(8,128)(2,1)S(1)}, u32[]{:S(2)}, u32[]{:S(2)}) collective-permute-start(bf16[128,2048]{1,0:T(8,128)(2,1)S(1)} %get-tuple-element.98.refs_4_), channel_id=1, source_target_pairs={{0,14},{1,15},{2,0},{3,1},{4,2},{5,3},{6,4},{7,5},{8,6},{9,7},{10,... | collective-permute-start | bytes 1572872 | tf_op jit(solution)/shard_map/ppermute | solution.py:42
  42.7 13.3 %collective-permute-start.12 = (bf16[128,2048]{1,0:T(8,128)(2,1)S(1)}, bf16[128,2048]{1,0:T(8,128)(2,1)S(1)}, u32[]{:S(2)}, u32[]{:S(2)}) collective-permute-start(bf16[128,2048]{1,0:T(8,128)(2,1)S(1)} %get-tuple-element.100.refs_5_), channel_id=1, source_target_pairs={{0,2},{1,3},{2,4},{3,5},{4,6},{5,7},{6,8},{7,9},{8,10},{9,11},{10,... | collective-permute-start | bytes 1572872 | tf_op jit(solution)/shard_map/ppermute | solution.py:42
  43.3 10.8 %collective-permute-start.11 = (bf16[64,2048]{1,0:T(8,128)(2,1)S(1)}, bf16[64,2048]{1,0:T(8,128)(2,1)S(1)}, u32[]{:S(2)}, u32[]{:S(2)}) collective-permute-start(bf16[64,2048]{1,0:T(8,128)(2,1)S(1)} %select.4.own_ref), channel_id=1, source_target_pairs={{0,128},{32,160},{64,192},{96,224},{128,0},{160,32},{192,64},{224,... | collective-permute-start | bytes 786440 | tf_op jit(solution)/shard_map/ppermute | solution.py:50
  44.8 18.0 %collective-permute-start.13 = (bf16[128,2048]{1,0:T(8,128)(2,1)S(1)}, bf16[128,2048]{1,0:T(8,128)(2,1)S(1)}, u32[]{:S(2)}, u32[]{:S(2)}) collective-permute-start(bf16[128,2048]{1,0:T(8,128)(2,1)S(1)} %get-tuple-element.100.refs_5_), channel_id=1, source_target_pairs={{0,16},{1,17},{2,18},{3,19},{4,20},{5,21},{6,22},{7,23},{8,24},{9,... | collective-permute-start | bytes 1572872 | tf_op jit(solution)/shard_map/ppermute | solution.py:42
  54.7 8.1 %collective-permute-start.15 = (bf16[64,2048]{1,0:T(8,128)(2,1)S(1)}, bf16[64,2048]{1,0:T(8,128)(2,1)S(1)}, u32[]{:S(2)}, u32[]{:S(2)}) collective-permute-start(bf16[64,2048]{1,0:T(8,128)(2,1)S(1)} %select.5.refs_0_), channel_id=1, source_target_pairs={{0,32},{32,0},{64,96},{96,64},{128,160},{160,128},{192,224},{224,1... | collective-permute-start | bytes 786440 | tf_op jit(solution)/shard_map/ppermute | solution.py:50
  56.0 16.1 %collective-permute-start.14 = (bf16[128,2048]{1,0:T(8,128)(2,1)S(1)}, bf16[128,2048]{1,0:T(8,128)(2,1)S(1)}, u32[]{:S(2)}, u32[]{:S(2)}) collective-permute-start(bf16[128,2048]{1,0:T(8,128)(2,1)S(1)} %get-tuple-element.109.refs_8_), channel_id=1, source_target_pairs={{0,2},{1,3},{2,4},{3,5},{4,6},{5,7},{6,8},{7,9},{8,10},{9,11},{10,... | collective-permute-start | bytes 1572872 | tf_op jit(solution)/shard_map/ppermute | solution.py:42
  56.0 16.1 %collective-permute-start.16 = (bf16[128,2048]{1,0:T(8,128)(2,1)S(1)}, bf16[128,2048]{1,0:T(8,128)(2,1)S(1)}, u32[]{:S(2)}, u32[]{:S(2)}) collective-permute-start(bf16[128,2048]{1,0:T(8,128)(2,1)S(1)} %get-tuple-element.102.refs_6_), channel_id=1, source_target_pairs={{0,14},{1,15},{2,0},{3,1},{4,2},{5,3},{6,4},{7,5},{8,6},{9,7},{10,... | collective-permute-start | bytes 1572872 | tf_op jit(solution)/shard_map/ppermute | solution.py:42
  59.2 14.8 %collective-permute-start.17 = (bf16[128,2048]{1,0:T(8,128)(2,1)S(1)}, bf16[128,2048]{1,0:T(8,128)(2,1)S(1)}, u32[]{:S(2)}, u32[]{:S(2)}) collective-permute-start(bf16[128,2048]{1,0:T(8,128)(2,1)S(1)} %get-tuple-element.109.refs_8_), channel_id=1, source_target_pairs={{0,16},{1,17},{2,18},{3,19},{4,20},{5,21},{6,22},{7,23},{8,24},{9,... | collective-permute-start | bytes 1572872 | tf_op jit(solution)/shard_map/ppermute | solution.py:42
  62.8 11.2 %collective-permute-start.19 = (bf16[128,2048]{1,0:T(8,128)(2,1)S(1)}, bf16[128,2048]{1,0:T(8,128)(2,1)S(1)}, u32[]{:S(2)}, u32[]{:S(2)}) collective-permute-start(bf16[128,2048]{1,0:T(8,128)(2,1)S(1)} %stack.1.refs_0_.a_ref.refs_20_), channel_id=1, source_target_pairs={{0,64},{32,96},{64,0},{96,32},{128,192},{160,224},{192,128},{224,1... | collective-permute-start | bytes 1572872 | tf_op jit(solution)/shard_map/ppermute | solution.py:50
  64.1 17.2 %collective-permute-start.20 = (bf16[128,2048]{1,0:T(8,128)(2,1)S(1)}, bf16[128,2048]{1,0:T(8,128)(2,1)S(1)}, u32[]{:S(2)}, u32[]{:S(2)}) collective-permute-start(bf16[128,2048]{1,0:T(8,128)(2,1)S(1)} %get-tuple-element.93.refs_3_), channel_id=1, source_target_pairs={{0,2},{1,3},{2,4},{3,5},{4,6},{5,7},{6,8},{7,9},{8,10},{9,11},{10,... | collective-permute-start | bytes 1572872 | tf_op jit(solution)/shard_map/ppermute | solution.py:42
  72.0 2.6 %copy-start.4 = (f32[2048]{0:T(1024)S(1)}, f32[2048]{0:T(1024)}, u32[]{:S(2)}) copy-start(f32[2048]{0:T(1024)} %param.8) | copy-start | bytes 24580
  72.0 9.3 %collective-permute-start.18 = (bf16[128,2048]{1,0:T(8,128)(2,1)S(1)}, bf16[128,2048]{1,0:T(8,128)(2,1)S(1)}, u32[]{:S(2)}, u32[]{:S(2)}) collective-permute-start(bf16[128,2048]{1,0:T(8,128)(2,1)S(1)} %get-tuple-element.117.refs_11_), channel_id=1, source_target_pairs={{0,14},{1,15},{2,0},{3,1},{4,2},{5,3},{6,4},{7,5},{8,6},{9,7},{10,... | collective-permute-start | bytes 1572872 | tf_op jit(solution)/shard_map/ppermute | solution.py:42
  72.3 10.5 %collective-permute-start.21 = (bf16[128,2048]{1,0:T(8,128)(2,1)S(1)}, bf16[128,2048]{1,0:T(8,128)(2,1)S(1)}, u32[]{:S(2)}, u32[]{:S(2)}) collective-permute-start(bf16[128,2048]{1,0:T(8,128)(2,1)S(1)} %get-tuple-element.115.refs_10_), channel_id=1, source_target_pairs={{0,16},{1,17},{2,18},{3,19},{4,20},{5,21},{6,22},{7,23},{8,24},{9,... | collective-permute-start | bytes 1572872 | tf_op jit(solution)/shard_map/ppermute | solution.py:42
  74.0 8.8 %collective-permute-start.22 = (bf16[128,2048]{1,0:T(8,128)(2,1)S(1)}, bf16[128,2048]{1,0:T(8,128)(2,1)S(1)}, u32[]{:S(2)}, u32[]{:S(2)}) collective-permute-start(bf16[128,2048]{1,0:T(8,128)(2,1)S(1)} %late.1), channel_id=1, source_target_pairs={{0,1},{1,0},{2,3},{3,2},{4,5},{5,4},{6,7},{7,6},{8,9},{9,8},{10,11... | collective-permute-start | bytes 1572872 | tf_op jit(solution)/shard_map/ppermute | solution.py:42
  74.1 8.7 %collective-permute-start.23 = (bf16[128,2048]{1,0:T(8,128)(2,1)S(1)}, bf16[128,2048]{1,0:T(8,128)(2,1)S(1)}, u32[]{:S(2)}, u32[]{:S(2)}) collective-permute-start(bf16[128,2048]{1,0:T(8,128)(2,1)S(1)} %get-tuple-element.128.refs_1_.b_ref.refs_21_), channel_id=1, source_target_pairs={{0,1},{1,0},{2,3},{3,2},{4,5},{5,4},{6,7},{7,6},{8,9},{9,8},{10,11... | collective-permute-start | bytes 1572872 | tf_op jit(solution)/shard_map/ppermute | solution.py:42
  98.3 3.1 %collective-permute-start.24 = (bf16[272,2048]{1,0:T(8,128)(2,1)S(1)}, bf16[272,2048]{1,0:T(8,128)(2,1)S(1)}, u32[]{:S(2)}, u32[]{:S(2)}) collective-permute-start(bf16[272,2048]{1,0:T(8,128)(2,1)S(1)} %get-tuple-element.146), channel_id=1, source_target_pairs={{0,1},{1,0},{2,3},{3,2},{4,5},{5,4},{6,7},{7,6},{8,9},{9,8},{10,11... | collective-permute-start | bytes 3342344 | tf_op jit(solution)/shard_map/ppermute | solution.py:42
  98.6 7.8 %collective-permute-start.25 = (bf16[256,2048]{1,0:T(8,128)(2,1)S(1)}, bf16[256,2048]{1,0:T(8,128)(2,1)S(1)}, u32[]{:S(2)}, u32[]{:S(2)}) collective-permute-start(bf16[256,2048]{1,0:T(8,128)(2,1)S(1)} %get-tuple-element.148), channel_id=1, source_target_pairs={{0,1},{1,0},{2,3},{3,2},{4,5},{5,4},{6,7},{7,6},{8,9},{9,8},{10,11... | collective-permute-start | bytes 3145736 | tf_op jit(solution)/shard_map/ppermute | solution.py:42
  101.7 21.5 %collective-permute-start.26 = (bf16[64,2048]{1,0:T(8,128)(2,1)S(1)}, bf16[64,2048]{1,0:T(8,128)(2,1)S(1)}, u32[]{:S(2)}, u32[]{:S(2)}) collective-permute-start(bf16[64,2048]{1,0:T(8,128)(2,1)S(1)} %get-tuple-element.153), channel_id=1, source_target_pairs={{0,32},{32,0},{64,96},{96,64},{128,160},{160,128},{192,224},{224,1... | collective-permute-start | bytes 786440 | tf_op jit(solution)/shard_map/ppermute | solution.py:50
  102.6 20.6 %collective-permute-start.27 = (bf16[64,2048]{1,0:T(8,128)(2,1)S(1)}, bf16[64,2048]{1,0:T(8,128)(2,1)S(1)}, u32[]{:S(2)}, u32[]{:S(2)}) collective-permute-start(bf16[64,2048]{1,0:T(8,128)(2,1)S(1)} %get-tuple-element.154), channel_id=1, source_target_pairs={{0,64},{32,96},{64,0},{96,32},{128,192},{160,224},{192,128},{224,1... | collective-permute-start | bytes 786440 | tf_op jit(solution)/shard_map/ppermute | solution.py:50
  104.1 19.1 %collective-permute-start.28 = (bf16[64,2048]{1,0:T(8,128)(2,1)S(1)}, bf16[64,2048]{1,0:T(8,128)(2,1)S(1)}, u32[]{:S(2)}, u32[]{:S(2)}) collective-permute-start(bf16[64,2048]{1,0:T(8,128)(2,1)S(1)} %get-tuple-element.155), channel_id=1, source_target_pairs={{0,96},{32,64},{64,32},{96,0},{128,224},{160,192},{192,160},{224,1... | collective-permute-start | bytes 786440 | tf_op jit(solution)/shard_map/ppermute | solution.py:50
  106.5 5.4 %collective-permute-start.31 = (f32[1,2048]{1,0:T(1,128)S(1)}, f32[1,2048]{1,0:T(1,128)S(1)}, u32[]{:S(2)}, u32[]{:S(2)}) collective-permute-start(f32[1,2048]{1,0:T(1,128)S(1)} %get-tuple-element.156.a_ref), channel_id=1, source_target_pairs={{0,6},{1,7},{2,4},{3,5},{4,2},{5,3},{6,0},{7,1},{8,14},{9,15},{10,... | collective-permute-start | bytes 24584 | tf_op jit(solution)/shard_map/ppermute | solution.py:42
  108.8 4.5 %collective-permute-start.30 = (f32[1,2048]{1,0:T(1,128)S(1)}, f32[1,2048]{1,0:T(1,128)S(1)}, u32[]{:S(2)}, u32[]{:S(2)}) collective-permute-start(f32[1,2048]{1,0:T(1,128)S(1)} %get-tuple-element.156.a_ref), channel_id=1, source_target_pairs={{0,4},{1,5},{2,6},{3,7},{4,0},{5,1},{6,2},{7,3},{8,12},{9,13},{10,... | collective-permute-start | bytes 24584 | tf_op jit(solution)/shard_map/ppermute | solution.py:42
  111.9 3.7 %collective-permute-start.29 = (f32[1,2048]{1,0:T(1,128)S(1)}, f32[1,2048]{1,0:T(1,128)S(1)}, u32[]{:S(2)}, u32[]{:S(2)}) collective-permute-start(f32[1,2048]{1,0:T(1,128)S(1)} %get-tuple-element.156.a_ref), channel_id=1, source_target_pairs={{0,2},{1,3},{2,0},{3,1},{4,6},{5,7},{6,4},{7,5},{8,10},{9,11},{10,... | collective-permute-start | bytes 24584 | tf_op jit(solution)/shard_map/ppermute | solution.py:42
  115.6 7.6 %collective-permute-start.32 = (f32[1,2048]{1,0:T(1,128)S(1)}, f32[1,2048]{1,0:T(1,128)S(1)}, u32[]{:S(2)}, u32[]{:S(2)}) collective-permute-start(f32[1,2048]{1,0:T(1,128)S(1)} %add.5.a_ref), channel_id=1, source_target_pairs={{0,8},{1,9},{2,10},{3,11},{4,12},{5,13},{6,14},{7,15},{8,0},{9,1},... | collective-permute-start | bytes 24584 | tf_op jit(solution)/shard_map/ppermute | solution.py:42
  123.3 9.9 %collective-permute-start.33 = (bf16[64,2048]{1,0:T(8,128)(2,1)S(1)}, bf16[64,2048]{1,0:T(8,128)(2,1)S(1)}, u32[]{:S(2)}, u32[]{:S(2)}) collective-permute-start(bf16[64,2048]{1,0:T(8,128)(2,1)S(1)} %get-tuple-element.163), channel_id=1, source_target_pairs={{0,128},{32,160},{64,192},{96,224},{128,0},{160,32},{192,64},{224,... | collective-permute-start | bytes 786440 | tf_op jit(solution)/shard_map/ppermute | solution.py:50
  125.8 4.9 %collective-permute-start.36 = (f32[1,2048]{1,0:T(1,128)S(1)}, f32[1,2048]{1,0:T(1,128)S(1)}, u32[]{:S(2)}, u32[]{:S(2)}) collective-permute-start(f32[1,2048]{1,0:T(1,128)S(1)} %get-tuple-element.164.a_ref), channel_id=1, source_target_pairs={{0,96},{32,64},{64,32},{96,0},{128,224},{160,192},{192,160},{224,1... | collective-permute-start | bytes 24584 | tf_op jit(solution)/shard_map/ppermute | solution.py:50
  127.9 5.3 %collective-permute-start.35 = (f32[1,2048]{1,0:T(1,128)S(1)}, f32[1,2048]{1,0:T(1,128)S(1)}, u32[]{:S(2)}, u32[]{:S(2)}) collective-permute-start(f32[1,2048]{1,0:T(1,128)S(1)} %get-tuple-element.164.a_ref), channel_id=1, source_target_pairs={{0,64},{32,96},{64,0},{96,32},{128,192},{160,224},{192,128},{224,1... | collective-permute-start | bytes 24584 | tf_op jit(solution)/shard_map/ppermute | solution.py:50
  128.6 4.6 %collective-permute-start.34 = (f32[1,2048]{1,0:T(1,128)S(1)}, f32[1,2048]{1,0:T(1,128)S(1)}, u32[]{:S(2)}, u32[]{:S(2)}) collective-permute-start(f32[1,2048]{1,0:T(1,128)S(1)} %get-tuple-element.164.a_ref), channel_id=1, source_target_pairs={{0,32},{32,0},{64,96},{96,64},{128,160},{160,128},{192,224},{224,1... | collective-permute-start | bytes 24584 | tf_op jit(solution)/shard_map/ppermute | solution.py:50
  133.3 13.6 %collective-permute-start.39 = (bf16[64,2048]{1,0:T(8,128)(2,1)S(1)}, bf16[64,2048]{1,0:T(8,128)(2,1)S(1)}, u32[]{:S(2)}, u32[]{:S(2)}) collective-permute-start(bf16[64,2048]{1,0:T(8,128)(2,1)S(1)} %get-tuple-element.165.refs_0_), channel_id=1, source_target_pairs={{0,96},{32,64},{64,32},{96,0},{128,224},{160,192},{192,160},{224,1... | collective-permute-start | bytes 786440 | tf_op jit(solution)/shard_map/ppermute | solution.py:50
  134.5 12.4 %collective-permute-start.38 = (bf16[64,2048]{1,0:T(8,128)(2,1)S(1)}, bf16[64,2048]{1,0:T(8,128)(2,1)S(1)}, u32[]{:S(2)}, u32[]{:S(2)}) collective-permute-start(bf16[64,2048]{1,0:T(8,128)(2,1)S(1)} %get-tuple-element.165.refs_0_), channel_id=1, source_target_pairs={{0,64},{32,96},{64,0},{96,32},{128,192},{160,224},{192,128},{224,1... | collective-permute-start | bytes 786440 | tf_op jit(solution)/shard_map/ppermute | solution.py:50
  135.8 11.1 %collective-permute-start.37 = (bf16[64,2048]{1,0:T(8,128)(2,1)S(1)}, bf16[64,2048]{1,0:T(8,128)(2,1)S(1)}, u32[]{:S(2)}, u32[]{:S(2)}) collective-permute-start(bf16[64,2048]{1,0:T(8,128)(2,1)S(1)} %get-tuple-element.165.refs_0_), channel_id=1, source_target_pairs={{0,32},{32,0},{64,96},{96,64},{128,160},{160,128},{192,224},{224,1... | collective-permute-start | bytes 786440 | tf_op jit(solution)/shard_map/ppermute | solution.py:50
  137.5 3.7 %collective-permute-start.40 = (f32[1,2048]{1,0:T(1,128)S(1)}, f32[1,2048]{1,0:T(1,128)S(1)}, u32[]{:S(2)}, u32[]{:S(2)}) collective-permute-start(f32[1,2048]{1,0:T(1,128)S(1)} %get-tuple-element.166.a_ref), channel_id=1, source_target_pairs={{0,16},{1,17},{2,18},{3,19},{4,20},{5,21},{6,22},{7,23},{8,24},{9,... | collective-permute-start | bytes 24584 | tf_op jit(solution)/shard_map/ppermute | solution.py:42
  141.1 5.2 %collective-permute-start.41 = (f32[1,2048]{1,0:T(1,128)S(1)}, f32[1,2048]{1,0:T(1,128)S(1)}, u32[]{:S(2)}, u32[]{:S(2)}) collective-permute-start(f32[1,2048]{1,0:T(1,128)S(1)} %add.8.a_ref), channel_id=1, source_target_pairs={{0,128},{32,160},{64,192},{96,224},{128,0},{160,32},{192,64},{224,... | collective-permute-start | bytes 24584 | tf_op jit(solution)/shard_map/ppermute | solution.py:50

commit v3 on v2

--- a/solution.py
+++ b/solution.py
@@ -182,6 +182,11 @@
     rows = out_ref.shape[0] // len(parts)
     for index, part in enumerate(parts):
         out_ref[index * rows:(index + 1) * rows, :] = part[...]
+
+
+def add_after_kernel(a_ref, b_ref, done_ref, out_ref):
+    del done_ref
+    out_ref[...] = a_ref[...] + b_ref[...]
 
 
 def late_kernel(a_ref, token_ref, out_ref):
@@ -373,6 +378,18 @@
     )(*args)
 
 
+def add_after(a, b, done):
+    return pl.pallas_call(
+        add_after_kernel,
+        in_specs=[VMEM, VMEM, ANY],
+        out_specs=VMEM,
+        out_shape=jax.ShapeDtypeStruct(a.shape, a.dtype),
+        compiler_params=pltpu.CompilerParams(vmem_limit_bytes=MIB),
+        cost_estimate=pl.CostEstimate(flops=0, bytes_accessed=1024, transcendentals=0),
+        name="add",
+    )(a, b, done)
+
+
 def bf16_rows(rows):
     return jax.ShapeDtypeStruct((rows, D), bf16)
 
@@ -472,15 +489,14 @@
     up, down, across = from_above(a[0]), from_below(a[0]), other_column(a[0])
     qg_oth = other_core(copy_call(give_kernel, bf16_rows(LEN), (rows, cot, a[0]), "give", 2))
 
+    a[1], qg_oth = order.take(up, qg_oth)
+    up, across_1 = from_above(a[1]), other_column(a[1])
+    a[-1] = order.take(down)
+    down = from_below(a[-1])
     hidden = order.take(hidden)
     mine, send = select(0, rows, hidden)
     hidden = other_y(send, 1)
-
-    a[1] = order.take(up)
-    up, across_1 = from_above(a[1]), other_column(a[1])
-    a[-1] = order.take(down)
-    down = from_below(a[-1])
-    b[0], qg_oth = order.take(across, qg_oth)
+    b[0] = order.take(across)
     hidden = order.take(hidden)
     mine = select(1, mine, hidden)
     hidden = other_high(mine)
@@ -549,7 +565,8 @@
     far, near, other = other_y(parts[1], 2), other_y(parts[0], 1), other_y(parts[2], 3)
     gain_part, got_out = order.take(gain_part, other_core(oth_out))
     gain_part = butterfly(gain_part, *[z_move(bits) for bits in (1, 2, 3)])
-    gain_part = add_from(gain_part, z_move(4))
+    section_out = put_out(0, section_map, own_out, got_out, [enc_out], "rows")
+    gain_part = add_after(gain_part, z_move(4)(gain_part), section_out)
     near, far, other, gain_part = order.take(near, far, other, gain_part)
     kept, sent, gain_part = small_call(
         sum_kernel, [ROWS32, quarter, LINE], (kept, gain_part, near, far, other), "sum"
@@ -561,7 +578,6 @@
     gain_part = add_from(gain_part, other_column)
     gain_part = add_from(gain_part, other_high)
     dhs = [dh, near, far, other]
-    section_out = put_out(0, section_map, own_out, got_out, [enc_out], "rows")
     section_grad = put_out(F, section_map, own_out, got_out, dhs, "grads")
     return (section_out[None], section_grad[None], gain_part.reshape(D))
 

time: 150 us -> 151 us (level)
  starting transfers between devices: 50.3 us -> 54.8 us
  waiting for transfers between devices: 71.8 us -> 67.9 us
    ppermute x16, starting transfers between devices: 23.6 us -> 28.7 us  [section_swap(): return lax.ppermute(x, 'section', pairs)]
    ppermute x16, waiting for transfers between devices: 27 us -> 24.2 us  [section_swap(): return lax.ppermute(x, 'section', pairs)]
    unnamed x12 -> x14, local copies, waits for them, and re-layouts: 2.27 us -> 3.58 us
    pallas_call x16 -> x15, Pallas kernels: 4.99 us -> 4.94 us  [small_call(): pl.pallas_call(kernel, in_specs=[SMEM] * len(first) + [VMEM] * len(args),...]
  transfers between devices with their start and end apart: 42 -> 42, of which waited for: 20 -> 21; matrix products, arithmetic and copies ran while one was open for 0% -> 0% of each run, Pallas kernels for 4% -> 4%
where the time goes in v3:
time: 151 us; the launch traced here: 150 us
  waiting for transfers between devices  67.9 us (45%)
  starting transfers between devices  54.8 us (36%)
  Pallas kernels  23.2 us (15%)
  local copies, waits for them, and re-layouts  3.58 us (2%)
    ppermute x26, waiting for transfers between devices, dp_swap(): return lax.ppermute(x, 'dp', pairs)  43.7 us
    ppermute x16, starting transfers between devices, section_swap(): return lax.ppermute(x, 'section', pairs)  28.7 us
    ppermute x26, starting transfers between devices, dp_swap(): return lax.ppermute(x, 'dp', pairs)  26 us
    ppermute x16, waiting for transfers between devices, section_swap(): return lax.ppermute(x, 'section', pairs)  24.2 us
    pallas_call x1, Pallas kernels, attend(): pl.pallas_call(main_kernel, in_specs=[VMEM] * (N_SLOT + 12) + [SMEM] + [V...  14.8 us
    pallas_call x15, Pallas kernels, small_call(): pl.pallas_call(kernel, in_specs=[SMEM] * len(first) + [VMEM] * len(args),...  4.94 us
    unnamed x14, local copies, waits for them, and re-layouts  3.58 us
    pallas_call x2, Pallas kernels, put_out(): pl.pallas_call(functools.partial(out_kernel, offset), in_specs=[SMEM] + [...  3.12 us
  transfers between devices with their start and end apart: 42, of which 21 were waited for; matrix products, arithmetic and copies ran while one was open for 0% of the time, Pallas kernels for 4%

profile of v3, /device:TPU:6, one launch (start us, length us, event | category | flops | bytes accessed | tf_op | source)
XLA Modules:
  0.0 150.5 jit_solution(13902808830778881915)
XLA Ops:
  0.6 1.1 copy-done.4
  2.0 1.5 %collective-permute-done.got_ref = bf16[64,2048]{1,0:T(8,128)(2,1)S(1)} collective-permute-done((bf16[64,2048]{1,0:T(8,128)(2,1)S(1)}, bf16[64,2048]{1,0:T(8,128)(2,1)S(1)}, u32[]{:S(2)}, u32[]{:S(2)}) %collective-permute-start) | collective-permute-done | bytes 262176 | tf_op jit(solution)/shard_map/ppermute | solution.py:42
  3.6 1.2 copy-done.1
  5.0 0.2 collective-permute-start.2
  5.2 5.9 %collective-permute-start.1 = (bf16[128,2048]{1,0:T(8,128)(2,1)S(1)}, bf16[128,2048]{1,0:T(8,128)(2,1)S(1)}, u32[]{:S(2)}, u32[]{:S(2)}) collective-permute-start(bf16[128,2048]{1,0:T(8,128)(2,1)S(1)} %unit.1.token_ref.refs_0_), channel_id=1, source_target_pairs={{0,14},{1,15},{2,0},{3,1},{4,2},{5,3},{6,4},{7,5},{8,6},{9,7},{10,... | collective-permute-start | bytes 1572872 | tf_op jit(solution)/shard_map/ppermute | solution.py:42
  11.1 3.3 %collective-permute-start.5 = (bf16[128,2048]{1,0:T(8,128)(2,1)S(1)}, bf16[128,2048]{1,0:T(8,128)(2,1)S(1)}, u32[]{:S(2)}, u32[]{:S(2)}) collective-permute-start(bf16[128,2048]{1,0:T(8,128)(2,1)S(1)} %half.1), channel_id=1, source_target_pairs={{0,64},{32,96},{64,0},{96,32},{128,192},{160,224},{192,128},{224,1... | collective-permute-start | bytes 1572872 | tf_op jit(solution)/shard_map/ppermute | solution.py:50
  14.4 0.8 collective-permute-start.4
  15.2 7.5 %collective-permute-done.1.refs_0_ = bf16[128,2048]{1,0:T(8,128)(2,1)S(1)} collective-permute-done((bf16[128,2048]{1,0:T(8,128)(2,1)S(1)}, bf16[128,2048]{1,0:T(8,128)(2,1)S(1)}, u32[]{:S(2)}, u32[]{:S(2)}) %collective-permute-start.1) | collective-permute-done | bytes 524320 | tf_op jit(solution)/shard_map/ppermute | solution.py:42
  22.8 3.7 %collective-permute-start.6 = (bf16[128,2048]{1,0:T(8,128)(2,1)S(1)}, bf16[128,2048]{1,0:T(8,128)(2,1)S(1)}, u32[]{:S(2)}, u32[]{:S(2)}) collective-permute-start(bf16[128,2048]{1,0:T(8,128)(2,1)S(1)} %get-tuple-element.88.refs_1_), channel_id=1, source_target_pairs={{0,14},{1,15},{2,0},{3,1},{4,2},{5,3},{6,4},{7,5},{8,6},{9,7},{10,... | collective-permute-start | bytes 1572872 | tf_op jit(solution)/shard_map/ppermute | solution.py:42
  26.5 0.1 collective-permute-done.5.refs_0_
  26.6 0.6 select.3
  27.2 1.7 %collective-permute-start.7 = (bf16[64,2048]{1,0:T(8,128)(2,1)S(1)}, bf16[64,2048]{1,0:T(8,128)(2,1)S(1)}, u32[]{:S(2)}, u32[]{:S(2)}) collective-permute-start(bf16[64,2048]{1,0:T(8,128)(2,1)S(1)} %get-tuple-element.95), channel_id=1, source_target_pairs={{0,32},{32,0},{64,96},{96,64},{128,160},{160,128},{192,224},{224,1... | collective-permute-start | bytes 786440 | tf_op jit(solution)/shard_map/ppermute | solution.py:50
  28.9 0.8 collective-permute-start.9
  29.7 5.0 %collective-permute-done.7.refs_0_ = bf16[64,2048]{1,0:T(8,128)(2,1)S(1)} collective-permute-done((bf16[64,2048]{1,0:T(8,128)(2,1)S(1)}, bf16[64,2048]{1,0:T(8,128)(2,1)S(1)}, u32[]{:S(2)}, u32[]{:S(2)}) %collective-permute-start.7) | collective-permute-done | bytes 262176 | tf_op jit(solution)/shard_map/ppermute | solution.py:50
  34.8 2.6 %collective-permute-done.6.refs_0_ = bf16[128,2048]{1,0:T(8,128)(2,1)S(1)} collective-permute-done((bf16[128,2048]{1,0:T(8,128)(2,1)S(1)}, bf16[128,2048]{1,0:T(8,128)(2,1)S(1)}, u32[]{:S(2)}, u32[]{:S(2)}) %collective-permute-start.6) | collective-permute-done | bytes 524320 | tf_op jit(solution)/shard_map/ppermute | solution.py:42
  37.4 3.7 %collective-permute-start.10 = (bf16[128,2048]{1,0:T(8,128)(2,1)S(1)}, bf16[128,2048]{1,0:T(8,128)(2,1)S(1)}, u32[]{:S(2)}, u32[]{:S(2)}) collective-permute-start(bf16[128,2048]{1,0:T(8,128)(2,1)S(1)} %get-tuple-element.98.refs_4_), channel_id=1, source_target_pairs={{0,14},{1,15},{2,0},{3,1},{4,2},{5,3},{6,4},{7,5},{8,6},{9,7},{10,... | collective-permute-start | bytes 1572872 | tf_op jit(solution)/shard_map/ppermute | solution.py:42
  41.1 0.6 select.4.own_ref
  41.6 1.5 collective-permute-start.11
  43.1 9.3 %collective-permute-done.11.refs_0_ = bf16[64,2048]{1,0:T(8,128)(2,1)S(1)} collective-permute-done((bf16[64,2048]{1,0:T(8,128)(2,1)S(1)}, bf16[64,2048]{1,0:T(8,128)(2,1)S(1)}, u32[]{:S(2)}, u32[]{:S(2)}) %collective-permute-start.11) | collective-permute-done | bytes 262176 | tf_op jit(solution)/shard_map/ppermute | solution.py:50
  52.5 0.6 select.5.refs_0_
  53.1 1.7 %collective-permute-start.15 = (bf16[64,2048]{1,0:T(8,128)(2,1)S(1)}, bf16[64,2048]{1,0:T(8,128)(2,1)S(1)}, u32[]{:S(2)}, u32[]{:S(2)}) collective-permute-start(bf16[64,2048]{1,0:T(8,128)(2,1)S(1)} %select.5.refs_0_), channel_id=1, source_target_pairs={{0,32},{32,0},{64,96},{96,64},{128,160},{160,128},{192,224},{224,1... | collective-permute-start | bytes 786440 | tf_op jit(solution)/shard_map/ppermute | solution.py:50
  54.8 3.3 %collective-permute-start.16 = (bf16[128,2048]{1,0:T(8,128)(2,1)S(1)}, bf16[128,2048]{1,0:T(8,128)(2,1)S(1)}, u32[]{:S(2)}, u32[]{:S(2)}) collective-permute-start(bf16[128,2048]{1,0:T(8,128)(2,1)S(1)} %get-tuple-element.102.refs_6_), channel_id=1, source_target_pairs={{0,14},{1,15},{2,0},{3,1},{4,2},{5,3},{6,4},{7,5},{8,6},{9,7},{10,... | collective-permute-start | bytes 1572872 | tf_op jit(solution)/shard_map/ppermute | solution.py:42
  58.1 0.8 collective-permute-start.17
  59.0 2.2 %collective-permute-done.13.refs_0_ = bf16[128,2048]{1,0:T(8,128)(2,1)S(1)} collective-permute-done((bf16[128,2048]{1,0:T(8,128)(2,1)S(1)}, bf16[128,2048]{1,0:T(8,128)(2,1)S(1)}, u32[]{:S(2)}, u32[]{:S(2)}) %collective-permute-start.13) | collective-permute-done | bytes 524320 | tf_op jit(solution)/shard_map/ppermute | solution.py:42
  61.2 3.3 %collective-permute-start.19 = (bf16[128,2048]{1,0:T(8,128)(2,1)S(1)}, bf16[128,2048]{1,0:T(8,128)(2,1)S(1)}, u32[]{:S(2)}, u32[]{:S(2)}) collective-permute-start(bf16[128,2048]{1,0:T(8,128)(2,1)S(1)} %stack.1.refs_0_.a_ref.refs_20_), channel_id=1, source_target_pairs={{0,64},{32,96},{64,0},{96,32},{128,192},{160,224},{192,128},{224,1... | collective-permute-start | bytes 1572872 | tf_op jit(solution)/shard_map/ppermute | solution.py:50
  64.5 6.2 %collective-permute-done.14.refs_0_ = bf16[128,2048]{1,0:T(8,128)(2,1)S(1)} collective-permute-done((bf16[128,2048]{1,0:T(8,128)(2,1)S(1)}, bf16[128,2048]{1,0:T(8,128)(2,1)S(1)}, u32[]{:S(2)}, u32[]{:S(2)}) %collective-permute-start.14) | collective-permute-done | bytes 524320 | tf_op jit(solution)/shard_map/ppermute | solution.py:42
  70.8 0.3 collective-permute-start.21
  71.1 1.3 collective-permute-done.17.refs_0_
  72.4 0.8 collective-permute-done.19.refs_0_
  73.4 0.5 collective-permute-start.23
  73.9 0.7 norm.2
  74.6 0.6 encoder.1
  75.2 4.8 %collective-permute-done.18.refs_0_ = bf16[128,2048]{1,0:T(8,128)(2,1)S(1)} collective-permute-done((bf16[128,2048]{1,0:T(8,128)(2,1)S(1)}, bf16[128,2048]{1,0:T(8,128)(2,1)S(1)}, u32[]{:S(2)}, u32[]{:S(2)}) %collective-permute-start.18) | collective-permute-done | bytes 524320 | tf_op jit(solution)/shard_map/ppermute | solution.py:42
  79.9 1.4 collective-permute-done.21.refs_0_
  81.3 0.7 norm.3
  82.1 14.8 %attend.1 = (bf16[256,2048]{1,0:T(8,128)(2,1)S(1)}, bf16[256,2048]{1,0:T(8,128)(2,1)S(1)}, bf16[256,2048]{1,0:T(8,128)(2,1)S(1)}, bf16[272,2048]{1,0:T(8,128)(2,1)S(1)}, f32[1,2048]{1,0:T(1,128)S(1)}) custom-call(bf16[128,2048]{1,0:T(8,128)(2,1)S(1)} %unit.1.token_ref.refs_0_, bf16[128,2048]{1,0:T(8,128)(2,1)S(1)} %get-tuple-element.88.refs_1_, ...), custom_call_target="tpu_custom_call" | custom-call | flops 10000000000 | bytes 20000000 | tf_op jit(solution)/shard_map/attend/pallas_call | solution.py:338
  96.8 0.3 collective-permute-start.24
  97.1 0.5 collective-permute-start.25
  97.6 2.2 %collective-permute-done.24.got_ref = bf16[272,2048]{1,0:T(8,128)(2,1)S(1)} collective-permute-done((bf16[272,2048]{1,0:T(8,128)(2,1)S(1)}, bf16[272,2048]{1,0:T(8,128)(2,1)S(1)}, u32[]{:S(2)}, u32[]{:S(2)}) %collective-permute-start.24) | collective-permute-done | bytes 1114144 | tf_op jit(solution)/shard_map/ppermute | solution.py:42
  99.9 0.3 split.1
  100.2 1.7 %collective-permute-start.26 = (bf16[64,2048]{1,0:T(8,128)(2,1)S(1)}, bf16[64,2048]{1,0:T(8,128)(2,1)S(1)}, u32[]{:S(2)}, u32[]{:S(2)}) collective-permute-start(bf16[64,2048]{1,0:T(8,128)(2,1)S(1)} %get-tuple-element.153), channel_id=1, source_target_pairs={{0,32},{32,0},{64,96},{96,64},{128,160},{160,128},{192,224},{224,1... | collective-permute-start | bytes 786440 | tf_op jit(solution)/shard_map/ppermute | solution.py:50
  101.8 2.9 %collective-permute-start.27 = (bf16[64,2048]{1,0:T(8,128)(2,1)S(1)}, bf16[64,2048]{1,0:T(8,128)(2,1)S(1)}, u32[]{:S(2)}, u32[]{:S(2)}) collective-permute-start(bf16[64,2048]{1,0:T(8,128)(2,1)S(1)} %get-tuple-element.154), channel_id=1, source_target_pairs={{0,64},{32,96},{64,0},{96,32},{128,192},{160,224},{192,128},{224,1... | collective-permute-start | bytes 786440 | tf_op jit(solution)/shard_map/ppermute | solution.py:50
  104.7 0.2 collective-permute-start.28
  105.0 2.3 %collective-permute-start.31 = (f32[1,2048]{1,0:T(1,128)S(1)}, f32[1,2048]{1,0:T(1,128)S(1)}, u32[]{:S(2)}, u32[]{:S(2)}) collective-permute-start(f32[1,2048]{1,0:T(1,128)S(1)} %get-tuple-element.156.a_ref), channel_id=1, source_target_pairs={{0,6},{1,7},{2,4},{3,5},{4,2},{5,3},{6,0},{7,1},{8,14},{9,15},{10,... | collective-permute-start | bytes 24584 | tf_op jit(solution)/shard_map/ppermute | solution.py:42
  107.3 3.1 %collective-permute-done.31.d_ref = f32[1,2048]{1,0:T(1,128)S(1)} collective-permute-done((f32[1,2048]{1,0:T(1,128)S(1)}, f32[1,2048]{1,0:T(1,128)S(1)}, u32[]{:S(2)}, u32[]{:S(2)}) %collective-permute-start.31) | collective-permute-done | bytes 8224 | tf_op jit(solution)/shard_map/ppermute | solution.py:42
  110.4 1.4 collective-permute-done.30.c_ref
  111.9 2.2 %collective-permute-done.29.b_ref = f32[1,2048]{1,0:T(1,128)S(1)} collective-permute-done((f32[1,2048]{1,0:T(1,128)S(1)}, f32[1,2048]{1,0:T(1,128)S(1)}, u32[]{:S(2)}, u32[]{:S(2)}) %collective-permute-start.29) | collective-permute-done | bytes 8224 | tf_op jit(solution)/shard_map/ppermute | solution.py:42
  114.1 2.5 %collective-permute-start.32 = (f32[1,2048]{1,0:T(1,128)S(1)}, f32[1,2048]{1,0:T(1,128)S(1)}, u32[]{:S(2)}, u32[]{:S(2)}) collective-permute-start(f32[1,2048]{1,0:T(1,128)S(1)} %add.5.a_ref), channel_id=1, source_target_pairs={{0,8},{1,9},{2,10},{3,11},{4,12},{5,13},{6,14},{7,15},{8,0},{9,1},... | collective-permute-start | bytes 24584 | tf_op jit(solution)/shard_map/ppermute | solution.py:42
  116.5 1.6 %rows.1.done_ref = bf16[256,2048]{1,0:T(8,128)(2,1)} custom-call(s32[8]{0:T(128)S(1)} %copy-done.6, bf16[256,2048]{1,0:T(8,128)(2,1)S(1)} %get-tuple-element.143.own_ref, bf16[256,2048]{1,0:T(8,128)(2,1)S(1)} %get-tuple-element.150.oth_ref, bf16[256,2048]{1,0:T(8,128)(2,1)S(1)} %get-tuple-element.151.refs_0_), custom_call_target="tpu_custom_call" | custom-call | bytes 2000000 | tf_op jit(solution)/shard_map/rows/pallas_call | solution.py:459
  118.1 3.5 %collective-permute-done.32.b_ref = f32[1,2048]{1,0:T(1,128)S(1)} collective-permute-done((f32[1,2048]{1,0:T(1,128)S(1)}, f32[1,2048]{1,0:T(1,128)S(1)}, u32[]{:S(2)}, u32[]{:S(2)}) %collective-permute-start.32) | collective-permute-done | bytes 8224 | tf_op jit(solution)/shard_map/ppermute | solution.py:42
  121.6 1.2 copy-done.3
  123.0 3.7 %collective-permute-start.33 = (bf16[64,2048]{1,0:T(8,128)(2,1)S(1)}, bf16[64,2048]{1,0:T(8,128)(2,1)S(1)}, u32[]{:S(2)}, u32[]{:S(2)}) collective-permute-start(bf16[64,2048]{1,0:T(8,128)(2,1)S(1)} %get-tuple-element.163), channel_id=1, source_target_pairs={{0,128},{32,160},{64,192},{96,224},{128,0},{160,32},{192,64},{224,... | collective-permute-start | bytes 786440 | tf_op jit(solution)/shard_map/ppermute | solution.py:50
  126.7 3.0 %collective-permute-start.36 = (f32[1,2048]{1,0:T(1,128)S(1)}, f32[1,2048]{1,0:T(1,128)S(1)}, u32[]{:S(2)}, u32[]{:S(2)}) collective-permute-start(f32[1,2048]{1,0:T(1,128)S(1)} %get-tuple-element.164.a_ref), channel_id=1, source_target_pairs={{0,96},{32,64},{64,32},{96,0},{128,224},{160,192},{192,160},{224,1... | collective-permute-start | bytes 24584 | tf_op jit(solution)/shard_map/ppermute | solution.py:50
  129.8 1.1 collective-permute-start.34
  130.8 0.8 collective-permute-done.36.d_ref
  131.6 3.5 %collective-permute-done.35.c_ref = f32[1,2048]{1,0:T(1,128)S(1)} collective-permute-done((f32[1,2048]{1,0:T(1,128)S(1)}, f32[1,2048]{1,0:T(1,128)S(1)}, u32[]{:S(2)}, u32[]{:S(2)}) %collective-permute-start.35) | collective-permute-done | bytes 8224 | tf_op jit(solution)/shard_map/ppermute | solution.py:50
  135.1 0.8 collective-permute-start.39
  135.9 1.4 collective-permute-start.38
  137.3 2.1 %collective-permute-start.37 = (bf16[64,2048]{1,0:T(8,128)(2,1)S(1)}, bf16[64,2048]{1,0:T(8,128)(2,1)S(1)}, u32[]{:S(2)}, u32[]{:S(2)}) collective-permute-start(bf16[64,2048]{1,0:T(8,128)(2,1)S(1)} %get-tuple-element.165.refs_0_), channel_id=1, source_target_pairs={{0,32},{32,0},{64,96},{96,64},{128,160},{160,128},{192,224},{224,1... | collective-permute-start | bytes 786440 | tf_op jit(solution)/shard_map/ppermute | solution.py:50
  139.3 3.6 %collective-permute-done.40.b_ref = f32[1,2048]{1,0:T(1,128)S(1)} collective-permute-done((f32[1,2048]{1,0:T(1,128)S(1)}, f32[1,2048]{1,0:T(1,128)S(1)}, u32[]{:S(2)}, u32[]{:S(2)}) %collective-permute-start.40) | collective-permute-done | bytes 8224 | tf_op jit(solution)/shard_map/ppermute | solution.py:42
  143.0 0.6 collective-permute-start.41
  143.6 4.6 %collective-permute-done.41.b_ref = f32[1,2048]{1,0:T(1,128)S(1)} collective-permute-done((f32[1,2048]{1,0:T(1,128)S(1)}, f32[1,2048]{1,0:T(1,128)S(1)}, u32[]{:S(2)}, u32[]{:S(2)}) %collective-permute-start.41) | collective-permute-done | bytes 8224 | tf_op jit(solution)/shard_map/ppermute | solution.py:50
  148.1 0.6 add.9
  148.8 1.6 %grads.1 = bf16[256,2048]{1,0:T(8,128)(2,1)} custom-call(s32[8]{0:T(128)S(1)} %copy-done.6, bf16[256,2048]{1,0:T(8,128)(2,1)S(1)} %get-tuple-element.143.own_ref, bf16[256,2048]{1,0:T(8,128)(2,1)S(1)} %get-tuple-element.150.oth_ref, bf16[64,2048]{1,0:T(8,128)(2,1)S(1)} %get-tuple-element.165.refs_0_, bf16[64,2048]{1,0:T(8,128)(2,1)S(1)} %collective-permute-done.37.refs_1_, ...), custom_call_target="tpu_custom_call" | custom-call | bytes 2000000 | tf_op jit(solution)/shard_map/grads/pallas_call | solution.py:459
  (80 shorter events, 1.1 us)
Async XLA Ops:
  0.6 3.0 %copy-start = (bf16[1,256,2048]{2,1,0:T(8,128)(2,1)S(1)}, bf16[1,256,2048]{2,1,0:T(8,128)(2,1)}, u32[]{:S(2)}) copy-start(bf16[1,256,2048]{2,1,0:T(8,128)(2,1)} %param.5) | copy-start | bytes 3145732
  0.6 1.1 copy-start.4
  1.9 1.6 %collective-permute-start = (bf16[64,2048]{1,0:T(8,128)(2,1)S(1)}, bf16[64,2048]{1,0:T(8,128)(2,1)S(1)}, u32[]{:S(2)}, u32[]{:S(2)}) collective-permute-start(bf16[64,2048]{1,0:T(8,128)(2,1)S(1)} %get-tuple-element.86), channel_id=1, source_target_pairs={{0,1},{1,0},{2,3},{3,2},{4,5},{5,4},{6,7},{7,6},{8,9},{9,8},{10,11... | collective-permute-start | bytes 786440 | tf_op jit(solution)/shard_map/ppermute | solution.py:42
  3.6 1.2 copy-start.1
  5.0 17.8 %collective-permute-start.2 = (bf16[256,2048]{1,0:T(8,128)(2,1)S(1)}, bf16[256,2048]{1,0:T(8,128)(2,1)S(1)}, u32[]{:S(2)}, u32[]{:S(2)}) collective-permute-start(bf16[256,2048]{1,0:T(8,128)(2,1)S(1)} %give.1), channel_id=1, source_target_pairs={{0,1},{1,0},{2,3},{3,2},{4,5},{5,4},{6,7},{7,6},{8,9},{9,8},{10,11... | collective-permute-start | bytes 3145736 | tf_op jit(solution)/shard_map/ppermute | solution.py:42
  5.2 17.6 %collective-permute-start.1 = (bf16[128,2048]{1,0:T(8,128)(2,1)S(1)}, bf16[128,2048]{1,0:T(8,128)(2,1)S(1)}, u32[]{:S(2)}, u32[]{:S(2)}) collective-permute-start(bf16[128,2048]{1,0:T(8,128)(2,1)S(1)} %unit.1.token_ref.refs_0_), channel_id=1, source_target_pairs={{0,14},{1,15},{2,0},{3,1},{4,2},{5,3},{6,4},{7,5},{8,6},{9,7},{10,... | collective-permute-start | bytes 1572872 | tf_op jit(solution)/shard_map/ppermute | solution.py:42
  11.0 15.4 %collective-permute-start.3 = (bf16[128,2048]{1,0:T(8,128)(2,1)S(1)}, bf16[128,2048]{1,0:T(8,128)(2,1)S(1)}, u32[]{:S(2)}, u32[]{:S(2)}) collective-permute-start(bf16[128,2048]{1,0:T(8,128)(2,1)S(1)} %unit.1.token_ref.refs_0_), channel_id=1, source_target_pairs={{0,2},{1,3},{2,4},{3,5},{4,6},{5,7},{6,8},{7,9},{8,10},{9,11},{10,... | collective-permute-start | bytes 1572872 | tf_op jit(solution)/shard_map/ppermute | solution.py:42
  11.1 15.5 %collective-permute-start.5 = (bf16[128,2048]{1,0:T(8,128)(2,1)S(1)}, bf16[128,2048]{1,0:T(8,128)(2,1)S(1)}, u32[]{:S(2)}, u32[]{:S(2)}) collective-permute-start(bf16[128,2048]{1,0:T(8,128)(2,1)S(1)} %half.1), channel_id=1, source_target_pairs={{0,64},{32,96},{64,0},{96,32},{128,192},{160,224},{192,128},{224,1... | collective-permute-start | bytes 1572872 | tf_op jit(solution)/shard_map/ppermute | solution.py:50
  14.4 15.4 %collective-permute-start.4 = (bf16[128,2048]{1,0:T(8,128)(2,1)S(1)}, bf16[128,2048]{1,0:T(8,128)(2,1)S(1)}, u32[]{:S(2)}, u32[]{:S(2)}) collective-permute-start(bf16[128,2048]{1,0:T(8,128)(2,1)S(1)} %unit.1.token_ref.refs_0_), channel_id=1, source_target_pairs={{0,16},{1,17},{2,18},{3,19},{4,20},{5,21},{6,22},{7,23},{8,24},{9,... | collective-permute-start | bytes 1572872 | tf_op jit(solution)/shard_map/ppermute | solution.py:42
  22.8 3.9 %copy-start.6 = (s32[8]{0:T(128)S(1)}, s32[8]{0:T(128)}, u32[]{:S(2)}) copy-start(s32[8]{0:T(128)} %map_ref.11) | copy-start | bytes 100
  22.8 14.6 %collective-permute-start.6 = (bf16[128,2048]{1,0:T(8,128)(2,1)S(1)}, bf16[128,2048]{1,0:T(8,128)(2,1)S(1)}, u32[]{:S(2)}, u32[]{:S(2)}) collective-permute-start(bf16[128,2048]{1,0:T(8,128)(2,1)S(1)} %get-tuple-element.88.refs_1_), channel_id=1, source_target_pairs={{0,14},{1,15},{2,0},{3,1},{4,2},{5,3},{6,4},{7,5},{8,6},{9,7},{10,... | collective-permute-start | bytes 1572872 | tf_op jit(solution)/shard_map/ppermute | solution.py:42
  26.5 14.6 %collective-permute-start.8 = (bf16[128,2048]{1,0:T(8,128)(2,1)S(1)}, bf16[128,2048]{1,0:T(8,128)(2,1)S(1)}, u32[]{:S(2)}, u32[]{:S(2)}) collective-permute-start(bf16[128,2048]{1,0:T(8,128)(2,1)S(1)} %get-tuple-element.90.refs_2_), channel_id=1, source_target_pairs={{0,2},{1,3},{2,4},{3,5},{4,6},{5,7},{6,8},{7,9},{8,10},{9,11},{10,... | collective-permute-start | bytes 1572872 | tf_op jit(solution)/shard_map/ppermute | solution.py:42
  27.2 7.5 %collective-permute-start.7 = (bf16[64,2048]{1,0:T(8,128)(2,1)S(1)}, bf16[64,2048]{1,0:T(8,128)(2,1)S(1)}, u32[]{:S(2)}, u32[]{:S(2)}) collective-permute-start(bf16[64,2048]{1,0:T(8,128)(2,1)S(1)} %get-tuple-element.95), channel_id=1, source_target_pairs={{0,32},{32,0},{64,96},{96,64},{128,160},{160,128},{192,224},{224,1... | collective-permute-start | bytes 786440 | tf_op jit(solution)/shard_map/ppermute | solution.py:50
  28.9 14.2 %collective-permute-start.9 = (bf16[128,2048]{1,0:T(8,128)(2,1)S(1)}, bf16[128,2048]{1,0:T(8,128)(2,1)S(1)}, u32[]{:S(2)}, u32[]{:S(2)}) collective-permute-start(bf16[128,2048]{1,0:T(8,128)(2,1)S(1)} %get-tuple-element.88.refs_1_), channel_id=1, source_target_pairs={{0,16},{1,17},{2,18},{3,19},{4,20},{5,21},{6,22},{7,23},{8,24},{9,... | collective-permute-start | bytes 1572872 | tf_op jit(solution)/shard_map/ppermute | solution.py:42
  37.4 17.4 %collective-permute-start.10 = (bf16[128,2048]{1,0:T(8,128)(2,1)S(1)}, bf16[128,2048]{1,0:T(8,128)(2,1)S(1)}, u32[]{:S(2)}, u32[]{:S(2)}) collective-permute-start(bf16[128,2048]{1,0:T(8,128)(2,1)S(1)} %get-tuple-element.98.refs_4_), channel_id=1, source_target_pairs={{0,14},{1,15},{2,0},{3,1},{4,2},{5,3},{6,4},{7,5},{8,6},{9,7},{10,... | collective-permute-start | bytes 1572872 | tf_op jit(solution)/shard_map/ppermute | solution.py:42
  41.1 13.7 %collective-permute-start.12 = (bf16[128,2048]{1,0:T(8,128)(2,1)S(1)}, bf16[128,2048]{1,0:T(8,128)(2,1)S(1)}, u32[]{:S(2)}, u32[]{:S(2)}) collective-permute-start(bf16[128,2048]{1,0:T(8,128)(2,1)S(1)} %get-tuple-element.100.refs_5_), channel_id=1, source_target_pairs={{0,2},{1,3},{2,4},{3,5},{4,6},{5,7},{6,8},{7,9},{8,10},{9,11},{10,... | collective-permute-start | bytes 1572872 | tf_op jit(solution)/shard_map/ppermute | solution.py:42
  41.6 10.8 %collective-permute-start.11 = (bf16[64,2048]{1,0:T(8,128)(2,1)S(1)}, bf16[64,2048]{1,0:T(8,128)(2,1)S(1)}, u32[]{:S(2)}, u32[]{:S(2)}) collective-permute-start(bf16[64,2048]{1,0:T(8,128)(2,1)S(1)} %select.4.own_ref), channel_id=1, source_target_pairs={{0,128},{32,160},{64,192},{96,224},{128,0},{160,32},{192,64},{224,... | collective-permute-start | bytes 786440 | tf_op jit(solution)/shard_map/ppermute | solution.py:50
  43.1 18.0 %collective-permute-start.13 = (bf16[128,2048]{1,0:T(8,128)(2,1)S(1)}, bf16[128,2048]{1,0:T(8,128)(2,1)S(1)}, u32[]{:S(2)}, u32[]{:S(2)}) collective-permute-start(bf16[128,2048]{1,0:T(8,128)(2,1)S(1)} %get-tuple-element.100.refs_5_), channel_id=1, source_target_pairs={{0,16},{1,17},{2,18},{3,19},{4,20},{5,21},{6,22},{7,23},{8,24},{9,... | collective-permute-start | bytes 1572872 | tf_op jit(solution)/shard_map/ppermute | solution.py:42
  53.1 8.1 %collective-permute-start.15 = (bf16[64,2048]{1,0:T(8,128)(2,1)S(1)}, bf16[64,2048]{1,0:T(8,128)(2,1)S(1)}, u32[]{:S(2)}, u32[]{:S(2)}) collective-permute-start(bf16[64,2048]{1,0:T(8,128)(2,1)S(1)} %select.5.refs_0_), channel_id=1, source_target_pairs={{0,32},{32,0},{64,96},{96,64},{128,160},{160,128},{192,224},{224,1... | collective-permute-start | bytes 786440 | tf_op jit(solution)/shard_map/ppermute | solution.py:50
  54.7 15.9 %collective-permute-start.14 = (bf16[128,2048]{1,0:T(8,128)(2,1)S(1)}, bf16[128,2048]{1,0:T(8,128)(2,1)S(1)}, u32[]{:S(2)}, u32[]{:S(2)}) collective-permute-start(bf16[128,2048]{1,0:T(8,128)(2,1)S(1)} %get-tuple-element.109.refs_8_), channel_id=1, source_target_pairs={{0,2},{1,3},{2,4},{3,5},{4,6},{5,7},{6,8},{7,9},{8,10},{9,11},{10,... | collective-permute-start | bytes 1572872 | tf_op jit(solution)/shard_map/ppermute | solution.py:42
  54.8 15.8 %collective-permute-start.16 = (bf16[128,2048]{1,0:T(8,128)(2,1)S(1)}, bf16[128,2048]{1,0:T(8,128)(2,1)S(1)}, u32[]{:S(2)}, u32[]{:S(2)}) collective-permute-start(bf16[128,2048]{1,0:T(8,128)(2,1)S(1)} %get-tuple-element.102.refs_6_), channel_id=1, source_target_pairs={{0,14},{1,15},{2,0},{3,1},{4,2},{5,3},{6,4},{7,5},{8,6},{9,7},{10,... | collective-permute-start | bytes 1572872 | tf_op jit(solution)/shard_map/ppermute | solution.py:42
  58.1 14.2 %collective-permute-start.17 = (bf16[128,2048]{1,0:T(8,128)(2,1)S(1)}, bf16[128,2048]{1,0:T(8,128)(2,1)S(1)}, u32[]{:S(2)}, u32[]{:S(2)}) collective-permute-start(bf16[128,2048]{1,0:T(8,128)(2,1)S(1)} %get-tuple-element.109.refs_8_), channel_id=1, source_target_pairs={{0,16},{1,17},{2,18},{3,19},{4,20},{5,21},{6,22},{7,23},{8,24},{9,... | collective-permute-start | bytes 1572872 | tf_op jit(solution)/shard_map/ppermute | solution.py:42
  61.2 12.0 %collective-permute-start.19 = (bf16[128,2048]{1,0:T(8,128)(2,1)S(1)}, bf16[128,2048]{1,0:T(8,128)(2,1)S(1)}, u32[]{:S(2)}, u32[]{:S(2)}) collective-permute-start(bf16[128,2048]{1,0:T(8,128)(2,1)S(1)} %stack.1.refs_0_.a_ref.refs_20_), channel_id=1, source_target_pairs={{0,64},{32,96},{64,0},{96,32},{128,192},{160,224},{192,128},{224,1... | collective-permute-start | bytes 1572872 | tf_op jit(solution)/shard_map/ppermute | solution.py:50
  64.5 15.5 %collective-permute-start.20 = (bf16[128,2048]{1,0:T(8,128)(2,1)S(1)}, bf16[128,2048]{1,0:T(8,128)(2,1)S(1)}, u32[]{:S(2)}, u32[]{:S(2)}) collective-permute-start(bf16[128,2048]{1,0:T(8,128)(2,1)S(1)} %get-tuple-element.93.refs_3_), channel_id=1, source_target_pairs={{0,2},{1,3},{2,4},{3,5},{4,6},{5,7},{6,8},{7,9},{8,10},{9,11},{10,... | collective-permute-start | bytes 1572872 | tf_op jit(solution)/shard_map/ppermute | solution.py:42
  70.7 3.2 %copy-start.5 = (f32[2048]{0:T(1024)S(1)}, f32[2048]{0:T(1024)}, u32[]{:S(2)}) copy-start(f32[2048]{0:T(1024)} %param.8) | copy-start | bytes 24580
  70.7 9.3 %collective-permute-start.18 = (bf16[128,2048]{1,0:T(8,128)(2,1)S(1)}, bf16[128,2048]{1,0:T(8,128)(2,1)S(1)}, u32[]{:S(2)}, u32[]{:S(2)}) collective-permute-start(bf16[128,2048]{1,0:T(8,128)(2,1)S(1)} %get-tuple-element.117.refs_11_), channel_id=1, source_target_pairs={{0,14},{1,15},{2,0},{3,1},{4,2},{5,3},{6,4},{7,5},{8,6},{9,7},{10,... | collective-permute-start | bytes 1572872 | tf_op jit(solution)/shard_map/ppermute | solution.py:42
  70.8 10.6 %collective-permute-start.21 = (bf16[128,2048]{1,0:T(8,128)(2,1)S(1)}, bf16[128,2048]{1,0:T(8,128)(2,1)S(1)}, u32[]{:S(2)}, u32[]{:S(2)}) collective-permute-start(bf16[128,2048]{1,0:T(8,128)(2,1)S(1)} %get-tuple-element.115.refs_10_), channel_id=1, source_target_pairs={{0,16},{1,17},{2,18},{3,19},{4,20},{5,21},{6,22},{7,23},{8,24},{9,... | collective-permute-start | bytes 1572872 | tf_op jit(solution)/shard_map/ppermute | solution.py:42
  73.2 1.4 copy-start.2
  73.3 8.1 %collective-permute-start.22 = (bf16[128,2048]{1,0:T(8,128)(2,1)S(1)}, bf16[128,2048]{1,0:T(8,128)(2,1)S(1)}, u32[]{:S(2)}, u32[]{:S(2)}) collective-permute-start(bf16[128,2048]{1,0:T(8,128)(2,1)S(1)} %late.1), channel_id=1, source_target_pairs={{0,1},{1,0},{2,3},{3,2},{4,5},{5,4},{6,7},{7,6},{8,9},{9,8},{10,11... | collective-permute-start | bytes 1572872 | tf_op jit(solution)/shard_map/ppermute | solution.py:42
  73.4 8.0 %collective-permute-start.23 = (bf16[128,2048]{1,0:T(8,128)(2,1)S(1)}, bf16[128,2048]{1,0:T(8,128)(2,1)S(1)}, u32[]{:S(2)}, u32[]{:S(2)}) collective-permute-start(bf16[128,2048]{1,0:T(8,128)(2,1)S(1)} %get-tuple-element.128.refs_1_.b_ref.refs_21_), channel_id=1, source_target_pairs={{0,1},{1,0},{2,3},{3,2},{4,5},{5,4},{6,7},{7,6},{8,9},{9,8},{10,11... | collective-permute-start | bytes 1572872 | tf_op jit(solution)/shard_map/ppermute | solution.py:42
  96.8 3.1 %collective-permute-start.24 = (bf16[272,2048]{1,0:T(8,128)(2,1)S(1)}, bf16[272,2048]{1,0:T(8,128)(2,1)S(1)}, u32[]{:S(2)}, u32[]{:S(2)}) collective-permute-start(bf16[272,2048]{1,0:T(8,128)(2,1)S(1)} %get-tuple-element.146), channel_id=1, source_target_pairs={{0,1},{1,0},{2,3},{3,2},{4,5},{5,4},{6,7},{7,6},{8,9},{9,8},{10,11... | collective-permute-start | bytes 3342344 | tf_op jit(solution)/shard_map/ppermute | solution.py:42
  97.1 7.8 %collective-permute-start.25 = (bf16[256,2048]{1,0:T(8,128)(2,1)S(1)}, bf16[256,2048]{1,0:T(8,128)(2,1)S(1)}, u32[]{:S(2)}, u32[]{:S(2)}) collective-permute-start(bf16[256,2048]{1,0:T(8,128)(2,1)S(1)} %get-tuple-element.148), channel_id=1, source_target_pairs={{0,1},{1,0},{2,3},{3,2},{4,5},{5,4},{6,7},{7,6},{8,9},{9,8},{10,11... | collective-permute-start | bytes 3145736 | tf_op jit(solution)/shard_map/ppermute | solution.py:42
  100.2 22.7 %collective-permute-start.26 = (bf16[64,2048]{1,0:T(8,128)(2,1)S(1)}, bf16[64,2048]{1,0:T(8,128)(2,1)S(1)}, u32[]{:S(2)}, u32[]{:S(2)}) collective-permute-start(bf16[64,2048]{1,0:T(8,128)(2,1)S(1)} %get-tuple-element.153), channel_id=1, source_target_pairs={{0,32},{32,0},{64,96},{96,64},{128,160},{160,128},{192,224},{224,1... | collective-permute-start | bytes 786440 | tf_op jit(solution)/shard_map/ppermute | solution.py:50
  101.8 21.0 %collective-permute-start.27 = (bf16[64,2048]{1,0:T(8,128)(2,1)S(1)}, bf16[64,2048]{1,0:T(8,128)(2,1)S(1)}, u32[]{:S(2)}, u32[]{:S(2)}) collective-permute-start(bf16[64,2048]{1,0:T(8,128)(2,1)S(1)} %get-tuple-element.154), channel_id=1, source_target_pairs={{0,64},{32,96},{64,0},{96,32},{128,192},{160,224},{192,128},{224,1... | collective-permute-start | bytes 786440 | tf_op jit(solution)/shard_map/ppermute | solution.py:50
  104.7 18.1 %collective-permute-start.28 = (bf16[64,2048]{1,0:T(8,128)(2,1)S(1)}, bf16[64,2048]{1,0:T(8,128)(2,1)S(1)}, u32[]{:S(2)}, u32[]{:S(2)}) collective-permute-start(bf16[64,2048]{1,0:T(8,128)(2,1)S(1)} %get-tuple-element.155), channel_id=1, source_target_pairs={{0,96},{32,64},{64,32},{96,0},{128,224},{160,192},{192,160},{224,1... | collective-permute-start | bytes 786440 | tf_op jit(solution)/shard_map/ppermute | solution.py:50
  105.0 5.4 %collective-permute-start.31 = (f32[1,2048]{1,0:T(1,128)S(1)}, f32[1,2048]{1,0:T(1,128)S(1)}, u32[]{:S(2)}, u32[]{:S(2)}) collective-permute-start(f32[1,2048]{1,0:T(1,128)S(1)} %get-tuple-element.156.a_ref), channel_id=1, source_target_pairs={{0,6},{1,7},{2,4},{3,5},{4,2},{5,3},{6,0},{7,1},{8,14},{9,15},{10,... | collective-permute-start | bytes 24584 | tf_op jit(solution)/shard_map/ppermute | solution.py:42
  107.3 4.5 %collective-permute-start.30 = (f32[1,2048]{1,0:T(1,128)S(1)}, f32[1,2048]{1,0:T(1,128)S(1)}, u32[]{:S(2)}, u32[]{:S(2)}) collective-permute-start(f32[1,2048]{1,0:T(1,128)S(1)} %get-tuple-element.156.a_ref), channel_id=1, source_target_pairs={{0,4},{1,5},{2,6},{3,7},{4,0},{5,1},{6,2},{7,3},{8,12},{9,13},{10,... | collective-permute-start | bytes 24584 | tf_op jit(solution)/shard_map/ppermute | solution.py:42
  110.4 3.7 %collective-permute-start.29 = (f32[1,2048]{1,0:T(1,128)S(1)}, f32[1,2048]{1,0:T(1,128)S(1)}, u32[]{:S(2)}, u32[]{:S(2)}) collective-permute-start(f32[1,2048]{1,0:T(1,128)S(1)} %get-tuple-element.156.a_ref), channel_id=1, source_target_pairs={{0,2},{1,3},{2,0},{3,1},{4,6},{5,7},{6,4},{7,5},{8,10},{9,11},{10,... | collective-permute-start | bytes 24584 | tf_op jit(solution)/shard_map/ppermute | solution.py:42
  114.1 7.6 %collective-permute-start.32 = (f32[1,2048]{1,0:T(1,128)S(1)}, f32[1,2048]{1,0:T(1,128)S(1)}, u32[]{:S(2)}, u32[]{:S(2)}) collective-permute-start(f32[1,2048]{1,0:T(1,128)S(1)} %add.5.a_ref), channel_id=1, source_target_pairs={{0,8},{1,9},{2,10},{3,11},{4,12},{5,13},{6,14},{7,15},{8,0},{9,1},... | collective-permute-start | bytes 24584 | tf_op jit(solution)/shard_map/ppermute | solution.py:42
  121.6 1.2 copy-start.3
  123.0 12.1 %collective-permute-start.33 = (bf16[64,2048]{1,0:T(8,128)(2,1)S(1)}, bf16[64,2048]{1,0:T(8,128)(2,1)S(1)}, u32[]{:S(2)}, u32[]{:S(2)}) collective-permute-start(bf16[64,2048]{1,0:T(8,128)(2,1)S(1)} %get-tuple-element.163), channel_id=1, source_target_pairs={{0,128},{32,160},{64,192},{96,224},{128,0},{160,32},{192,64},{224,... | collective-permute-start | bytes 786440 | tf_op jit(solution)/shard_map/ppermute | solution.py:50
  126.7 4.9 %collective-permute-start.36 = (f32[1,2048]{1,0:T(1,128)S(1)}, f32[1,2048]{1,0:T(1,128)S(1)}, u32[]{:S(2)}, u32[]{:S(2)}) collective-permute-start(f32[1,2048]{1,0:T(1,128)S(1)} %get-tuple-element.164.a_ref), channel_id=1, source_target_pairs={{0,96},{32,64},{64,32},{96,0},{128,224},{160,192},{192,160},{224,1... | collective-permute-start | bytes 24584 | tf_op jit(solution)/shard_map/ppermute | solution.py:50
  129.8 5.3 %collective-permute-start.35 = (f32[1,2048]{1,0:T(1,128)S(1)}, f32[1,2048]{1,0:T(1,128)S(1)}, u32[]{:S(2)}, u32[]{:S(2)}) collective-permute-start(f32[1,2048]{1,0:T(1,128)S(1)} %get-tuple-element.164.a_ref), channel_id=1, source_target_pairs={{0,64},{32,96},{64,0},{96,32},{128,192},{160,224},{192,128},{224,1... | collective-permute-start | bytes 24584 | tf_op jit(solution)/shard_map/ppermute | solution.py:50
  129.8 5.3 %collective-permute-start.34 = (f32[1,2048]{1,0:T(1,128)S(1)}, f32[1,2048]{1,0:T(1,128)S(1)}, u32[]{:S(2)}, u32[]{:S(2)}) collective-permute-start(f32[1,2048]{1,0:T(1,128)S(1)} %get-tuple-element.164.a_ref), channel_id=1, source_target_pairs={{0,32},{32,0},{64,96},{96,64},{128,160},{160,128},{192,224},{224,1... | collective-permute-start | bytes 24584 | tf_op jit(solution)/shard_map/ppermute | solution.py:50
  135.1 13.6 %collective-permute-start.39 = (bf16[64,2048]{1,0:T(8,128)(2,1)S(1)}, bf16[64,2048]{1,0:T(8,128)(2,1)S(1)}, u32[]{:S(2)}, u32[]{:S(2)}) collective-permute-start(bf16[64,2048]{1,0:T(8,128)(2,1)S(1)} %get-tuple-element.165.refs_0_), channel_id=1, source_target_pairs={{0,96},{32,64},{64,32},{96,0},{128,224},{160,192},{192,160},{224,1... | collective-permute-start | bytes 786440 | tf_op jit(solution)/shard_map/ppermute | solution.py:50
  135.9 12.8 %collective-permute-start.38 = (bf16[64,2048]{1,0:T(8,128)(2,1)S(1)}, bf16[64,2048]{1,0:T(8,128)(2,1)S(1)}, u32[]{:S(2)}, u32[]{:S(2)}) collective-permute-start(bf16[64,2048]{1,0:T(8,128)(2,1)S(1)} %get-tuple-element.165.refs_0_), channel_id=1, source_target_pairs={{0,64},{32,96},{64,0},{96,32},{128,192},{160,224},{192,128},{224,1... | collective-permute-start | bytes 786440 | tf_op jit(solution)/shard_map/ppermute | solution.py:50
  137.3 11.5 %collective-permute-start.37 = (bf16[64,2048]{1,0:T(8,128)(2,1)S(1)}, bf16[64,2048]{1,0:T(8,128)(2,1)S(1)}, u32[]{:S(2)}, u32[]{:S(2)}) collective-permute-start(bf16[64,2048]{1,0:T(8,128)(2,1)S(1)} %get-tuple-element.165.refs_0_), channel_id=1, source_target_pairs={{0,32},{32,0},{64,96},{96,64},{128,160},{160,128},{192,224},{224,1... | collective-permute-start | bytes 786440 | tf_op jit(solution)/shard_map/ppermute | solution.py:50
  139.3 3.7 %collective-permute-start.40 = (f32[1,2048]{1,0:T(1,128)S(1)}, f32[1,2048]{1,0:T(1,128)S(1)}, u32[]{:S(2)}, u32[]{:S(2)}) collective-permute-start(f32[1,2048]{1,0:T(1,128)S(1)} %get-tuple-element.166.a_ref), channel_id=1, source_target_pairs={{0,16},{1,17},{2,18},{3,19},{4,20},{5,21},{6,22},{7,23},{8,24},{9,... | collective-permute-start | bytes 24584 | tf_op jit(solution)/shard_map/ppermute | solution.py:42
  143.0 5.2 %collective-permute-start.41 = (f32[1,2048]{1,0:T(1,128)S(1)}, f32[1,2048]{1,0:T(1,128)S(1)}, u32[]{:S(2)}, u32[]{:S(2)}) collective-permute-start(f32[1,2048]{1,0:T(1,128)S(1)} %add.8.a_ref), channel_id=1, source_target_pairs={{0,128},{32,160},{64,192},{96,224},{128,0},{160,32},{192,64},{224,... | collective-permute-start | bytes 24584 | tf_op jit(solution)/shard_map/ppermute | solution.py:50

commit v4 on v2

--- a/solution.py
+++ b/solution.py
@@ -15,6 +15,7 @@
 F = HALF * HEAD
 QUARTER = LEN // 4
 PIECE = LEN // 2
+NORM = 32
 
 eps = 1e-06
 bf16 = jnp.bfloat16
@@ -160,8 +161,12 @@
     ], sems)
 
 
-def butterfly_kernel(a_ref, b_ref, c_ref, d_ref, out_ref):
-    out_ref[...] = (a_ref[...] + b_ref[...]) + (c_ref[...] + d_ref[...])
+def butterfly_kernel(*refs):
+    *parts, out_ref = refs
+    parts = [ref[...] for ref in parts]
+    while len(parts) > 1:
+        parts = [parts[i] + parts[i + 1] for i in range(0, len(parts), 2)]
+    out_ref[...] = parts[0]
 
 
 def select_kernel(step, map_ref, own_ref, got_ref, *outs):
@@ -189,6 +194,39 @@
     out_ref[...] = a_ref[...]
 
 
+def butterfly_kernel(*refs):
+    *parts, out_ref = refs
+    parts = [ref[...] for ref in parts]
+    while len(parts) > 1:
+        parts = [parts[i] + parts[i + 1] for i in range(0, len(parts), 2)]
+    out_ref[...] = parts[0]
+
+
+def select_kernel(step, map_ref, own_ref, got_ref, *outs):
+    y, root = y_index(), root_of(map_ref)
+    if step == 0:
+        mine = y // 2 == root % 4 // 2
+        keep_ref, send_ref = outs
+        for ref, quarter in ((keep_ref, y), (send_ref, y ^ 1)):
+            ref[...] = jnp.where(mine, own_ref[row_block(quarter, QUARTER), :], got_ref[row_block(quarter % 2, QUARTER), :])
+    elif step == 1:
+        outs[0][...] = jnp.where(y % 2 == root % 2, own_ref[...], got_ref[...])
+    else:
+        outs[0][...] = jnp.where(lax.axis_index("section") // 4 == root // 4, own_ref[...], got_ref[...])
+
+
+def stack_kernel(*refs):
+    *parts, out_ref = refs
+    rows = out_ref.shape[0] // len(parts)
+    for index, part in enumerate(parts):
+        out_ref[index * rows:(index + 1) * rows, :] = part[...]
+
+
+def late_kernel(a_ref, token_ref, out_ref):
+    del token_ref
+    out_ref[...] = a_ref[...]
+
+
 def add_kernel(a_ref, b_ref, out_ref):
     out_ref[...] = a_ref[...] + b_ref[...]
 
@@ -201,12 +239,12 @@
 
 
 def norm_block(ref, gain_ref, enc_ref, inv_ref):
-    @pl.loop(0, PIECE // QUARTER)
+    @pl.loop(0, PIECE // NORM)
     def _(block):
-        rows = row_block(block, QUARTER)
+        rows = row_block(block, NORM)
         hidden = ref[rows, :].astype(f32)
         inv = lax.rsqrt(jnp.mean(hidden * hidden, axis=1, keepdims=True) + eps)
-        inv_ref[rows, :] = jnp.broadcast_to(inv, (QUARTER, 128))
+        inv_ref[rows, :] = jnp.broadcast_to(inv, (NORM, 128))
         for slot in range(N_SLOT):
             cols = pl.ds(slot_column(*SLOTS[slot]), SLOT)
             part = ref[rows, cols].astype(f32)
@@ -219,7 +257,9 @@
         norm_block(refs[index], gain_ref, refs[count + 2 * index], refs[count + 2 * index + 1])
 
 
-def encoder_kernel(map_ref, gain_ref, cot_ref, a_ref, b_ref, dh_ref, gp_ref, full_ref):
+def encoder_kernel(map_ref, gain_ref, cot_ref, a_ref, b_ref, dh_ref, gp_ref, full_ref, flag_ref):
+    flag_ref[...] = jnp.where(is_encoder(map_ref), 1.0, 0.0) * jnp.ones_like(flag_ref)
+
     @pl.when(is_encoder(map_ref))
     def _():
         y = y_index()
@@ -227,13 +267,14 @@
         gp_ref[...] = jnp.zeros_like(gp_ref)
         for index, ref in enumerate((a_ref, b_ref)):
 
-            @pl.loop(0, PIECE // QUARTER)
+            @pl.loop(0, PIECE // NORM)
             def _(block):
-                quarter = index * (PIECE // QUARTER) + block
-                rows = row_block(quarter, QUARTER)
-                place = row_block(y ^ quarter, QUARTER)
+                part = QUARTER // NORM
+                quarter = index * (PIECE // QUARTER) + block // part
+                rows = row_block(index * (PIECE // NORM) + block, NORM)
+                place = row_block((y ^ quarter) * part + block % part, NORM)
                 g = cot_ref[place, :].astype(f32)
-                hidden = ref[row_block(block, QUARTER), :].astype(f32)
+                hidden = ref[row_block(block, NORM), :].astype(f32)
                 inv = lax.rsqrt(jnp.mean(hidden * hidden, axis=1, keepdims=True) + eps)
                 full_ref[place, :] = (hidden * inv * gain).astype(bf16)
                 mean = jnp.mean(hidden * gain * g, axis=1, keepdims=True)
@@ -404,12 +445,14 @@
     dh_ref[...] = (sum_ref[...] + got_ref[...].astype(f32)).astype(bf16)
 
 
-def out_kernel(offset, map_ref, own_ref, oth_ref, *refs):
+def out_kernel(offset, flag_ref, own_ref, oth_ref, *refs):
     *parts, out_ref, sems = refs
     core, y = core_index(), y_index()
     rows = LEN // len(parts)
 
-    @pl.when(jnp.logical_not(is_encoder(map_ref)))
+    encoder = jnp.max(flag_ref[...]) > 0.5
+
+    @pl.when(jnp.logical_not(encoder))
     def _():
         copies = [
             pltpu.make_async_copy(
@@ -424,7 +467,7 @@
         for copy in copies:
             copy.wait()
 
-    @pl.when(is_encoder(map_ref))
+    @pl.when(encoder)
     def _():
         copies = []
         for index, part in enumerate(parts):
@@ -441,7 +484,7 @@
 def put_out(offset, where, own, oth, parts, name):
     return pl.pallas_call(
         functools.partial(out_kernel, offset),
-        in_specs=[SMEM] + [ANY] * (2 + len(parts)),
+        in_specs=[VMEM] + [ANY] * (2 + len(parts)),
         out_specs=ANY,
         out_shape=jax.ShapeDtypeStruct((LEN, D), bf16),
         scratch_shapes=[pltpu.SemaphoreType.DMA((4,))],
@@ -472,15 +515,14 @@
     up, down, across = from_above(a[0]), from_below(a[0]), other_column(a[0])
     qg_oth = other_core(copy_call(give_kernel, bf16_rows(LEN), (rows, cot, a[0]), "give", 2))
 
+    a[1], qg_oth = order.take(up, qg_oth)
+    up, across_1 = from_above(a[1]), other_column(a[1])
+    a[-1] = order.take(down)
+    down = from_below(a[-1])
     hidden = order.take(hidden)
     mine, send = select(0, rows, hidden)
     hidden = other_y(send, 1)
-
-    a[1] = order.take(up)
-    up, across_1 = from_above(a[1]), other_column(a[1])
-    a[-1] = order.take(down)
-    down = from_below(a[-1])
-    b[0], qg_oth = order.take(across, qg_oth)
+    b[0] = order.take(across)
     hidden = order.take(hidden)
     mine = select(1, mine, hidden)
     hidden = other_high(mine)
@@ -523,8 +565,8 @@
 
     enc_0, inv_0, enc_1, inv_1 = normalise(own_a, own_b)
     enc_2, inv_2, enc_3, inv_3 = normalise(oth_a, oth_b)
-    dh_enc, gp_enc, enc_out = small_call(
-        encoder_kernel, [bf16_rows(LEN), LINE, bf16_rows(LEN)], (gain, cot, own_a, own_b), "encoder",
+    dh_enc, gp_enc, enc_out, flag = small_call(
+        encoder_kernel, [bf16_rows(LEN), LINE, bf16_rows(LEN), jax.ShapeDtypeStruct((8, 128), f32)], (gain, cot, own_a, own_b), "encoder",
         where=section_map,
     )
     pieces = (enc_0, enc_1, enc_2, enc_3, own_a, own_b, oth_a, oth_b, inv_0, inv_1, inv_2, inv_3)
@@ -532,11 +574,6 @@
         units, pieces, section_map, rows, cot, qg_oth, gain, dh_enc, gp_enc
     )
 
-    def add_from(part, *moves):
-        for move in moves:
-            part = small_call(add_kernel, LINE, (part, move(part)), "add", limit=1)
-        return part
-
     def butterfly(part, *moves):
         return small_call(butterfly_kernel, LINE, (part, *[move(part) for move in moves]), "add", limit=1)
 
@@ -548,8 +585,7 @@
     )
     far, near, other = other_y(parts[1], 2), other_y(parts[0], 1), other_y(parts[2], 3)
     gain_part, got_out = order.take(gain_part, other_core(oth_out))
-    gain_part = butterfly(gain_part, *[z_move(bits) for bits in (1, 2, 3)])
-    gain_part = add_from(gain_part, z_move(4))
+    gain_part = butterfly(gain_part, *[z_move(bits) for bits in range(1, 8)])
     near, far, other, gain_part = order.take(near, far, other, gain_part)
     kept, sent, gain_part = small_call(
         sum_kernel, [ROWS32, quarter, LINE], (kept, gain_part, near, far, other), "sum"
@@ -558,11 +594,10 @@
     gain_part = butterfly(gain_part, *[lambda v, bits=bits: other_y(v, bits) for bits in (1, 2, 3)])
     dh, gain_part = small_call(last_kernel, [quarter, LINE], (kept, crossed, gain_part), "last")
     far, near, other = other_y(dh, 2), other_y(dh, 1), other_y(dh, 3)
-    gain_part = add_from(gain_part, other_column)
-    gain_part = add_from(gain_part, other_high)
+    gain_part = butterfly(butterfly(gain_part, other_column), other_high)
     dhs = [dh, near, far, other]
-    section_out = put_out(0, section_map, own_out, got_out, [enc_out], "rows")
-    section_grad = put_out(F, section_map, own_out, got_out, dhs, "grads")
+    section_out = put_out(0, flag, own_out, got_out, [enc_out], "rows")
+    section_grad = put_out(F, flag, own_out, got_out, dhs, "grads")
     return (section_out[None], section_grad[None], gain_part.reshape(D))
 
 

time: 150 us -> 154 us (1.027)
  starting transfers between devices: 50.3 us -> 67.4 us
  waiting for transfers between devices: 71.8 us -> 63.7 us
  Pallas kernels: 23.2 us -> 19.4 us
    ppermute x16, starting transfers between devices: 23.6 us -> 34.2 us  [section_swap(): return lax.ppermute(x, 'section', pairs)]
    ppermute x26 -> x29, starting transfers between devices: 26.7 us -> 33.1 us  [dp_swap(): return lax.ppermute(x, 'dp', pairs)]
    pallas_call x1, Pallas kernels: 14.8 us -> 9.21 us  [attend(): pl.pallas_call(main_kernel, in_specs=[VMEM] * (N_SLOT + 12) + [SMEM] + [V...]
    ppermute x16, waiting for transfers between devices: 27 us -> 22.5 us  [section_swap(): return lax.ppermute(x, 'section', pairs)]
    ppermute x26 -> x29, waiting for transfers between devices: 44.8 us -> 41.1 us  [dp_swap(): return lax.ppermute(x, 'dp', pairs)]
    pallas_call x16 -> x15, Pallas kernels: 4.99 us -> 7.61 us  [small_call(): pl.pallas_call(kernel, in_specs=[SMEM] * len(first) + [VMEM] * len(args),...]
  transfers between devices with their start and end apart: 42 -> 45, of which waited for: 20 -> 23; matrix products, arithmetic and copies ran while one was open for 0% -> 0% of each run, Pallas kernels for 4% -> 5%
where the time goes in v4:
time: 154 us
  starting transfers between devices  67.4 us (44%)
  waiting for transfers between devices  63.7 us (41%)
  Pallas kernels  19.4 us (13%)
  local copies, waits for them, and re-layouts  2.36 us (2%)
    ppermute x29, waiting for transfers between devices, dp_swap(): return lax.ppermute(x, 'dp', pairs)  41.1 us
    ppermute x16, starting transfers between devices, section_swap(): return lax.ppermute(x, 'section', pairs)  34.2 us
    ppermute x29, starting transfers between devices, dp_swap(): return lax.ppermute(x, 'dp', pairs)  33.1 us
    ppermute x16, waiting for transfers between devices, section_swap(): return lax.ppermute(x, 'section', pairs)  22.5 us
    pallas_call x1, Pallas kernels, attend(): pl.pallas_call(main_kernel, in_specs=[VMEM] * (N_SLOT + 12) + [SMEM] + [V...  9.21 us
    pallas_call x15, Pallas kernels, small_call(): pl.pallas_call(kernel, in_specs=[SMEM] * len(first) + [VMEM] * len(args),...  7.61 us
  transfers between devices with their start and end apart: 45, of which 23 were waited for; matrix products, arithmetic and copies ran while one was open for 0% of the time, Pallas kernels for 5%

profile of v4, /device:TPU:6, one launch (start us, length us, event | category | flops | bytes accessed | tf_op | source)
XLA Modules:
  0.0 153.9 jit_solution(12281634983396734067)
XLA Ops:
  0.6 1.1 copy-done.3
  2.0 1.5 collective-permute-done.1.got_ref
  3.6 1.2 copy-done.1
  5.2 5.9 %collective-permute-start.3 = (bf16[128,2048]{1,0:T(8,128)(2,1)S(1)}, bf16[128,2048]{1,0:T(8,128)(2,1)S(1)}, u32[]{:S(2)}, u32[]{:S(2)}) collective-permute-start(bf16[128,2048]{1,0:T(8,128)(2,1)S(1)} %unit.1.token_ref.refs_0_), channel_id=1, source_target_pairs={{0,14},{1,15},{2,0},{3,1},{4,2},{5,3},{6,4},{7,5},{8,6},{9,7},{10,... | collective-permute-start | bytes 1572872 | tf_op jit(solution)/shard_map/ppermute | solution.py:43
  11.1 3.3 %collective-permute-start = (bf16[128,2048]{1,0:T(8,128)(2,1)S(1)}, bf16[128,2048]{1,0:T(8,128)(2,1)S(1)}, u32[]{:S(2)}, u32[]{:S(2)}) collective-permute-start(bf16[128,2048]{1,0:T(8,128)(2,1)S(1)} %half.1), channel_id=1, source_target_pairs={{0,64},{32,96},{64,0},{96,32},{128,192},{160,224},{192,128},{224,1... | collective-permute-start | bytes 1572872 | tf_op jit(solution)/shard_map/ppermute | solution.py:51
  14.4 0.8 collective-permute-start.6
  15.2 7.6 %collective-permute-done.3.refs_0_ = bf16[128,2048]{1,0:T(8,128)(2,1)S(1)} collective-permute-done((bf16[128,2048]{1,0:T(8,128)(2,1)S(1)}, bf16[128,2048]{1,0:T(8,128)(2,1)S(1)}, u32[]{:S(2)}, u32[]{:S(2)}) %collective-permute-start.3) | collective-permute-done | bytes 524320 | tf_op jit(solution)/shard_map/ppermute | solution.py:43
  22.8 3.7 %collective-permute-start.10 = (bf16[128,2048]{1,0:T(8,128)(2,1)S(1)}, bf16[128,2048]{1,0:T(8,128)(2,1)S(1)}, u32[]{:S(2)}, u32[]{:S(2)}) collective-permute-start(bf16[128,2048]{1,0:T(8,128)(2,1)S(1)} %get-tuple-element.97.refs_1_), channel_id=1, source_target_pairs={{0,14},{1,15},{2,0},{3,1},{4,2},{5,3},{6,4},{7,5},{8,6},{9,7},{10,... | collective-permute-start | bytes 1572872 | tf_op jit(solution)/shard_map/ppermute | solution.py:43
  26.6 0.6 select.3
  27.3 1.7 %collective-permute-start.5 = (bf16[64,2048]{1,0:T(8,128)(2,1)S(1)}, bf16[64,2048]{1,0:T(8,128)(2,1)S(1)}, u32[]{:S(2)}, u32[]{:S(2)}) collective-permute-start(bf16[64,2048]{1,0:T(8,128)(2,1)S(1)} %get-tuple-element.93), channel_id=1, source_target_pairs={{0,32},{32,0},{64,96},{96,64},{128,160},{160,128},{192,224},{224,1... | collective-permute-start | bytes 786440 | tf_op jit(solution)/shard_map/ppermute | solution.py:51
  28.9 0.8 collective-permute-start.8
  29.8 5.1 %collective-permute-done.5.refs_0_ = bf16[64,2048]{1,0:T(8,128)(2,1)S(1)} collective-permute-done((bf16[64,2048]{1,0:T(8,128)(2,1)S(1)}, bf16[64,2048]{1,0:T(8,128)(2,1)S(1)}, u32[]{:S(2)}, u32[]{:S(2)}) %collective-permute-start.5) | collective-permute-done | bytes 262176 | tf_op jit(solution)/shard_map/ppermute | solution.py:51
  34.9 2.6 %collective-permute-done.10.refs_0_ = bf16[128,2048]{1,0:T(8,128)(2,1)S(1)} collective-permute-done((bf16[128,2048]{1,0:T(8,128)(2,1)S(1)}, bf16[128,2048]{1,0:T(8,128)(2,1)S(1)}, u32[]{:S(2)}, u32[]{:S(2)}) %collective-permute-start.10) | collective-permute-done | bytes 524320 | tf_op jit(solution)/shard_map/ppermute | solution.py:43
  37.5 3.7 %collective-permute-start.14 = (bf16[128,2048]{1,0:T(8,128)(2,1)S(1)}, bf16[128,2048]{1,0:T(8,128)(2,1)S(1)}, u32[]{:S(2)}, u32[]{:S(2)}) collective-permute-start(bf16[128,2048]{1,0:T(8,128)(2,1)S(1)} %get-tuple-element.105.refs_4_), channel_id=1, source_target_pairs={{0,14},{1,15},{2,0},{3,1},{4,2},{5,3},{6,4},{7,5},{8,6},{9,7},{10,... | collective-permute-start | bytes 1572872 | tf_op jit(solution)/shard_map/ppermute | solution.py:43
  41.2 0.6 select.4.own_ref
  41.8 1.5 collective-permute-start.7
  43.3 9.3 %collective-permute-done.7.refs_0_ = bf16[64,2048]{1,0:T(8,128)(2,1)S(1)} collective-permute-done((bf16[64,2048]{1,0:T(8,128)(2,1)S(1)}, bf16[64,2048]{1,0:T(8,128)(2,1)S(1)}, u32[]{:S(2)}, u32[]{:S(2)}) %collective-permute-start.7) | collective-permute-done | bytes 262176 | tf_op jit(solution)/shard_map/ppermute | solution.py:51
  52.6 0.6 select.5.refs_0_
  53.2 1.7 %collective-permute-start.11 = (bf16[64,2048]{1,0:T(8,128)(2,1)S(1)}, bf16[64,2048]{1,0:T(8,128)(2,1)S(1)}, u32[]{:S(2)}, u32[]{:S(2)}) collective-permute-start(bf16[64,2048]{1,0:T(8,128)(2,1)S(1)} %select.5.refs_0_), channel_id=1, source_target_pairs={{0,32},{32,0},{64,96},{96,64},{128,160},{160,128},{192,224},{224,1... | collective-permute-start | bytes 786440 | tf_op jit(solution)/shard_map/ppermute | solution.py:51
  55.0 3.3 %collective-permute-start.17 = (bf16[128,2048]{1,0:T(8,128)(2,1)S(1)}, bf16[128,2048]{1,0:T(8,128)(2,1)S(1)}, u32[]{:S(2)}, u32[]{:S(2)}) collective-permute-start(bf16[128,2048]{1,0:T(8,128)(2,1)S(1)} %get-tuple-element.112.refs_6_), channel_id=1, source_target_pairs={{0,14},{1,15},{2,0},{3,1},{4,2},{5,3},{6,4},{7,5},{8,6},{9,7},{10,... | collective-permute-start | bytes 1572872 | tf_op jit(solution)/shard_map/ppermute | solution.py:43
  58.3 0.8 collective-permute-start.16
  59.1 2.2 %collective-permute-done.12.refs_0_ = bf16[128,2048]{1,0:T(8,128)(2,1)S(1)} collective-permute-done((bf16[128,2048]{1,0:T(8,128)(2,1)S(1)}, bf16[128,2048]{1,0:T(8,128)(2,1)S(1)}, u32[]{:S(2)}, u32[]{:S(2)}) %collective-permute-start.12) | collective-permute-done | bytes 524320 | tf_op jit(solution)/shard_map/ppermute | solution.py:43
  61.3 3.3 %collective-permute-start.15 = (bf16[128,2048]{1,0:T(8,128)(2,1)S(1)}, bf16[128,2048]{1,0:T(8,128)(2,1)S(1)}, u32[]{:S(2)}, u32[]{:S(2)}) collective-permute-start(bf16[128,2048]{1,0:T(8,128)(2,1)S(1)} %stack.1.a_ref.refs_0_.refs_20_), channel_id=1, source_target_pairs={{0,64},{32,96},{64,0},{96,32},{128,192},{160,224},{192,128},{224,1... | collective-permute-start | bytes 1572872 | tf_op jit(solution)/shard_map/ppermute | solution.py:51
  64.6 6.4 %collective-permute-done.18.refs_0_ = bf16[128,2048]{1,0:T(8,128)(2,1)S(1)} collective-permute-done((bf16[128,2048]{1,0:T(8,128)(2,1)S(1)}, bf16[128,2048]{1,0:T(8,128)(2,1)S(1)}, u32[]{:S(2)}, u32[]{:S(2)}) %collective-permute-start.18) | collective-permute-done | bytes 524320 | tf_op jit(solution)/shard_map/ppermute | solution.py:43
  71.1 2.0 %collective-permute-done.16.refs_0_ = bf16[128,2048]{1,0:T(8,128)(2,1)S(1)} collective-permute-done((bf16[128,2048]{1,0:T(8,128)(2,1)S(1)}, bf16[128,2048]{1,0:T(8,128)(2,1)S(1)}, u32[]{:S(2)}, u32[]{:S(2)}) %collective-permute-start.16) | collective-permute-done | bytes 524320 | tf_op jit(solution)/shard_map/ppermute | solution.py:43
  73.1 0.2 collective-permute-done.15.refs_0_
  73.5 0.5 collective-permute-start.23
  74.0 1.1 norm.2
  75.1 2.5 %encoder.1 = (bf16[256,2048]{1,0:T(8,128)(2,1)S(1)}, f32[1,2048]{1,0:T(1,128)S(1)}, bf16[256,2048]{1,0:T(8,128)(2,1)S(1)}, f32[8,128]{1,0:T(8,128)S(1)}) custom-call(s32[8]{0:T(128)S(1)} %copy-done.5, f32[1,2048]{1,0:T(1,128)S(1)} %bitcast.16, bf16[256,2048]{1,0:T(8,128)(2,1)S(1)} %bitcast.12, bf16[128,2048]{1,0:T(8,128)(2,1)S(1)} %stack.1.a_ref.refs_0_.refs_20_, ...), custom_call_target="tpu_custom_call" | custom-call | bytes 1024 | tf_op jit(solution)/shard_map/encoder/pallas_call | solution.py:393
  77.6 2.7 %collective-permute-done.19.refs_0_ = bf16[128,2048]{1,0:T(8,128)(2,1)S(1)} collective-permute-done((bf16[128,2048]{1,0:T(8,128)(2,1)S(1)}, bf16[128,2048]{1,0:T(8,128)(2,1)S(1)}, u32[]{:S(2)}, u32[]{:S(2)}) %collective-permute-start.19) | collective-permute-done | bytes 524320 | tf_op jit(solution)/shard_map/ppermute | solution.py:43
  80.3 1.2 collective-permute-done.21.refs_0_
  81.6 1.1 norm.3
  82.7 9.2 %attend.1 = (bf16[256,2048]{1,0:T(8,128)(2,1)S(1)}, bf16[256,2048]{1,0:T(8,128)(2,1)S(1)}, bf16[256,2048]{1,0:T(8,128)(2,1)S(1)}, bf16[272,2048]{1,0:T(8,128)(2,1)S(1)}, f32[1,2048]{1,0:T(1,128)S(1)}) custom-call(bf16[128,2048]{1,0:T(8,128)(2,1)S(1)} %unit.1.token_ref.refs_0_, bf16[128,2048]{1,0:T(8,128)(2,1)S(1)} %get-tuple-element.97.refs_1_, ...), custom_call_target="tpu_custom_call" | custom-call | flops 10000000000 | bytes 20000000 | tf_op jit(solution)/shard_map/attend/pallas_call | solution.py:374
  92.0 0.5 collective-permute-start.25
  92.5 2.2 %collective-permute-done.24.got_ref = bf16[272,2048]{1,0:T(8,128)(2,1)S(1)} collective-permute-done((bf16[272,2048]{1,0:T(8,128)(2,1)S(1)}, bf16[272,2048]{1,0:T(8,128)(2,1)S(1)}, u32[]{:S(2)}, u32[]{:S(2)}) %collective-permute-start.24) | collective-permute-done | bytes 1114144 | tf_op jit(solution)/shard_map/ppermute | solution.py:43
  94.7 0.3 split.1
  95.0 7.2 %collective-permute-start.26 = (bf16[64,2048]{1,0:T(8,128)(2,1)S(1)}, bf16[64,2048]{1,0:T(8,128)(2,1)S(1)}, u32[]{:S(2)}, u32[]{:S(2)}) collective-permute-start(bf16[64,2048]{1,0:T(8,128)(2,1)S(1)} %get-tuple-element.155), channel_id=1, source_target_pairs={{0,32},{32,0},{64,96},{96,64},{128,160},{160,128},{192,224},{224,1... | collective-permute-start | bytes 786440 | tf_op jit(solution)/shard_map/ppermute | solution.py:51
  102.2 2.9 %collective-permute-start.27 = (bf16[64,2048]{1,0:T(8,128)(2,1)S(1)}, bf16[64,2048]{1,0:T(8,128)(2,1)S(1)}, u32[]{:S(2)}, u32[]{:S(2)}) collective-permute-start(bf16[64,2048]{1,0:T(8,128)(2,1)S(1)} %get-tuple-element.156), channel_id=1, source_target_pairs={{0,64},{32,96},{64,0},{96,32},{128,192},{160,224},{192,128},{224,1... | collective-permute-start | bytes 786440 | tf_op jit(solution)/shard_map/ppermute | solution.py:51
  105.1 3.0 %collective-permute-start.35 = (f32[1,2048]{1,0:T(1,128)S(1)}, f32[1,2048]{1,0:T(1,128)S(1)}, u32[]{:S(2)}, u32[]{:S(2)}) collective-permute-start(f32[1,2048]{1,0:T(1,128)S(1)} %get-tuple-element.158.refs_0_), channel_id=1, source_target_pairs={{0,14},{1,15},{2,12},{3,13},{4,10},{5,11},{6,8},{7,9},{8,6},{9,7},... | collective-permute-start | bytes 24584 | tf_op jit(solution)/shard_map/ppermute | solution.py:43
  108.0 1.9 %collective-permute-done.35.refs_7_ = f32[1,2048]{1,0:T(1,128)S(1)} collective-permute-done((f32[1,2048]{1,0:T(1,128)S(1)}, f32[1,2048]{1,0:T(1,128)S(1)}, u32[]{:S(2)}, u32[]{:S(2)}) %collective-permute-start.35) | collective-permute-done | bytes 8224 | tf_op jit(solution)/shard_map/ppermute | solution.py:43
  110.0 2.9 %collective-permute-start.33 = (f32[1,2048]{1,0:T(1,128)S(1)}, f32[1,2048]{1,0:T(1,128)S(1)}, u32[]{:S(2)}, u32[]{:S(2)}) collective-permute-start(f32[1,2048]{1,0:T(1,128)S(1)} %get-tuple-element.158.refs_0_), channel_id=1, source_target_pairs={{0,10},{1,11},{2,8},{3,9},{4,14},{5,15},{6,12},{7,13},{8,2},{9,3},... | collective-permute-start | bytes 24584 | tf_op jit(solution)/shard_map/ppermute | solution.py:43
  112.8 1.0 collective-permute-done.34.refs_6_
  113.8 2.0 %collective-permute-start.32 = (f32[1,2048]{1,0:T(1,128)S(1)}, f32[1,2048]{1,0:T(1,128)S(1)}, u32[]{:S(2)}, u32[]{:S(2)}) collective-permute-start(f32[1,2048]{1,0:T(1,128)S(1)} %get-tuple-element.158.refs_0_), channel_id=1, source_target_pairs={{0,8},{1,9},{2,10},{3,11},{4,12},{5,13},{6,14},{7,15},{8,0},{9,1},... | collective-permute-start | bytes 24584 | tf_op jit(solution)/shard_map/ppermute | solution.py:43
  115.8 0.9 collective-permute-done.33.refs_5_
  116.6 2.2 %collective-permute-start.31 = (f32[1,2048]{1,0:T(1,128)S(1)}, f32[1,2048]{1,0:T(1,128)S(1)}, u32[]{:S(2)}, u32[]{:S(2)}) collective-permute-start(f32[1,2048]{1,0:T(1,128)S(1)} %get-tuple-element.158.refs_0_), channel_id=1, source_target_pairs={{0,6},{1,7},{2,4},{3,5},{4,2},{5,3},{6,0},{7,1},{8,14},{9,15},{10,... | collective-permute-start | bytes 24584 | tf_op jit(solution)/shard_map/ppermute | solution.py:43
  118.8 2.5 %collective-permute-done.32.refs_4_ = f32[1,2048]{1,0:T(1,128)S(1)} collective-permute-done((f32[1,2048]{1,0:T(1,128)S(1)}, f32[1,2048]{1,0:T(1,128)S(1)}, u32[]{:S(2)}, u32[]{:S(2)}) %collective-permute-start.32) | collective-permute-done | bytes 8224 | tf_op jit(solution)/shard_map/ppermute | solution.py:43
  121.4 1.5 collective-permute-start.30
  122.8 1.0 collective-permute-start.29
  123.8 2.1 %collective-permute-done.30.refs_2_ = f32[1,2048]{1,0:T(1,128)S(1)} collective-permute-done((f32[1,2048]{1,0:T(1,128)S(1)}, f32[1,2048]{1,0:T(1,128)S(1)}, u32[]{:S(2)}, u32[]{:S(2)}) %collective-permute-start.30) | collective-permute-done | bytes 8224 | tf_op jit(solution)/shard_map/ppermute | solution.py:43
  125.9 0.6 collective-permute-done.29.refs_1_
  126.7 3.9 %collective-permute-start.36 = (bf16[64,2048]{1,0:T(8,128)(2,1)S(1)}, bf16[64,2048]{1,0:T(8,128)(2,1)S(1)}, u32[]{:S(2)}, u32[]{:S(2)}) collective-permute-start(bf16[64,2048]{1,0:T(8,128)(2,1)S(1)} %get-tuple-element.165), channel_id=1, source_target_pairs={{0,128},{32,160},{64,192},{96,224},{128,0},{160,32},{192,64},{224,... | collective-permute-start | bytes 786440 | tf_op jit(solution)/shard_map/ppermute | solution.py:51
  130.6 3.0 %collective-permute-start.39 = (f32[1,2048]{1,0:T(1,128)S(1)}, f32[1,2048]{1,0:T(1,128)S(1)}, u32[]{:S(2)}, u32[]{:S(2)}) collective-permute-start(f32[1,2048]{1,0:T(1,128)S(1)} %get-tuple-element.166.refs_0_), channel_id=1, source_target_pairs={{0,96},{32,64},{64,32},{96,0},{128,224},{160,192},{192,160},{224,1... | collective-permute-start | bytes 24584 | tf_op jit(solution)/shard_map/ppermute | solution.py:51
  133.6 1.1 collective-permute-start.37
  134.7 0.8 collective-permute-done.39.refs_3_
  135.5 3.5 %collective-permute-done.38.refs_2_ = f32[1,2048]{1,0:T(1,128)S(1)} collective-permute-done((f32[1,2048]{1,0:T(1,128)S(1)}, f32[1,2048]{1,0:T(1,128)S(1)}, u32[]{:S(2)}, u32[]{:S(2)}) %collective-permute-start.38) | collective-permute-done | bytes 8224 | tf_op jit(solution)/shard_map/ppermute | solution.py:51
  139.0 0.8 collective-permute-start.42
  139.8 1.4 collective-permute-start.41
  141.2 2.0 %collective-permute-start.40 = (bf16[64,2048]{1,0:T(8,128)(2,1)S(1)}, bf16[64,2048]{1,0:T(8,128)(2,1)S(1)}, u32[]{:S(2)}, u32[]{:S(2)}) collective-permute-start(bf16[64,2048]{1,0:T(8,128)(2,1)S(1)} %get-tuple-element.167.refs_0_), channel_id=1, source_target_pairs={{0,32},{32,0},{64,96},{96,64},{128,160},{160,128},{192,224},{224,1... | collective-permute-start | bytes 786440 | tf_op jit(solution)/shard_map/ppermute | solution.py:51
  143.2 3.6 %collective-permute-done.43.refs_1_ = f32[1,2048]{1,0:T(1,128)S(1)} collective-permute-done((f32[1,2048]{1,0:T(1,128)S(1)}, f32[1,2048]{1,0:T(1,128)S(1)}, u32[]{:S(2)}, u32[]{:S(2)}) %collective-permute-start.43) | collective-permute-done | bytes 8224 | tf_op jit(solution)/shard_map/ppermute | solution.py:43
  146.9 0.6 collective-permute-start.44
  147.4 1.1 rows.1
  148.6 3.5 %collective-permute-done.44.refs_1_ = f32[1,2048]{1,0:T(1,128)S(1)} collective-permute-done((f32[1,2048]{1,0:T(1,128)S(1)}, f32[1,2048]{1,0:T(1,128)S(1)}, u32[]{:S(2)}, u32[]{:S(2)}) %collective-permute-start.44) | collective-permute-done | bytes 8224 | tf_op jit(solution)/shard_map/ppermute | solution.py:51
  152.0 0.6 add.7
  152.6 1.1 grads.1
  (83 shorter events, 1.6 us)
Async XLA Ops:
  0.6 3.0 %copy-start = (bf16[1,256,2048]{2,1,0:T(8,128)(2,1)S(1)}, bf16[1,256,2048]{2,1,0:T(8,128)(2,1)}, u32[]{:S(2)}) copy-start(bf16[1,256,2048]{2,1,0:T(8,128)(2,1)} %param.5) | copy-start | bytes 3145732
  0.6 1.1 copy-start.3
  1.9 1.6 %collective-permute-start.1 = (bf16[64,2048]{1,0:T(8,128)(2,1)S(1)}, bf16[64,2048]{1,0:T(8,128)(2,1)S(1)}, u32[]{:S(2)}, u32[]{:S(2)}) collective-permute-start(bf16[64,2048]{1,0:T(8,128)(2,1)S(1)} %get-tuple-element.87), channel_id=1, source_target_pairs={{0,1},{1,0},{2,3},{3,2},{4,5},{5,4},{6,7},{7,6},{8,9},{9,8},{10,11... | collective-permute-start | bytes 786440 | tf_op jit(solution)/shard_map/ppermute | solution.py:43
  3.6 1.2 copy-start.1
  5.0 17.8 %collective-permute-start.4 = (bf16[256,2048]{1,0:T(8,128)(2,1)S(1)}, bf16[256,2048]{1,0:T(8,128)(2,1)S(1)}, u32[]{:S(2)}, u32[]{:S(2)}) collective-permute-start(bf16[256,2048]{1,0:T(8,128)(2,1)S(1)} %give.1), channel_id=1, source_target_pairs={{0,1},{1,0},{2,3},{3,2},{4,5},{5,4},{6,7},{7,6},{8,9},{9,8},{10,11... | collective-permute-start | bytes 3145736 | tf_op jit(solution)/shard_map/ppermute | solution.py:43
  5.2 17.6 %collective-permute-start.3 = (bf16[128,2048]{1,0:T(8,128)(2,1)S(1)}, bf16[128,2048]{1,0:T(8,128)(2,1)S(1)}, u32[]{:S(2)}, u32[]{:S(2)}) collective-permute-start(bf16[128,2048]{1,0:T(8,128)(2,1)S(1)} %unit.1.token_ref.refs_0_), channel_id=1, source_target_pairs={{0,14},{1,15},{2,0},{3,1},{4,2},{5,3},{6,4},{7,5},{8,6},{9,7},{10,... | collective-permute-start | bytes 1572872 | tf_op jit(solution)/shard_map/ppermute | solution.py:43
  11.0 15.5 %collective-permute-start.2 = (bf16[128,2048]{1,0:T(8,128)(2,1)S(1)}, bf16[128,2048]{1,0:T(8,128)(2,1)S(1)}, u32[]{:S(2)}, u32[]{:S(2)}) collective-permute-start(bf16[128,2048]{1,0:T(8,128)(2,1)S(1)} %unit.1.token_ref.refs_0_), channel_id=1, source_target_pairs={{0,2},{1,3},{2,4},{3,5},{4,6},{5,7},{6,8},{7,9},{8,10},{9,11},{10,... | collective-permute-start | bytes 1572872 | tf_op jit(solution)/shard_map/ppermute | solution.py:43
  11.1 15.6 %collective-permute-start = (bf16[128,2048]{1,0:T(8,128)(2,1)S(1)}, bf16[128,2048]{1,0:T(8,128)(2,1)S(1)}, u32[]{:S(2)}, u32[]{:S(2)}) collective-permute-start(bf16[128,2048]{1,0:T(8,128)(2,1)S(1)} %half.1), channel_id=1, source_target_pairs={{0,64},{32,96},{64,0},{96,32},{128,192},{160,224},{192,128},{224,1... | collective-permute-start | bytes 1572872 | tf_op jit(solution)/shard_map/ppermute | solution.py:51
  14.4 15.4 %collective-permute-start.6 = (bf16[128,2048]{1,0:T(8,128)(2,1)S(1)}, bf16[128,2048]{1,0:T(8,128)(2,1)S(1)}, u32[]{:S(2)}, u32[]{:S(2)}) collective-permute-start(bf16[128,2048]{1,0:T(8,128)(2,1)S(1)} %unit.1.token_ref.refs_0_), channel_id=1, source_target_pairs={{0,16},{1,17},{2,18},{3,19},{4,20},{5,21},{6,22},{7,23},{8,24},{9,... | collective-permute-start | bytes 1572872 | tf_op jit(solution)/shard_map/ppermute | solution.py:43
  22.8 3.9 %copy-start.5 = (s32[8]{0:T(128)S(1)}, s32[8]{0:T(128)}, u32[]{:S(2)}) copy-start(s32[8]{0:T(128)} %refs_28_.1) | copy-start | bytes 100
  22.8 14.7 %collective-permute-start.10 = (bf16[128,2048]{1,0:T(8,128)(2,1)S(1)}, bf16[128,2048]{1,0:T(8,128)(2,1)S(1)}, u32[]{:S(2)}, u32[]{:S(2)}) collective-permute-start(bf16[128,2048]{1,0:T(8,128)(2,1)S(1)} %get-tuple-element.97.refs_1_), channel_id=1, source_target_pairs={{0,14},{1,15},{2,0},{3,1},{4,2},{5,3},{6,4},{7,5},{8,6},{9,7},{10,... | collective-permute-start | bytes 1572872 | tf_op jit(solution)/shard_map/ppermute | solution.py:43
  26.5 14.7 %collective-permute-start.9 = (bf16[128,2048]{1,0:T(8,128)(2,1)S(1)}, bf16[128,2048]{1,0:T(8,128)(2,1)S(1)}, u32[]{:S(2)}, u32[]{:S(2)}) collective-permute-start(bf16[128,2048]{1,0:T(8,128)(2,1)S(1)} %get-tuple-element.98.refs_2_), channel_id=1, source_target_pairs={{0,2},{1,3},{2,4},{3,5},{4,6},{5,7},{6,8},{7,9},{8,10},{9,11},{10,... | collective-permute-start | bytes 1572872 | tf_op jit(solution)/shard_map/ppermute | solution.py:43
  27.3 7.6 %collective-permute-start.5 = (bf16[64,2048]{1,0:T(8,128)(2,1)S(1)}, bf16[64,2048]{1,0:T(8,128)(2,1)S(1)}, u32[]{:S(2)}, u32[]{:S(2)}) collective-permute-start(bf16[64,2048]{1,0:T(8,128)(2,1)S(1)} %get-tuple-element.93), channel_id=1, source_target_pairs={{0,32},{32,0},{64,96},{96,64},{128,160},{160,128},{192,224},{224,1... | collective-permute-start | bytes 786440 | tf_op jit(solution)/shard_map/ppermute | solution.py:51
  28.9 14.3 %collective-permute-start.8 = (bf16[128,2048]{1,0:T(8,128)(2,1)S(1)}, bf16[128,2048]{1,0:T(8,128)(2,1)S(1)}, u32[]{:S(2)}, u32[]{:S(2)}) collective-permute-start(bf16[128,2048]{1,0:T(8,128)(2,1)S(1)} %get-tuple-element.97.refs_1_), channel_id=1, source_target_pairs={{0,16},{1,17},{2,18},{3,19},{4,20},{5,21},{6,22},{7,23},{8,24},{9,... | collective-permute-start | bytes 1572872 | tf_op jit(solution)/shard_map/ppermute | solution.py:43
  37.5 17.4 %collective-permute-start.14 = (bf16[128,2048]{1,0:T(8,128)(2,1)S(1)}, bf16[128,2048]{1,0:T(8,128)(2,1)S(1)}, u32[]{:S(2)}, u32[]{:S(2)}) collective-permute-start(bf16[128,2048]{1,0:T(8,128)(2,1)S(1)} %get-tuple-element.105.refs_4_), channel_id=1, source_target_pairs={{0,14},{1,15},{2,0},{3,1},{4,2},{5,3},{6,4},{7,5},{8,6},{9,7},{10,... | collective-permute-start | bytes 1572872 | tf_op jit(solution)/shard_map/ppermute | solution.py:43
  41.2 13.7 %collective-permute-start.13 = (bf16[128,2048]{1,0:T(8,128)(2,1)S(1)}, bf16[128,2048]{1,0:T(8,128)(2,1)S(1)}, u32[]{:S(2)}, u32[]{:S(2)}) collective-permute-start(bf16[128,2048]{1,0:T(8,128)(2,1)S(1)} %get-tuple-element.104.refs_5_), channel_id=1, source_target_pairs={{0,2},{1,3},{2,4},{3,5},{4,6},{5,7},{6,8},{7,9},{8,10},{9,11},{10,... | collective-permute-start | bytes 1572872 | tf_op jit(solution)/shard_map/ppermute | solution.py:43
  41.8 10.8 %collective-permute-start.7 = (bf16[64,2048]{1,0:T(8,128)(2,1)S(1)}, bf16[64,2048]{1,0:T(8,128)(2,1)S(1)}, u32[]{:S(2)}, u32[]{:S(2)}) collective-permute-start(bf16[64,2048]{1,0:T(8,128)(2,1)S(1)} %select.4.own_ref), channel_id=1, source_target_pairs={{0,128},{32,160},{64,192},{96,224},{128,0},{160,32},{192,64},{224,... | collective-permute-start | bytes 786440 | tf_op jit(solution)/shard_map/ppermute | solution.py:51
  43.3 18.0 %collective-permute-start.12 = (bf16[128,2048]{1,0:T(8,128)(2,1)S(1)}, bf16[128,2048]{1,0:T(8,128)(2,1)S(1)}, u32[]{:S(2)}, u32[]{:S(2)}) collective-permute-start(bf16[128,2048]{1,0:T(8,128)(2,1)S(1)} %get-tuple-element.104.refs_5_), channel_id=1, source_target_pairs={{0,16},{1,17},{2,18},{3,19},{4,20},{5,21},{6,22},{7,23},{8,24},{9,... | collective-permute-start | bytes 1572872 | tf_op jit(solution)/shard_map/ppermute | solution.py:43
  53.2 8.1 %collective-permute-start.11 = (bf16[64,2048]{1,0:T(8,128)(2,1)S(1)}, bf16[64,2048]{1,0:T(8,128)(2,1)S(1)}, u32[]{:S(2)}, u32[]{:S(2)}) collective-permute-start(bf16[64,2048]{1,0:T(8,128)(2,1)S(1)} %select.5.refs_0_), channel_id=1, source_target_pairs={{0,32},{32,0},{64,96},{96,64},{128,160},{160,128},{192,224},{224,1... | collective-permute-start | bytes 786440 | tf_op jit(solution)/shard_map/ppermute | solution.py:51
  54.9 16.2 %collective-permute-start.18 = (bf16[128,2048]{1,0:T(8,128)(2,1)S(1)}, bf16[128,2048]{1,0:T(8,128)(2,1)S(1)}, u32[]{:S(2)}, u32[]{:S(2)}) collective-permute-start(bf16[128,2048]{1,0:T(8,128)(2,1)S(1)} %get-tuple-element.111.refs_8_), channel_id=1, source_target_pairs={{0,2},{1,3},{2,4},{3,5},{4,6},{5,7},{6,8},{7,9},{8,10},{9,11},{10,... | collective-permute-start | bytes 1572872 | tf_op jit(solution)/shard_map/ppermute | solution.py:43
  55.0 16.1 %collective-permute-start.17 = (bf16[128,2048]{1,0:T(8,128)(2,1)S(1)}, bf16[128,2048]{1,0:T(8,128)(2,1)S(1)}, u32[]{:S(2)}, u32[]{:S(2)}) collective-permute-start(bf16[128,2048]{1,0:T(8,128)(2,1)S(1)} %get-tuple-element.112.refs_6_), channel_id=1, source_target_pairs={{0,14},{1,15},{2,0},{3,1},{4,2},{5,3},{6,4},{7,5},{8,6},{9,7},{10,... | collective-permute-start | bytes 1572872 | tf_op jit(solution)/shard_map/ppermute | solution.py:43
  58.3 14.9 %collective-permute-start.16 = (bf16[128,2048]{1,0:T(8,128)(2,1)S(1)}, bf16[128,2048]{1,0:T(8,128)(2,1)S(1)}, u32[]{:S(2)}, u32[]{:S(2)}) collective-permute-start(bf16[128,2048]{1,0:T(8,128)(2,1)S(1)} %get-tuple-element.111.refs_8_), channel_id=1, source_target_pairs={{0,16},{1,17},{2,18},{3,19},{4,20},{5,21},{6,22},{7,23},{8,24},{9,... | collective-permute-start | bytes 1572872 | tf_op jit(solution)/shard_map/ppermute | solution.py:43
  61.3 12.0 %collective-permute-start.15 = (bf16[128,2048]{1,0:T(8,128)(2,1)S(1)}, bf16[128,2048]{1,0:T(8,128)(2,1)S(1)}, u32[]{:S(2)}, u32[]{:S(2)}) collective-permute-start(bf16[128,2048]{1,0:T(8,128)(2,1)S(1)} %stack.1.a_ref.refs_0_.refs_20_), channel_id=1, source_target_pairs={{0,64},{32,96},{64,0},{96,32},{128,192},{160,224},{192,128},{224,1... | collective-permute-start | bytes 1572872 | tf_op jit(solution)/shard_map/ppermute | solution.py:51
  64.6 15.7 %collective-permute-start.20 = (bf16[128,2048]{1,0:T(8,128)(2,1)S(1)}, bf16[128,2048]{1,0:T(8,128)(2,1)S(1)}, u32[]{:S(2)}, u32[]{:S(2)}) collective-permute-start(bf16[128,2048]{1,0:T(8,128)(2,1)S(1)} %get-tuple-element.119.refs_3_), channel_id=1, source_target_pairs={{0,2},{1,3},{2,4},{3,5},{4,6},{5,7},{6,8},{7,9},{8,10},{9,11},{10,... | collective-permute-start | bytes 1572872 | tf_op jit(solution)/shard_map/ppermute | solution.py:43
  71.0 10.5 %collective-permute-start.21 = (bf16[128,2048]{1,0:T(8,128)(2,1)S(1)}, bf16[128,2048]{1,0:T(8,128)(2,1)S(1)}, u32[]{:S(2)}, u32[]{:S(2)}) collective-permute-start(bf16[128,2048]{1,0:T(8,128)(2,1)S(1)} %get-tuple-element.122.refs_10_), channel_id=1, source_target_pairs={{0,16},{1,17},{2,18},{3,19},{4,20},{5,21},{6,22},{7,23},{8,24},{9,... | collective-permute-start | bytes 1572872 | tf_op jit(solution)/shard_map/ppermute | solution.py:43
  71.0 2.9 %copy-start.4 = (f32[2048]{0:T(1024)S(1)}, f32[2048]{0:T(1024)}, u32[]{:S(2)}) copy-start(f32[2048]{0:T(1024)} %param.8) | copy-start | bytes 24580
  71.0 9.3 %collective-permute-start.19 = (bf16[128,2048]{1,0:T(8,128)(2,1)S(1)}, bf16[128,2048]{1,0:T(8,128)(2,1)S(1)}, u32[]{:S(2)}, u32[]{:S(2)}) collective-permute-start(bf16[128,2048]{1,0:T(8,128)(2,1)S(1)} %get-tuple-element.123.refs_11_), channel_id=1, source_target_pairs={{0,14},{1,15},{2,0},{3,1},{4,2},{5,3},{6,4},{7,5},{8,6},{9,7},{10,... | collective-permute-start | bytes 1572872 | tf_op jit(solution)/shard_map/ppermute | solution.py:43
  73.3 1.7 %copy-start.2 = (bf16[1,256,2048]{2,1,0:T(8,128)(2,1)S(1)}, bf16[1,256,2048]{2,1,0:T(8,128)(2,1)}, u32[]{:S(2)}) copy-start(bf16[1,256,2048]{2,1,0:T(8,128)(2,1)} %param.7) | copy-start | bytes 3145732
  73.4 8.2 %collective-permute-start.22 = (bf16[128,2048]{1,0:T(8,128)(2,1)S(1)}, bf16[128,2048]{1,0:T(8,128)(2,1)S(1)}, u32[]{:S(2)}, u32[]{:S(2)}) collective-permute-start(bf16[128,2048]{1,0:T(8,128)(2,1)S(1)} %late.1), channel_id=1, source_target_pairs={{0,1},{1,0},{2,3},{3,2},{4,5},{5,4},{6,7},{7,6},{8,9},{9,8},{10,11... | collective-permute-start | bytes 1572872 | tf_op jit(solution)/shard_map/ppermute | solution.py:43
  73.5 8.1 %collective-permute-start.23 = (bf16[128,2048]{1,0:T(8,128)(2,1)S(1)}, bf16[128,2048]{1,0:T(8,128)(2,1)S(1)}, u32[]{:S(2)}, u32[]{:S(2)}) collective-permute-start(bf16[128,2048]{1,0:T(8,128)(2,1)S(1)} %get-tuple-element.117.b_ref.refs_1_.refs_21_), channel_id=1, source_target_pairs={{0,1},{1,0},{2,3},{3,2},{4,5},{5,4},{6,7},{7,6},{8,9},{9,8},{10,11... | collective-permute-start | bytes 1572872 | tf_op jit(solution)/shard_map/ppermute | solution.py:43
  91.9 2.8 %collective-permute-start.24 = (bf16[272,2048]{1,0:T(8,128)(2,1)S(1)}, bf16[272,2048]{1,0:T(8,128)(2,1)S(1)}, u32[]{:S(2)}, u32[]{:S(2)}) collective-permute-start(bf16[272,2048]{1,0:T(8,128)(2,1)S(1)} %get-tuple-element.148), channel_id=1, source_target_pairs={{0,1},{1,0},{2,3},{3,2},{4,5},{5,4},{6,7},{7,6},{8,9},{9,8},{10,11... | collective-permute-start | bytes 3342344 | tf_op jit(solution)/shard_map/ppermute | solution.py:43
  92.0 13.1 %collective-permute-start.25 = (bf16[256,2048]{1,0:T(8,128)(2,1)S(1)}, bf16[256,2048]{1,0:T(8,128)(2,1)S(1)}, u32[]{:S(2)}, u32[]{:S(2)}) collective-permute-start(bf16[256,2048]{1,0:T(8,128)(2,1)S(1)} %get-tuple-element.150), channel_id=1, source_target_pairs={{0,1},{1,0},{2,3},{3,2},{4,5},{5,4},{6,7},{7,6},{8,9},{9,8},{10,11... | collective-permute-start | bytes 3145736 | tf_op jit(solution)/shard_map/ppermute | solution.py:43
  95.0 31.5 %collective-permute-start.26 = (bf16[64,2048]{1,0:T(8,128)(2,1)S(1)}, bf16[64,2048]{1,0:T(8,128)(2,1)S(1)}, u32[]{:S(2)}, u32[]{:S(2)}) collective-permute-start(bf16[64,2048]{1,0:T(8,128)(2,1)S(1)} %get-tuple-element.155), channel_id=1, source_target_pairs={{0,32},{32,0},{64,96},{96,64},{128,160},{160,128},{192,224},{224,1... | collective-permute-start | bytes 786440 | tf_op jit(solution)/shard_map/ppermute | solution.py:51
  102.2 24.3 %collective-permute-start.27 = (bf16[64,2048]{1,0:T(8,128)(2,1)S(1)}, bf16[64,2048]{1,0:T(8,128)(2,1)S(1)}, u32[]{:S(2)}, u32[]{:S(2)}) collective-permute-start(bf16[64,2048]{1,0:T(8,128)(2,1)S(1)} %get-tuple-element.156), channel_id=1, source_target_pairs={{0,64},{32,96},{64,0},{96,32},{128,192},{160,224},{192,128},{224,1... | collective-permute-start | bytes 786440 | tf_op jit(solution)/shard_map/ppermute | solution.py:51
  105.1 21.4 %collective-permute-start.28 = (bf16[64,2048]{1,0:T(8,128)(2,1)S(1)}, bf16[64,2048]{1,0:T(8,128)(2,1)S(1)}, u32[]{:S(2)}, u32[]{:S(2)}) collective-permute-start(bf16[64,2048]{1,0:T(8,128)(2,1)S(1)} %get-tuple-element.157), channel_id=1, source_target_pairs={{0,96},{32,64},{64,32},{96,0},{128,224},{160,192},{192,160},{224,1... | collective-permute-start | bytes 786440 | tf_op jit(solution)/shard_map/ppermute | solution.py:51
  105.1 4.9 %collective-permute-start.35 = (f32[1,2048]{1,0:T(1,128)S(1)}, f32[1,2048]{1,0:T(1,128)S(1)}, u32[]{:S(2)}, u32[]{:S(2)}) collective-permute-start(f32[1,2048]{1,0:T(1,128)S(1)} %get-tuple-element.158.refs_0_), channel_id=1, source_target_pairs={{0,14},{1,15},{2,12},{3,13},{4,10},{5,11},{6,8},{7,9},{8,6},{9,7},... | collective-permute-start | bytes 24584 | tf_op jit(solution)/shard_map/ppermute | solution.py:43
  108.0 5.8 %collective-permute-start.34 = (f32[1,2048]{1,0:T(1,128)S(1)}, f32[1,2048]{1,0:T(1,128)S(1)}, u32[]{:S(2)}, u32[]{:S(2)}) collective-permute-start(f32[1,2048]{1,0:T(1,128)S(1)} %get-tuple-element.158.refs_0_), channel_id=1, source_target_pairs={{0,12},{1,13},{2,14},{3,15},{4,8},{5,9},{6,10},{7,11},{8,4},{9,5},... | collective-permute-start | bytes 24584 | tf_op jit(solution)/shard_map/ppermute | solution.py:43
  110.0 6.7 %collective-permute-start.33 = (f32[1,2048]{1,0:T(1,128)S(1)}, f32[1,2048]{1,0:T(1,128)S(1)}, u32[]{:S(2)}, u32[]{:S(2)}) collective-permute-start(f32[1,2048]{1,0:T(1,128)S(1)} %get-tuple-element.158.refs_0_), channel_id=1, source_target_pairs={{0,10},{1,11},{2,8},{3,9},{4,14},{5,15},{6,12},{7,13},{8,2},{9,3},... | collective-permute-start | bytes 24584 | tf_op jit(solution)/shard_map/ppermute | solution.py:43
  113.8 7.6 %collective-permute-start.32 = (f32[1,2048]{1,0:T(1,128)S(1)}, f32[1,2048]{1,0:T(1,128)S(1)}, u32[]{:S(2)}, u32[]{:S(2)}) collective-permute-start(f32[1,2048]{1,0:T(1,128)S(1)} %get-tuple-element.158.refs_0_), channel_id=1, source_target_pairs={{0,8},{1,9},{2,10},{3,11},{4,12},{5,13},{6,14},{7,15},{8,0},{9,1},... | collective-permute-start | bytes 24584 | tf_op jit(solution)/shard_map/ppermute | solution.py:43
  116.6 6.2 %collective-permute-start.31 = (f32[1,2048]{1,0:T(1,128)S(1)}, f32[1,2048]{1,0:T(1,128)S(1)}, u32[]{:S(2)}, u32[]{:S(2)}) collective-permute-start(f32[1,2048]{1,0:T(1,128)S(1)} %get-tuple-element.158.refs_0_), channel_id=1, source_target_pairs={{0,6},{1,7},{2,4},{3,5},{4,2},{5,3},{6,0},{7,1},{8,14},{9,15},{10,... | collective-permute-start | bytes 24584 | tf_op jit(solution)/shard_map/ppermute | solution.py:43
  121.4 4.5 %collective-permute-start.30 = (f32[1,2048]{1,0:T(1,128)S(1)}, f32[1,2048]{1,0:T(1,128)S(1)}, u32[]{:S(2)}, u32[]{:S(2)}) collective-permute-start(f32[1,2048]{1,0:T(1,128)S(1)} %get-tuple-element.158.refs_0_), channel_id=1, source_target_pairs={{0,4},{1,5},{2,6},{3,7},{4,0},{5,1},{6,2},{7,3},{8,12},{9,13},{10,... | collective-permute-start | bytes 24584 | tf_op jit(solution)/shard_map/ppermute | solution.py:43
  122.8 3.7 %collective-permute-start.29 = (f32[1,2048]{1,0:T(1,128)S(1)}, f32[1,2048]{1,0:T(1,128)S(1)}, u32[]{:S(2)}, u32[]{:S(2)}) collective-permute-start(f32[1,2048]{1,0:T(1,128)S(1)} %get-tuple-element.158.refs_0_), channel_id=1, source_target_pairs={{0,2},{1,3},{2,0},{3,1},{4,6},{5,7},{6,4},{7,5},{8,10},{9,11},{10,... | collective-permute-start | bytes 24584 | tf_op jit(solution)/shard_map/ppermute | solution.py:43
  126.7 12.3 %collective-permute-start.36 = (bf16[64,2048]{1,0:T(8,128)(2,1)S(1)}, bf16[64,2048]{1,0:T(8,128)(2,1)S(1)}, u32[]{:S(2)}, u32[]{:S(2)}) collective-permute-start(bf16[64,2048]{1,0:T(8,128)(2,1)S(1)} %get-tuple-element.165), channel_id=1, source_target_pairs={{0,128},{32,160},{64,192},{96,224},{128,0},{160,32},{192,64},{224,... | collective-permute-start | bytes 786440 | tf_op jit(solution)/shard_map/ppermute | solution.py:51
  130.6 4.9 %collective-permute-start.39 = (f32[1,2048]{1,0:T(1,128)S(1)}, f32[1,2048]{1,0:T(1,128)S(1)}, u32[]{:S(2)}, u32[]{:S(2)}) collective-permute-start(f32[1,2048]{1,0:T(1,128)S(1)} %get-tuple-element.166.refs_0_), channel_id=1, source_target_pairs={{0,96},{32,64},{64,32},{96,0},{128,224},{160,192},{192,160},{224,1... | collective-permute-start | bytes 24584 | tf_op jit(solution)/shard_map/ppermute | solution.py:51
  133.6 5.3 %collective-permute-start.38 = (f32[1,2048]{1,0:T(1,128)S(1)}, f32[1,2048]{1,0:T(1,128)S(1)}, u32[]{:S(2)}, u32[]{:S(2)}) collective-permute-start(f32[1,2048]{1,0:T(1,128)S(1)} %get-tuple-element.166.refs_0_), channel_id=1, source_target_pairs={{0,64},{32,96},{64,0},{96,32},{128,192},{160,224},{192,128},{224,1... | collective-permute-start | bytes 24584 | tf_op jit(solution)/shard_map/ppermute | solution.py:51
  133.6 5.3 %collective-permute-start.37 = (f32[1,2048]{1,0:T(1,128)S(1)}, f32[1,2048]{1,0:T(1,128)S(1)}, u32[]{:S(2)}, u32[]{:S(2)}) collective-permute-start(f32[1,2048]{1,0:T(1,128)S(1)} %get-tuple-element.166.refs_0_), channel_id=1, source_target_pairs={{0,32},{32,0},{64,96},{96,64},{128,160},{160,128},{192,224},{224,1... | collective-permute-start | bytes 24584 | tf_op jit(solution)/shard_map/ppermute | solution.py:51
  139.0 13.6 %collective-permute-start.42 = (bf16[64,2048]{1,0:T(8,128)(2,1)S(1)}, bf16[64,2048]{1,0:T(8,128)(2,1)S(1)}, u32[]{:S(2)}, u32[]{:S(2)}) collective-permute-start(bf16[64,2048]{1,0:T(8,128)(2,1)S(1)} %get-tuple-element.167.refs_0_), channel_id=1, source_target_pairs={{0,96},{32,64},{64,32},{96,0},{128,224},{160,192},{192,160},{224,1... | collective-permute-start | bytes 786440 | tf_op jit(solution)/shard_map/ppermute | solution.py:51
  139.8 12.8 %collective-permute-start.41 = (bf16[64,2048]{1,0:T(8,128)(2,1)S(1)}, bf16[64,2048]{1,0:T(8,128)(2,1)S(1)}, u32[]{:S(2)}, u32[]{:S(2)}) collective-permute-start(bf16[64,2048]{1,0:T(8,128)(2,1)S(1)} %get-tuple-element.167.refs_0_), channel_id=1, source_target_pairs={{0,64},{32,96},{64,0},{96,32},{128,192},{160,224},{192,128},{224,1... | collective-permute-start | bytes 786440 | tf_op jit(solution)/shard_map/ppermute | solution.py:51
  141.2 11.4 %collective-permute-start.40 = (bf16[64,2048]{1,0:T(8,128)(2,1)S(1)}, bf16[64,2048]{1,0:T(8,128)(2,1)S(1)}, u32[]{:S(2)}, u32[]{:S(2)}) collective-permute-start(bf16[64,2048]{1,0:T(8,128)(2,1)S(1)} %get-tuple-element.167.refs_0_), channel_id=1, source_target_pairs={{0,32},{32,0},{64,96},{96,64},{128,160},{160,128},{192,224},{224,1... | collective-permute-start | bytes 786440 | tf_op jit(solution)/shard_map/ppermute | solution.py:51
  143.2 3.7 %collective-permute-start.43 = (f32[1,2048]{1,0:T(1,128)S(1)}, f32[1,2048]{1,0:T(1,128)S(1)}, u32[]{:S(2)}, u32[]{:S(2)}) collective-permute-start(f32[1,2048]{1,0:T(1,128)S(1)} %get-tuple-element.168.refs_0_), channel_id=1, source_target_pairs={{0,16},{1,17},{2,18},{3,19},{4,20},{5,21},{6,22},{7,23},{8,24},{9,... | collective-permute-start | bytes 24584 | tf_op jit(solution)/shard_map/ppermute | solution.py:43
  146.9 5.2 %collective-permute-start.44 = (f32[1,2048]{1,0:T(1,128)S(1)}, f32[1,2048]{1,0:T(1,128)S(1)}, u32[]{:S(2)}, u32[]{:S(2)}) collective-permute-start(f32[1,2048]{1,0:T(1,128)S(1)} %add.6.refs_0_), channel_id=1, source_target_pairs={{0,128},{32,160},{64,192},{96,224},{128,0},{160,32},{192,64},{224,... | collective-permute-start | bytes 24584 | tf_op jit(solution)/shard_map/ppermute | solution.py:51

commit v5 on v2

--- a/solution.py
+++ b/solution.py
@@ -219,7 +219,9 @@
         norm_block(refs[index], gain_ref, refs[count + 2 * index], refs[count + 2 * index + 1])
 
 
-def encoder_kernel(map_ref, gain_ref, cot_ref, a_ref, b_ref, dh_ref, gp_ref, full_ref):
+def encoder_kernel(map_ref, gain_ref, cot_ref, a_ref, b_ref, dh_ref, gp_ref, full_ref, flag_ref):
+    flag_ref[...] = jnp.where(is_encoder(map_ref), 1.0, 0.0) * jnp.ones_like(flag_ref)
+
     @pl.when(is_encoder(map_ref))
     def _():
         y = y_index()
@@ -404,12 +406,14 @@
     dh_ref[...] = (sum_ref[...] + got_ref[...].astype(f32)).astype(bf16)
 
 
-def out_kernel(offset, map_ref, own_ref, oth_ref, *refs):
+def out_kernel(offset, flag_ref, own_ref, oth_ref, *refs):
     *parts, out_ref, sems = refs
     core, y = core_index(), y_index()
     rows = LEN // len(parts)
 
-    @pl.when(jnp.logical_not(is_encoder(map_ref)))
+    encoder = jnp.max(flag_ref[...]) > 0.5
+
+    @pl.when(jnp.logical_not(encoder))
     def _():
         copies = [
             pltpu.make_async_copy(
@@ -424,7 +428,7 @@
         for copy in copies:
             copy.wait()
 
-    @pl.when(is_encoder(map_ref))
+    @pl.when(encoder)
     def _():
         copies = []
         for index, part in enumerate(parts):
@@ -441,7 +445,7 @@
 def put_out(offset, where, own, oth, parts, name):
     return pl.pallas_call(
         functools.partial(out_kernel, offset),
-        in_specs=[SMEM] + [ANY] * (2 + len(parts)),
+        in_specs=[VMEM] + [ANY] * (2 + len(parts)),
         out_specs=ANY,
         out_shape=jax.ShapeDtypeStruct((LEN, D), bf16),
         scratch_shapes=[pltpu.SemaphoreType.DMA((4,))],
@@ -472,15 +476,14 @@
     up, down, across = from_above(a[0]), from_below(a[0]), other_column(a[0])
     qg_oth = other_core(copy_call(give_kernel, bf16_rows(LEN), (rows, cot, a[0]), "give", 2))
 
+    a[1], qg_oth = order.take(up, qg_oth)
+    up, across_1 = from_above(a[1]), other_column(a[1])
+    a[-1] = order.take(down)
+    down = from_below(a[-1])
     hidden = order.take(hidden)
     mine, send = select(0, rows, hidden)
     hidden = other_y(send, 1)
-
-    a[1] = order.take(up)
-    up, across_1 = from_above(a[1]), other_column(a[1])
-    a[-1] = order.take(down)
-    down = from_below(a[-1])
-    b[0], qg_oth = order.take(across, qg_oth)
+    b[0] = order.take(across)
     hidden = order.take(hidden)
     mine = select(1, mine, hidden)
     hidden = other_high(mine)
@@ -523,9 +526,9 @@
 
     enc_0, inv_0, enc_1, inv_1 = normalise(own_a, own_b)
     enc_2, inv_2, enc_3, inv_3 = normalise(oth_a, oth_b)
-    dh_enc, gp_enc, enc_out = small_call(
-        encoder_kernel, [bf16_rows(LEN), LINE, bf16_rows(LEN)], (gain, cot, own_a, own_b), "encoder",
-        where=section_map,
+    dh_enc, gp_enc, enc_out, flag = small_call(
+        encoder_kernel, [bf16_rows(LEN), LINE, bf16_rows(LEN), jax.ShapeDtypeStruct((8, 128), f32)],
+        (gain, cot, own_a, own_b), "encoder", where=section_map,
     )
     pieces = (enc_0, enc_1, enc_2, enc_3, own_a, own_b, oth_a, oth_b, inv_0, inv_1, inv_2, inv_3)
     own_out, oth_out, dh_own, dh_oth, gp = attend(
@@ -561,8 +564,8 @@
     gain_part = add_from(gain_part, other_column)
     gain_part = add_from(gain_part, other_high)
     dhs = [dh, near, far, other]
-    section_out = put_out(0, section_map, own_out, got_out, [enc_out], "rows")
-    section_grad = put_out(F, section_map, own_out, got_out, dhs, "grads")
+    section_out = put_out(0, flag, own_out, got_out, [enc_out], "rows")
+    section_grad = put_out(F, flag, own_out, got_out, dhs, "grads")
     return (section_out[None], section_grad[None], gain_part.reshape(D))
 
 

time: 150 us -> 149 us (level)
  starting transfers between devices: 50.3 us -> 54.3 us
  waiting for transfers between devices: 71.8 us -> 69 us
    ppermute x16, starting transfers between devices: 23.6 us -> 28.8 us  [section_swap(): return lax.ppermute(x, 'section', pairs)]
    ppermute x16, waiting for transfers between devices: 27 us -> 22.5 us  [section_swap(): return lax.ppermute(x, 'section', pairs)]
    ppermute x26, waiting for transfers between devices: 44.8 us -> 46.5 us  [dp_swap(): return lax.ppermute(x, 'dp', pairs)]
  transfers between devices with their start and end apart: 42 -> 42, of which waited for: 20 -> 21; matrix products, arithmetic and copies ran while one was open for 0% -> 0% of each run, Pallas kernels for 4% -> 3%
where the time goes in v5:
time: 149 us
  waiting for transfers between devices  69 us (46%)
  starting transfers between devices  54.3 us (36%)
  Pallas kernels  22.3 us (15%)
  local copies, waits for them, and re-layouts  2.36 us (2%)
    ppermute x26, waiting for transfers between devices, dp_swap(): return lax.ppermute(x, 'dp', pairs)  46.5 us
    ppermute x16, starting transfers between devices, section_swap(): return lax.ppermute(x, 'section', pairs)  28.8 us
    ppermute x26, starting transfers between devices, dp_swap(): return lax.ppermute(x, 'dp', pairs)  25.5 us
    ppermute x16, waiting for transfers between devices, section_swap(): return lax.ppermute(x, 'section', pairs)  22.5 us
    pallas_call x1, Pallas kernels, attend(): pl.pallas_call(main_kernel, in_specs=[VMEM] * (N_SLOT + 12) + [SMEM] + [V...  14.7 us
    pallas_call x16, Pallas kernels, small_call(): pl.pallas_call(kernel, in_specs=[SMEM] * len(first) + [VMEM] * len(args),...  4.94 us
  transfers between devices with their start and end apart: 42, of which 21 were waited for; matrix products, arithmetic and copies ran while one was open for 0% of the time, Pallas kernels for 3%

profile of v5, /device:TPU:6, one launch (start us, length us, event | category | flops | bytes accessed | tf_op | source)
XLA Modules:
  0.0 149.0 jit_solution(13312954128277720862)
XLA Ops:
  0.6 1.1 copy-done.3
  1.8 0.1 columns.1
  2.0 1.5 %collective-permute-done.1.got_ref = bf16[64,2048]{1,0:T(8,128)(2,1)S(1)} collective-permute-done((bf16[64,2048]{1,0:T(8,128)(2,1)S(1)}, bf16[64,2048]{1,0:T(8,128)(2,1)S(1)}, u32[]{:S(2)}, u32[]{:S(2)}) %collective-permute-start.1) | collective-permute-done | bytes 262176 | tf_op jit(solution)/shard_map/ppermute | solution.py:42
  3.6 1.2 copy-done.1
  4.8 0.1 give.1
  5.0 0.2 collective-permute-start.4
  5.2 5.9 %collective-permute-start.3 = (bf16[128,2048]{1,0:T(8,128)(2,1)S(1)}, bf16[128,2048]{1,0:T(8,128)(2,1)S(1)}, u32[]{:S(2)}, u32[]{:S(2)}) collective-permute-start(bf16[128,2048]{1,0:T(8,128)(2,1)S(1)} %unit.1.token_ref.refs_0_), channel_id=1, source_target_pairs={{0,14},{1,15},{2,0},{3,1},{4,2},{5,3},{6,4},{7,5},{8,6},{9,7},{10,... | collective-permute-start | bytes 1572872 | tf_op jit(solution)/shard_map/ppermute | solution.py:42
  11.1 3.3 %collective-permute-start = (bf16[128,2048]{1,0:T(8,128)(2,1)S(1)}, bf16[128,2048]{1,0:T(8,128)(2,1)S(1)}, u32[]{:S(2)}, u32[]{:S(2)}) collective-permute-start(bf16[128,2048]{1,0:T(8,128)(2,1)S(1)} %half.1), channel_id=1, source_target_pairs={{0,64},{32,96},{64,0},{96,32},{128,192},{160,224},{192,128},{224,1... | collective-permute-start | bytes 1572872 | tf_op jit(solution)/shard_map/ppermute | solution.py:50
  14.4 0.8 collective-permute-start.6
  15.2 7.6 %collective-permute-done.3.refs_0_ = bf16[128,2048]{1,0:T(8,128)(2,1)S(1)} collective-permute-done((bf16[128,2048]{1,0:T(8,128)(2,1)S(1)}, bf16[128,2048]{1,0:T(8,128)(2,1)S(1)}, u32[]{:S(2)}, u32[]{:S(2)}) %collective-permute-start.3) | collective-permute-done | bytes 524320 | tf_op jit(solution)/shard_map/ppermute | solution.py:42
  22.8 3.7 %collective-permute-start.10 = (bf16[128,2048]{1,0:T(8,128)(2,1)S(1)}, bf16[128,2048]{1,0:T(8,128)(2,1)S(1)}, u32[]{:S(2)}, u32[]{:S(2)}) collective-permute-start(bf16[128,2048]{1,0:T(8,128)(2,1)S(1)} %get-tuple-element.97.refs_1_), channel_id=1, source_target_pairs={{0,14},{1,15},{2,0},{3,1},{4,2},{5,3},{6,4},{7,5},{8,6},{9,7},{10,... | collective-permute-start | bytes 1572872 | tf_op jit(solution)/shard_map/ppermute | solution.py:42
  26.5 0.1 collective-permute-done.refs_0_
  26.6 0.6 select.3
  27.3 1.7 %collective-permute-start.5 = (bf16[64,2048]{1,0:T(8,128)(2,1)S(1)}, bf16[64,2048]{1,0:T(8,128)(2,1)S(1)}, u32[]{:S(2)}, u32[]{:S(2)}) collective-permute-start(bf16[64,2048]{1,0:T(8,128)(2,1)S(1)} %get-tuple-element.93), channel_id=1, source_target_pairs={{0,32},{32,0},{64,96},{96,64},{128,160},{160,128},{192,224},{224,1... | collective-permute-start | bytes 786440 | tf_op jit(solution)/shard_map/ppermute | solution.py:50
  28.9 0.8 collective-permute-start.8
  29.8 5.1 %collective-permute-done.5.refs_0_ = bf16[64,2048]{1,0:T(8,128)(2,1)S(1)} collective-permute-done((bf16[64,2048]{1,0:T(8,128)(2,1)S(1)}, bf16[64,2048]{1,0:T(8,128)(2,1)S(1)}, u32[]{:S(2)}, u32[]{:S(2)}) %collective-permute-start.5) | collective-permute-done | bytes 262176 | tf_op jit(solution)/shard_map/ppermute | solution.py:50
  34.9 2.6 %collective-permute-done.10.refs_0_ = bf16[128,2048]{1,0:T(8,128)(2,1)S(1)} collective-permute-done((bf16[128,2048]{1,0:T(8,128)(2,1)S(1)}, bf16[128,2048]{1,0:T(8,128)(2,1)S(1)}, u32[]{:S(2)}, u32[]{:S(2)}) %collective-permute-start.10) | collective-permute-done | bytes 524320 | tf_op jit(solution)/shard_map/ppermute | solution.py:42
  37.5 3.7 %collective-permute-start.14 = (bf16[128,2048]{1,0:T(8,128)(2,1)S(1)}, bf16[128,2048]{1,0:T(8,128)(2,1)S(1)}, u32[]{:S(2)}, u32[]{:S(2)}) collective-permute-start(bf16[128,2048]{1,0:T(8,128)(2,1)S(1)} %get-tuple-element.105.refs_4_), channel_id=1, source_target_pairs={{0,14},{1,15},{2,0},{3,1},{4,2},{5,3},{6,4},{7,5},{8,6},{9,7},{10,... | collective-permute-start | bytes 1572872 | tf_op jit(solution)/shard_map/ppermute | solution.py:42
  41.2 0.6 select.4.own_ref
  41.8 1.5 %collective-permute-start.7 = (bf16[64,2048]{1,0:T(8,128)(2,1)S(1)}, bf16[64,2048]{1,0:T(8,128)(2,1)S(1)}, u32[]{:S(2)}, u32[]{:S(2)}) collective-permute-start(bf16[64,2048]{1,0:T(8,128)(2,1)S(1)} %select.4.own_ref), channel_id=1, source_target_pairs={{0,128},{32,160},{64,192},{96,224},{128,0},{160,32},{192,64},{224,... | collective-permute-start | bytes 786440 | tf_op jit(solution)/shard_map/ppermute | solution.py:50
  43.3 9.3 %collective-permute-done.7.refs_0_ = bf16[64,2048]{1,0:T(8,128)(2,1)S(1)} collective-permute-done((bf16[64,2048]{1,0:T(8,128)(2,1)S(1)}, bf16[64,2048]{1,0:T(8,128)(2,1)S(1)}, u32[]{:S(2)}, u32[]{:S(2)}) %collective-permute-start.7) | collective-permute-done | bytes 262176 | tf_op jit(solution)/shard_map/ppermute | solution.py:50
  52.6 0.6 select.5.refs_0_
  53.2 1.7 %collective-permute-start.11 = (bf16[64,2048]{1,0:T(8,128)(2,1)S(1)}, bf16[64,2048]{1,0:T(8,128)(2,1)S(1)}, u32[]{:S(2)}, u32[]{:S(2)}) collective-permute-start(bf16[64,2048]{1,0:T(8,128)(2,1)S(1)} %select.5.refs_0_), channel_id=1, source_target_pairs={{0,32},{32,0},{64,96},{96,64},{128,160},{160,128},{192,224},{224,1... | collective-permute-start | bytes 786440 | tf_op jit(solution)/shard_map/ppermute | solution.py:50
  55.0 3.3 %collective-permute-start.17 = (bf16[128,2048]{1,0:T(8,128)(2,1)S(1)}, bf16[128,2048]{1,0:T(8,128)(2,1)S(1)}, u32[]{:S(2)}, u32[]{:S(2)}) collective-permute-start(bf16[128,2048]{1,0:T(8,128)(2,1)S(1)} %get-tuple-element.112.refs_6_), channel_id=1, source_target_pairs={{0,14},{1,15},{2,0},{3,1},{4,2},{5,3},{6,4},{7,5},{8,6},{9,7},{10,... | collective-permute-start | bytes 1572872 | tf_op jit(solution)/shard_map/ppermute | solution.py:42
  58.3 0.8 collective-permute-start.16
  59.1 2.2 %collective-permute-done.12.refs_0_ = bf16[128,2048]{1,0:T(8,128)(2,1)S(1)} collective-permute-done((bf16[128,2048]{1,0:T(8,128)(2,1)S(1)}, bf16[128,2048]{1,0:T(8,128)(2,1)S(1)}, u32[]{:S(2)}, u32[]{:S(2)}) %collective-permute-start.12) | collective-permute-done | bytes 524320 | tf_op jit(solution)/shard_map/ppermute | solution.py:42
  61.3 3.3 %collective-permute-start.15 = (bf16[128,2048]{1,0:T(8,128)(2,1)S(1)}, bf16[128,2048]{1,0:T(8,128)(2,1)S(1)}, u32[]{:S(2)}, u32[]{:S(2)}) collective-permute-start(bf16[128,2048]{1,0:T(8,128)(2,1)S(1)} %stack.1.a_ref.refs_0_.refs_20_), channel_id=1, source_target_pairs={{0,64},{32,96},{64,0},{96,32},{128,192},{160,224},{192,128},{224,1... | collective-permute-start | bytes 1572872 | tf_op jit(solution)/shard_map/ppermute | solution.py:50
  64.6 6.4 %collective-permute-done.18.refs_0_ = bf16[128,2048]{1,0:T(8,128)(2,1)S(1)} collective-permute-done((bf16[128,2048]{1,0:T(8,128)(2,1)S(1)}, bf16[128,2048]{1,0:T(8,128)(2,1)S(1)}, u32[]{:S(2)}, u32[]{:S(2)}) %collective-permute-start.18) | collective-permute-done | bytes 524320 | tf_op jit(solution)/shard_map/ppermute | solution.py:42
  71.1 2.0 %collective-permute-done.16.refs_0_ = bf16[128,2048]{1,0:T(8,128)(2,1)S(1)} collective-permute-done((bf16[128,2048]{1,0:T(8,128)(2,1)S(1)}, bf16[128,2048]{1,0:T(8,128)(2,1)S(1)}, u32[]{:S(2)}, u32[]{:S(2)}) %collective-permute-start.16) | collective-permute-done | bytes 524320 | tf_op jit(solution)/shard_map/ppermute | solution.py:42
  73.1 0.2 collective-permute-done.15.refs_0_
  73.5 0.5 collective-permute-start.23
  74.0 0.7 norm.2
  74.7 0.6 encoder.1
  75.3 5.0 %collective-permute-done.19.refs_0_ = bf16[128,2048]{1,0:T(8,128)(2,1)S(1)} collective-permute-done((bf16[128,2048]{1,0:T(8,128)(2,1)S(1)}, bf16[128,2048]{1,0:T(8,128)(2,1)S(1)}, u32[]{:S(2)}, u32[]{:S(2)}) %collective-permute-start.19) | collective-permute-done | bytes 524320 | tf_op jit(solution)/shard_map/ppermute | solution.py:42
  80.3 1.2 collective-permute-done.21.refs_0_
  81.6 0.7 norm.3
  82.3 14.7 %attend.1 = (bf16[256,2048]{1,0:T(8,128)(2,1)S(1)}, bf16[256,2048]{1,0:T(8,128)(2,1)S(1)}, bf16[256,2048]{1,0:T(8,128)(2,1)S(1)}, bf16[272,2048]{1,0:T(8,128)(2,1)S(1)}, f32[1,2048]{1,0:T(1,128)S(1)}) custom-call(bf16[128,2048]{1,0:T(8,128)(2,1)S(1)} %unit.1.token_ref.refs_0_, bf16[128,2048]{1,0:T(8,128)(2,1)S(1)} %get-tuple-element.97.refs_1_, ...), custom_call_target="tpu_custom_call" | custom-call | flops 10000000000 | bytes 20000000 | tf_op jit(solution)/shard_map/attend/pallas_call | solution.py:335
  97.0 0.3 collective-permute-start.24
  97.3 0.5 collective-permute-start.25
  97.8 2.2 %collective-permute-done.24.got_ref = bf16[272,2048]{1,0:T(8,128)(2,1)S(1)} collective-permute-done((bf16[272,2048]{1,0:T(8,128)(2,1)S(1)}, bf16[272,2048]{1,0:T(8,128)(2,1)S(1)}, u32[]{:S(2)}, u32[]{:S(2)}) %collective-permute-start.24) | collective-permute-done | bytes 1114144 | tf_op jit(solution)/shard_map/ppermute | solution.py:42
  100.1 0.3 split.1
  100.5 4.5 %collective-permute-start.27 = (bf16[64,2048]{1,0:T(8,128)(2,1)S(1)}, bf16[64,2048]{1,0:T(8,128)(2,1)S(1)}, u32[]{:S(2)}, u32[]{:S(2)}) collective-permute-start(bf16[64,2048]{1,0:T(8,128)(2,1)S(1)} %get-tuple-element.156), channel_id=1, source_target_pairs={{0,64},{32,96},{64,0},{96,32},{128,192},{160,224},{192,128},{224,1... | collective-permute-start | bytes 786440 | tf_op jit(solution)/shard_map/ppermute | solution.py:50
  104.9 0.2 collective-permute-start.28
  105.2 2.2 %collective-permute-start.31 = (f32[1,2048]{1,0:T(1,128)S(1)}, f32[1,2048]{1,0:T(1,128)S(1)}, u32[]{:S(2)}, u32[]{:S(2)}) collective-permute-start(f32[1,2048]{1,0:T(1,128)S(1)} %get-tuple-element.158.a_ref), channel_id=1, source_target_pairs={{0,6},{1,7},{2,4},{3,5},{4,2},{5,3},{6,0},{7,1},{8,14},{9,15},{10,... | collective-permute-start | bytes 24584 | tf_op jit(solution)/shard_map/ppermute | solution.py:42
  107.4 3.2 %collective-permute-done.31.d_ref = f32[1,2048]{1,0:T(1,128)S(1)} collective-permute-done((f32[1,2048]{1,0:T(1,128)S(1)}, f32[1,2048]{1,0:T(1,128)S(1)}, u32[]{:S(2)}, u32[]{:S(2)}) %collective-permute-start.31) | collective-permute-done | bytes 8224 | tf_op jit(solution)/shard_map/ppermute | solution.py:42
  110.6 1.3 collective-permute-done.30.c_ref
  111.9 2.3 %collective-permute-done.29.b_ref = f32[1,2048]{1,0:T(1,128)S(1)} collective-permute-done((f32[1,2048]{1,0:T(1,128)S(1)}, f32[1,2048]{1,0:T(1,128)S(1)}, u32[]{:S(2)}, u32[]{:S(2)}) %collective-permute-start.29) | collective-permute-done | bytes 8224 | tf_op jit(solution)/shard_map/ppermute | solution.py:42
  114.3 2.4 %collective-permute-start.32 = (f32[1,2048]{1,0:T(1,128)S(1)}, f32[1,2048]{1,0:T(1,128)S(1)}, u32[]{:S(2)}, u32[]{:S(2)}) collective-permute-start(f32[1,2048]{1,0:T(1,128)S(1)} %add.5.a_ref), channel_id=1, source_target_pairs={{0,8},{1,9},{2,10},{3,11},{4,12},{5,13},{6,14},{7,15},{8,0},{9,1},... | collective-permute-start | bytes 24584 | tf_op jit(solution)/shard_map/ppermute | solution.py:42
  116.6 5.2 %collective-permute-done.32.b_ref = f32[1,2048]{1,0:T(1,128)S(1)} collective-permute-done((f32[1,2048]{1,0:T(1,128)S(1)}, f32[1,2048]{1,0:T(1,128)S(1)}, u32[]{:S(2)}, u32[]{:S(2)}) %collective-permute-start.32) | collective-permute-done | bytes 8224 | tf_op jit(solution)/shard_map/ppermute | solution.py:42
  121.9 0.1 sum.1
  122.0 3.7 %collective-permute-start.33 = (bf16[64,2048]{1,0:T(8,128)(2,1)S(1)}, bf16[64,2048]{1,0:T(8,128)(2,1)S(1)}, u32[]{:S(2)}, u32[]{:S(2)}) collective-permute-start(bf16[64,2048]{1,0:T(8,128)(2,1)S(1)} %get-tuple-element.165), channel_id=1, source_target_pairs={{0,128},{32,160},{64,192},{96,224},{128,0},{160,32},{192,64},{224,... | collective-permute-start | bytes 786440 | tf_op jit(solution)/shard_map/ppermute | solution.py:50
  125.7 3.0 %collective-permute-start.36 = (f32[1,2048]{1,0:T(1,128)S(1)}, f32[1,2048]{1,0:T(1,128)S(1)}, u32[]{:S(2)}, u32[]{:S(2)}) collective-permute-start(f32[1,2048]{1,0:T(1,128)S(1)} %get-tuple-element.166.a_ref), channel_id=1, source_target_pairs={{0,96},{32,64},{64,32},{96,0},{128,224},{160,192},{192,160},{224,1... | collective-permute-start | bytes 24584 | tf_op jit(solution)/shard_map/ppermute | solution.py:50
  128.7 1.1 collective-permute-start.34
  129.8 0.8 collective-permute-done.36.d_ref
  130.6 3.5 %collective-permute-done.35.c_ref = f32[1,2048]{1,0:T(1,128)S(1)} collective-permute-done((f32[1,2048]{1,0:T(1,128)S(1)}, f32[1,2048]{1,0:T(1,128)S(1)}, u32[]{:S(2)}, u32[]{:S(2)}) %collective-permute-start.35) | collective-permute-done | bytes 8224 | tf_op jit(solution)/shard_map/ppermute | solution.py:50
  134.1 0.8 collective-permute-start.39
  134.9 1.4 collective-permute-start.38
  136.2 2.1 %collective-permute-start.37 = (bf16[64,2048]{1,0:T(8,128)(2,1)S(1)}, bf16[64,2048]{1,0:T(8,128)(2,1)S(1)}, u32[]{:S(2)}, u32[]{:S(2)}) collective-permute-start(bf16[64,2048]{1,0:T(8,128)(2,1)S(1)} %get-tuple-element.167.refs_0_), channel_id=1, source_target_pairs={{0,32},{32,0},{64,96},{96,64},{128,160},{160,128},{192,224},{224,1... | collective-permute-start | bytes 786440 | tf_op jit(solution)/shard_map/ppermute | solution.py:50
  138.3 3.6 %collective-permute-done.40.b_ref = f32[1,2048]{1,0:T(1,128)S(1)} collective-permute-done((f32[1,2048]{1,0:T(1,128)S(1)}, f32[1,2048]{1,0:T(1,128)S(1)}, u32[]{:S(2)}, u32[]{:S(2)}) %collective-permute-start.40) | collective-permute-done | bytes 8224 | tf_op jit(solution)/shard_map/ppermute | solution.py:42
  142.0 0.6 collective-permute-start.41
  142.6 1.1 rows.1
  143.7 3.4 %collective-permute-done.41.b_ref = f32[1,2048]{1,0:T(1,128)S(1)} collective-permute-done((f32[1,2048]{1,0:T(1,128)S(1)}, f32[1,2048]{1,0:T(1,128)S(1)}, u32[]{:S(2)}, u32[]{:S(2)}) %collective-permute-start.41) | collective-permute-done | bytes 8224 | tf_op jit(solution)/shard_map/ppermute | solution.py:50
  147.1 0.6 add.9
  147.7 1.1 grads.1
  (78 shorter events, 0.8 us)
Async XLA Ops:
  0.6 3.0 %copy-start = (bf16[1,256,2048]{2,1,0:T(8,128)(2,1)S(1)}, bf16[1,256,2048]{2,1,0:T(8,128)(2,1)}, u32[]{:S(2)}) copy-start(bf16[1,256,2048]{2,1,0:T(8,128)(2,1)} %param.5) | copy-start | bytes 3145732
  0.6 1.1 copy-start.3
  1.9 1.6 %collective-permute-start.1 = (bf16[64,2048]{1,0:T(8,128)(2,1)S(1)}, bf16[64,2048]{1,0:T(8,128)(2,1)S(1)}, u32[]{:S(2)}, u32[]{:S(2)}) collective-permute-start(bf16[64,2048]{1,0:T(8,128)(2,1)S(1)} %get-tuple-element.87), channel_id=1, source_target_pairs={{0,1},{1,0},{2,3},{3,2},{4,5},{5,4},{6,7},{7,6},{8,9},{9,8},{10,11... | collective-permute-start | bytes 786440 | tf_op jit(solution)/shard_map/ppermute | solution.py:42
  3.6 1.2 copy-start.1
  5.0 17.8 %collective-permute-start.4 = (bf16[256,2048]{1,0:T(8,128)(2,1)S(1)}, bf16[256,2048]{1,0:T(8,128)(2,1)S(1)}, u32[]{:S(2)}, u32[]{:S(2)}) collective-permute-start(bf16[256,2048]{1,0:T(8,128)(2,1)S(1)} %give.1), channel_id=1, source_target_pairs={{0,1},{1,0},{2,3},{3,2},{4,5},{5,4},{6,7},{7,6},{8,9},{9,8},{10,11... | collective-permute-start | bytes 3145736 | tf_op jit(solution)/shard_map/ppermute | solution.py:42
  5.2 17.6 %collective-permute-start.3 = (bf16[128,2048]{1,0:T(8,128)(2,1)S(1)}, bf16[128,2048]{1,0:T(8,128)(2,1)S(1)}, u32[]{:S(2)}, u32[]{:S(2)}) collective-permute-start(bf16[128,2048]{1,0:T(8,128)(2,1)S(1)} %unit.1.token_ref.refs_0_), channel_id=1, source_target_pairs={{0,14},{1,15},{2,0},{3,1},{4,2},{5,3},{6,4},{7,5},{8,6},{9,7},{10,... | collective-permute-start | bytes 1572872 | tf_op jit(solution)/shard_map/ppermute | solution.py:42
  11.0 15.5 %collective-permute-start.2 = (bf16[128,2048]{1,0:T(8,128)(2,1)S(1)}, bf16[128,2048]{1,0:T(8,128)(2,1)S(1)}, u32[]{:S(2)}, u32[]{:S(2)}) collective-permute-start(bf16[128,2048]{1,0:T(8,128)(2,1)S(1)} %unit.1.token_ref.refs_0_), channel_id=1, source_target_pairs={{0,2},{1,3},{2,4},{3,5},{4,6},{5,7},{6,8},{7,9},{8,10},{9,11},{10,... | collective-permute-start | bytes 1572872 | tf_op jit(solution)/shard_map/ppermute | solution.py:42
  11.1 15.6 %collective-permute-start = (bf16[128,2048]{1,0:T(8,128)(2,1)S(1)}, bf16[128,2048]{1,0:T(8,128)(2,1)S(1)}, u32[]{:S(2)}, u32[]{:S(2)}) collective-permute-start(bf16[128,2048]{1,0:T(8,128)(2,1)S(1)} %half.1), channel_id=1, source_target_pairs={{0,64},{32,96},{64,0},{96,32},{128,192},{160,224},{192,128},{224,1... | collective-permute-start | bytes 1572872 | tf_op jit(solution)/shard_map/ppermute | solution.py:50
  14.4 15.4 %collective-permute-start.6 = (bf16[128,2048]{1,0:T(8,128)(2,1)S(1)}, bf16[128,2048]{1,0:T(8,128)(2,1)S(1)}, u32[]{:S(2)}, u32[]{:S(2)}) collective-permute-start(bf16[128,2048]{1,0:T(8,128)(2,1)S(1)} %unit.1.token_ref.refs_0_), channel_id=1, source_target_pairs={{0,16},{1,17},{2,18},{3,19},{4,20},{5,21},{6,22},{7,23},{8,24},{9,... | collective-permute-start | bytes 1572872 | tf_op jit(solution)/shard_map/ppermute | solution.py:42
  22.8 3.9 %copy-start.5 = (s32[8]{0:T(128)S(1)}, s32[8]{0:T(128)}, u32[]{:S(2)}) copy-start(s32[8]{0:T(128)} %refs_28_.1) | copy-start | bytes 100
  22.8 14.7 %collective-permute-start.10 = (bf16[128,2048]{1,0:T(8,128)(2,1)S(1)}, bf16[128,2048]{1,0:T(8,128)(2,1)S(1)}, u32[]{:S(2)}, u32[]{:S(2)}) collective-permute-start(bf16[128,2048]{1,0:T(8,128)(2,1)S(1)} %get-tuple-element.97.refs_1_), channel_id=1, source_target_pairs={{0,14},{1,15},{2,0},{3,1},{4,2},{5,3},{6,4},{7,5},{8,6},{9,7},{10,... | collective-permute-start | bytes 1572872 | tf_op jit(solution)/shard_map/ppermute | solution.py:42
  26.5 14.7 %collective-permute-start.9 = (bf16[128,2048]{1,0:T(8,128)(2,1)S(1)}, bf16[128,2048]{1,0:T(8,128)(2,1)S(1)}, u32[]{:S(2)}, u32[]{:S(2)}) collective-permute-start(bf16[128,2048]{1,0:T(8,128)(2,1)S(1)} %get-tuple-element.98.refs_2_), channel_id=1, source_target_pairs={{0,2},{1,3},{2,4},{3,5},{4,6},{5,7},{6,8},{7,9},{8,10},{9,11},{10,... | collective-permute-start | bytes 1572872 | tf_op jit(solution)/shard_map/ppermute | solution.py:42
  27.3 7.6 %collective-permute-start.5 = (bf16[64,2048]{1,0:T(8,128)(2,1)S(1)}, bf16[64,2048]{1,0:T(8,128)(2,1)S(1)}, u32[]{:S(2)}, u32[]{:S(2)}) collective-permute-start(bf16[64,2048]{1,0:T(8,128)(2,1)S(1)} %get-tuple-element.93), channel_id=1, source_target_pairs={{0,32},{32,0},{64,96},{96,64},{128,160},{160,128},{192,224},{224,1... | collective-permute-start | bytes 786440 | tf_op jit(solution)/shard_map/ppermute | solution.py:50
  28.9 14.3 %collective-permute-start.8 = (bf16[128,2048]{1,0:T(8,128)(2,1)S(1)}, bf16[128,2048]{1,0:T(8,128)(2,1)S(1)}, u32[]{:S(2)}, u32[]{:S(2)}) collective-permute-start(bf16[128,2048]{1,0:T(8,128)(2,1)S(1)} %get-tuple-element.97.refs_1_), channel_id=1, source_target_pairs={{0,16},{1,17},{2,18},{3,19},{4,20},{5,21},{6,22},{7,23},{8,24},{9,... | collective-permute-start | bytes 1572872 | tf_op jit(solution)/shard_map/ppermute | solution.py:42
  37.5 17.4 %collective-permute-start.14 = (bf16[128,2048]{1,0:T(8,128)(2,1)S(1)}, bf16[128,2048]{1,0:T(8,128)(2,1)S(1)}, u32[]{:S(2)}, u32[]{:S(2)}) collective-permute-start(bf16[128,2048]{1,0:T(8,128)(2,1)S(1)} %get-tuple-element.105.refs_4_), channel_id=1, source_target_pairs={{0,14},{1,15},{2,0},{3,1},{4,2},{5,3},{6,4},{7,5},{8,6},{9,7},{10,... | collective-permute-start | bytes 1572872 | tf_op jit(solution)/shard_map/ppermute | solution.py:42
  41.2 13.7 %collective-permute-start.13 = (bf16[128,2048]{1,0:T(8,128)(2,1)S(1)}, bf16[128,2048]{1,0:T(8,128)(2,1)S(1)}, u32[]{:S(2)}, u32[]{:S(2)}) collective-permute-start(bf16[128,2048]{1,0:T(8,128)(2,1)S(1)} %get-tuple-element.104.refs_5_), channel_id=1, source_target_pairs={{0,2},{1,3},{2,4},{3,5},{4,6},{5,7},{6,8},{7,9},{8,10},{9,11},{10,... | collective-permute-start | bytes 1572872 | tf_op jit(solution)/shard_map/ppermute | solution.py:42
  41.8 10.8 %collective-permute-start.7 = (bf16[64,2048]{1,0:T(8,128)(2,1)S(1)}, bf16[64,2048]{1,0:T(8,128)(2,1)S(1)}, u32[]{:S(2)}, u32[]{:S(2)}) collective-permute-start(bf16[64,2048]{1,0:T(8,128)(2,1)S(1)} %select.4.own_ref), channel_id=1, source_target_pairs={{0,128},{32,160},{64,192},{96,224},{128,0},{160,32},{192,64},{224,... | collective-permute-start | bytes 786440 | tf_op jit(solution)/shard_map/ppermute | solution.py:50
  43.3 18.0 %collective-permute-start.12 = (bf16[128,2048]{1,0:T(8,128)(2,1)S(1)}, bf16[128,2048]{1,0:T(8,128)(2,1)S(1)}, u32[]{:S(2)}, u32[]{:S(2)}) collective-permute-start(bf16[128,2048]{1,0:T(8,128)(2,1)S(1)} %get-tuple-element.104.refs_5_), channel_id=1, source_target_pairs={{0,16},{1,17},{2,18},{3,19},{4,20},{5,21},{6,22},{7,23},{8,24},{9,... | collective-permute-start | bytes 1572872 | tf_op jit(solution)/shard_map/ppermute | solution.py:42
  53.2 8.1 %collective-permute-start.11 = (bf16[64,2048]{1,0:T(8,128)(2,1)S(1)}, bf16[64,2048]{1,0:T(8,128)(2,1)S(1)}, u32[]{:S(2)}, u32[]{:S(2)}) collective-permute-start(bf16[64,2048]{1,0:T(8,128)(2,1)S(1)} %select.5.refs_0_), channel_id=1, source_target_pairs={{0,32},{32,0},{64,96},{96,64},{128,160},{160,128},{192,224},{224,1... | collective-permute-start | bytes 786440 | tf_op jit(solution)/shard_map/ppermute | solution.py:50
  54.9 16.2 %collective-permute-start.18 = (bf16[128,2048]{1,0:T(8,128)(2,1)S(1)}, bf16[128,2048]{1,0:T(8,128)(2,1)S(1)}, u32[]{:S(2)}, u32[]{:S(2)}) collective-permute-start(bf16[128,2048]{1,0:T(8,128)(2,1)S(1)} %get-tuple-element.111.refs_8_), channel_id=1, source_target_pairs={{0,2},{1,3},{2,4},{3,5},{4,6},{5,7},{6,8},{7,9},{8,10},{9,11},{10,... | collective-permute-start | bytes 1572872 | tf_op jit(solution)/shard_map/ppermute | solution.py:42
  55.0 16.1 %collective-permute-start.17 = (bf16[128,2048]{1,0:T(8,128)(2,1)S(1)}, bf16[128,2048]{1,0:T(8,128)(2,1)S(1)}, u32[]{:S(2)}, u32[]{:S(2)}) collective-permute-start(bf16[128,2048]{1,0:T(8,128)(2,1)S(1)} %get-tuple-element.112.refs_6_), channel_id=1, source_target_pairs={{0,14},{1,15},{2,0},{3,1},{4,2},{5,3},{6,4},{7,5},{8,6},{9,7},{10,... | collective-permute-start | bytes 1572872 | tf_op jit(solution)/shard_map/ppermute | solution.py:42
  58.3 14.9 %collective-permute-start.16 = (bf16[128,2048]{1,0:T(8,128)(2,1)S(1)}, bf16[128,2048]{1,0:T(8,128)(2,1)S(1)}, u32[]{:S(2)}, u32[]{:S(2)}) collective-permute-start(bf16[128,2048]{1,0:T(8,128)(2,1)S(1)} %get-tuple-element.111.refs_8_), channel_id=1, source_target_pairs={{0,16},{1,17},{2,18},{3,19},{4,20},{5,21},{6,22},{7,23},{8,24},{9,... | collective-permute-start | bytes 1572872 | tf_op jit(solution)/shard_map/ppermute | solution.py:42
  61.3 12.0 %collective-permute-start.15 = (bf16[128,2048]{1,0:T(8,128)(2,1)S(1)}, bf16[128,2048]{1,0:T(8,128)(2,1)S(1)}, u32[]{:S(2)}, u32[]{:S(2)}) collective-permute-start(bf16[128,2048]{1,0:T(8,128)(2,1)S(1)} %stack.1.a_ref.refs_0_.refs_20_), channel_id=1, source_target_pairs={{0,64},{32,96},{64,0},{96,32},{128,192},{160,224},{192,128},{224,1... | collective-permute-start | bytes 1572872 | tf_op jit(solution)/shard_map/ppermute | solution.py:50
  64.6 15.7 %collective-permute-start.20 = (bf16[128,2048]{1,0:T(8,128)(2,1)S(1)}, bf16[128,2048]{1,0:T(8,128)(2,1)S(1)}, u32[]{:S(2)}, u32[]{:S(2)}) collective-permute-start(bf16[128,2048]{1,0:T(8,128)(2,1)S(1)} %get-tuple-element.119.refs_3_), channel_id=1, source_target_pairs={{0,2},{1,3},{2,4},{3,5},{4,6},{5,7},{6,8},{7,9},{8,10},{9,11},{10,... | collective-permute-start | bytes 1572872 | tf_op jit(solution)/shard_map/ppermute | solution.py:42
  71.0 10.5 %collective-permute-start.21 = (bf16[128,2048]{1,0:T(8,128)(2,1)S(1)}, bf16[128,2048]{1,0:T(8,128)(2,1)S(1)}, u32[]{:S(2)}, u32[]{:S(2)}) collective-permute-start(bf16[128,2048]{1,0:T(8,128)(2,1)S(1)} %get-tuple-element.122.refs_10_), channel_id=1, source_target_pairs={{0,16},{1,17},{2,18},{3,19},{4,20},{5,21},{6,22},{7,23},{8,24},{9,... | collective-permute-start | bytes 1572872 | tf_op jit(solution)/shard_map/ppermute | solution.py:42
  71.0 2.9 %copy-start.4 = (f32[2048]{0:T(1024)S(1)}, f32[2048]{0:T(1024)}, u32[]{:S(2)}) copy-start(f32[2048]{0:T(1024)} %param.8) | copy-start | bytes 24580
  71.0 9.3 %collective-permute-start.19 = (bf16[128,2048]{1,0:T(8,128)(2,1)S(1)}, bf16[128,2048]{1,0:T(8,128)(2,1)S(1)}, u32[]{:S(2)}, u32[]{:S(2)}) collective-permute-start(bf16[128,2048]{1,0:T(8,128)(2,1)S(1)} %get-tuple-element.123.refs_11_), channel_id=1, source_target_pairs={{0,14},{1,15},{2,0},{3,1},{4,2},{5,3},{6,4},{7,5},{8,6},{9,7},{10,... | collective-permute-start | bytes 1572872 | tf_op jit(solution)/shard_map/ppermute | solution.py:42
  73.3 1.4 copy-start.2
  73.4 8.2 %collective-permute-start.22 = (bf16[128,2048]{1,0:T(8,128)(2,1)S(1)}, bf16[128,2048]{1,0:T(8,128)(2,1)S(1)}, u32[]{:S(2)}, u32[]{:S(2)}) collective-permute-start(bf16[128,2048]{1,0:T(8,128)(2,1)S(1)} %late.1), channel_id=1, source_target_pairs={{0,1},{1,0},{2,3},{3,2},{4,5},{5,4},{6,7},{7,6},{8,9},{9,8},{10,11... | collective-permute-start | bytes 1572872 | tf_op jit(solution)/shard_map/ppermute | solution.py:42
  73.5 8.1 %collective-permute-start.23 = (bf16[128,2048]{1,0:T(8,128)(2,1)S(1)}, bf16[128,2048]{1,0:T(8,128)(2,1)S(1)}, u32[]{:S(2)}, u32[]{:S(2)}) collective-permute-start(bf16[128,2048]{1,0:T(8,128)(2,1)S(1)} %get-tuple-element.117.b_ref.refs_1_.refs_21_), channel_id=1, source_target_pairs={{0,1},{1,0},{2,3},{3,2},{4,5},{5,4},{6,7},{7,6},{8,9},{9,8},{10,11... | collective-permute-start | bytes 1572872 | tf_op jit(solution)/shard_map/ppermute | solution.py:42
  97.0 3.1 %collective-permute-start.24 = (bf16[272,2048]{1,0:T(8,128)(2,1)S(1)}, bf16[272,2048]{1,0:T(8,128)(2,1)S(1)}, u32[]{:S(2)}, u32[]{:S(2)}) collective-permute-start(bf16[272,2048]{1,0:T(8,128)(2,1)S(1)} %get-tuple-element.148), channel_id=1, source_target_pairs={{0,1},{1,0},{2,3},{3,2},{4,5},{5,4},{6,7},{7,6},{8,9},{9,8},{10,11... | collective-permute-start | bytes 3342344 | tf_op jit(solution)/shard_map/ppermute | solution.py:42
  97.3 7.8 %collective-permute-start.25 = (bf16[256,2048]{1,0:T(8,128)(2,1)S(1)}, bf16[256,2048]{1,0:T(8,128)(2,1)S(1)}, u32[]{:S(2)}, u32[]{:S(2)}) collective-permute-start(bf16[256,2048]{1,0:T(8,128)(2,1)S(1)} %get-tuple-element.150), channel_id=1, source_target_pairs={{0,1},{1,0},{2,3},{3,2},{4,5},{5,4},{6,7},{7,6},{8,9},{9,8},{10,11... | collective-permute-start | bytes 3145736 | tf_op jit(solution)/shard_map/ppermute | solution.py:42
  100.4 21.5 %collective-permute-start.26 = (bf16[64,2048]{1,0:T(8,128)(2,1)S(1)}, bf16[64,2048]{1,0:T(8,128)(2,1)S(1)}, u32[]{:S(2)}, u32[]{:S(2)}) collective-permute-start(bf16[64,2048]{1,0:T(8,128)(2,1)S(1)} %get-tuple-element.155), channel_id=1, source_target_pairs={{0,32},{32,0},{64,96},{96,64},{128,160},{160,128},{192,224},{224,1... | collective-permute-start | bytes 786440 | tf_op jit(solution)/shard_map/ppermute | solution.py:50
  100.5 21.4 %collective-permute-start.27 = (bf16[64,2048]{1,0:T(8,128)(2,1)S(1)}, bf16[64,2048]{1,0:T(8,128)(2,1)S(1)}, u32[]{:S(2)}, u32[]{:S(2)}) collective-permute-start(bf16[64,2048]{1,0:T(8,128)(2,1)S(1)} %get-tuple-element.156), channel_id=1, source_target_pairs={{0,64},{32,96},{64,0},{96,32},{128,192},{160,224},{192,128},{224,1... | collective-permute-start | bytes 786440 | tf_op jit(solution)/shard_map/ppermute | solution.py:50
  104.9 16.9 %collective-permute-start.28 = (bf16[64,2048]{1,0:T(8,128)(2,1)S(1)}, bf16[64,2048]{1,0:T(8,128)(2,1)S(1)}, u32[]{:S(2)}, u32[]{:S(2)}) collective-permute-start(bf16[64,2048]{1,0:T(8,128)(2,1)S(1)} %get-tuple-element.157), channel_id=1, source_target_pairs={{0,96},{32,64},{64,32},{96,0},{128,224},{160,192},{192,160},{224,1... | collective-permute-start | bytes 786440 | tf_op jit(solution)/shard_map/ppermute | solution.py:50
  105.2 5.4 %collective-permute-start.31 = (f32[1,2048]{1,0:T(1,128)S(1)}, f32[1,2048]{1,0:T(1,128)S(1)}, u32[]{:S(2)}, u32[]{:S(2)}) collective-permute-start(f32[1,2048]{1,0:T(1,128)S(1)} %get-tuple-element.158.a_ref), channel_id=1, source_target_pairs={{0,6},{1,7},{2,4},{3,5},{4,2},{5,3},{6,0},{7,1},{8,14},{9,15},{10,... | collective-permute-start | bytes 24584 | tf_op jit(solution)/shard_map/ppermute | solution.py:42
  107.4 4.5 %collective-permute-start.30 = (f32[1,2048]{1,0:T(1,128)S(1)}, f32[1,2048]{1,0:T(1,128)S(1)}, u32[]{:S(2)}, u32[]{:S(2)}) collective-permute-start(f32[1,2048]{1,0:T(1,128)S(1)} %get-tuple-element.158.a_ref), channel_id=1, source_target_pairs={{0,4},{1,5},{2,6},{3,7},{4,0},{5,1},{6,2},{7,3},{8,12},{9,13},{10,... | collective-permute-start | bytes 24584 | tf_op jit(solution)/shard_map/ppermute | solution.py:42
  110.6 3.7 %collective-permute-start.29 = (f32[1,2048]{1,0:T(1,128)S(1)}, f32[1,2048]{1,0:T(1,128)S(1)}, u32[]{:S(2)}, u32[]{:S(2)}) collective-permute-start(f32[1,2048]{1,0:T(1,128)S(1)} %get-tuple-element.158.a_ref), channel_id=1, source_target_pairs={{0,2},{1,3},{2,0},{3,1},{4,6},{5,7},{6,4},{7,5},{8,10},{9,11},{10,... | collective-permute-start | bytes 24584 | tf_op jit(solution)/shard_map/ppermute | solution.py:42
  114.3 7.6 %collective-permute-start.32 = (f32[1,2048]{1,0:T(1,128)S(1)}, f32[1,2048]{1,0:T(1,128)S(1)}, u32[]{:S(2)}, u32[]{:S(2)}) collective-permute-start(f32[1,2048]{1,0:T(1,128)S(1)} %add.5.a_ref), channel_id=1, source_target_pairs={{0,8},{1,9},{2,10},{3,11},{4,12},{5,13},{6,14},{7,15},{8,0},{9,1},... | collective-permute-start | bytes 24584 | tf_op jit(solution)/shard_map/ppermute | solution.py:42
  122.0 12.1 %collective-permute-start.33 = (bf16[64,2048]{1,0:T(8,128)(2,1)S(1)}, bf16[64,2048]{1,0:T(8,128)(2,1)S(1)}, u32[]{:S(2)}, u32[]{:S(2)}) collective-permute-start(bf16[64,2048]{1,0:T(8,128)(2,1)S(1)} %get-tuple-element.165), channel_id=1, source_target_pairs={{0,128},{32,160},{64,192},{96,224},{128,0},{160,32},{192,64},{224,... | collective-permute-start | bytes 786440 | tf_op jit(solution)/shard_map/ppermute | solution.py:50
  125.7 4.9 %collective-permute-start.36 = (f32[1,2048]{1,0:T(1,128)S(1)}, f32[1,2048]{1,0:T(1,128)S(1)}, u32[]{:S(2)}, u32[]{:S(2)}) collective-permute-start(f32[1,2048]{1,0:T(1,128)S(1)} %get-tuple-element.166.a_ref), channel_id=1, source_target_pairs={{0,96},{32,64},{64,32},{96,0},{128,224},{160,192},{192,160},{224,1... | collective-permute-start | bytes 24584 | tf_op jit(solution)/shard_map/ppermute | solution.py:50
  128.7 5.3 %collective-permute-start.35 = (f32[1,2048]{1,0:T(1,128)S(1)}, f32[1,2048]{1,0:T(1,128)S(1)}, u32[]{:S(2)}, u32[]{:S(2)}) collective-permute-start(f32[1,2048]{1,0:T(1,128)S(1)} %get-tuple-element.166.a_ref), channel_id=1, source_target_pairs={{0,64},{32,96},{64,0},{96,32},{128,192},{160,224},{192,128},{224,1... | collective-permute-start | bytes 24584 | tf_op jit(solution)/shard_map/ppermute | solution.py:50
  128.7 5.3 %collective-permute-start.34 = (f32[1,2048]{1,0:T(1,128)S(1)}, f32[1,2048]{1,0:T(1,128)S(1)}, u32[]{:S(2)}, u32[]{:S(2)}) collective-permute-start(f32[1,2048]{1,0:T(1,128)S(1)} %get-tuple-element.166.a_ref), channel_id=1, source_target_pairs={{0,32},{32,0},{64,96},{96,64},{128,160},{160,128},{192,224},{224,1... | collective-permute-start | bytes 24584 | tf_op jit(solution)/shard_map/ppermute | solution.py:50
  134.1 13.6 %collective-permute-start.39 = (bf16[64,2048]{1,0:T(8,128)(2,1)S(1)}, bf16[64,2048]{1,0:T(8,128)(2,1)S(1)}, u32[]{:S(2)}, u32[]{:S(2)}) collective-permute-start(bf16[64,2048]{1,0:T(8,128)(2,1)S(1)} %get-tuple-element.167.refs_0_), channel_id=1, source_target_pairs={{0,96},{32,64},{64,32},{96,0},{128,224},{160,192},{192,160},{224,1... | collective-permute-start | bytes 786440 | tf_op jit(solution)/shard_map/ppermute | solution.py:50
  134.9 12.8 %collective-permute-start.38 = (bf16[64,2048]{1,0:T(8,128)(2,1)S(1)}, bf16[64,2048]{1,0:T(8,128)(2,1)S(1)}, u32[]{:S(2)}, u32[]{:S(2)}) collective-permute-start(bf16[64,2048]{1,0:T(8,128)(2,1)S(1)} %get-tuple-element.167.refs_0_), channel_id=1, source_target_pairs={{0,64},{32,96},{64,0},{96,32},{128,192},{160,224},{192,128},{224,1... | collective-permute-start | bytes 786440 | tf_op jit(solution)/shard_map/ppermute | solution.py:50
  136.2 11.5 %collective-permute-start.37 = (bf16[64,2048]{1,0:T(8,128)(2,1)S(1)}, bf16[64,2048]{1,0:T(8,128)(2,1)S(1)}, u32[]{:S(2)}, u32[]{:S(2)}) collective-permute-start(bf16[64,2048]{1,0:T(8,128)(2,1)S(1)} %get-tuple-element.167.refs_0_), channel_id=1, source_target_pairs={{0,32},{32,0},{64,96},{96,64},{128,160},{160,128},{192,224},{224,1... | collective-permute-start | bytes 786440 | tf_op jit(solution)/shard_map/ppermute | solution.py:50
  138.3 3.7 %collective-permute-start.40 = (f32[1,2048]{1,0:T(1,128)S(1)}, f32[1,2048]{1,0:T(1,128)S(1)}, u32[]{:S(2)}, u32[]{:S(2)}) collective-permute-start(f32[1,2048]{1,0:T(1,128)S(1)} %get-tuple-element.168.a_ref), channel_id=1, source_target_pairs={{0,16},{1,17},{2,18},{3,19},{4,20},{5,21},{6,22},{7,23},{8,24},{9,... | collective-permute-start | bytes 24584 | tf_op jit(solution)/shard_map/ppermute | solution.py:42
  142.0 5.2 %collective-permute-start.41 = (f32[1,2048]{1,0:T(1,128)S(1)}, f32[1,2048]{1,0:T(1,128)S(1)}, u32[]{:S(2)}, u32[]{:S(2)}) collective-permute-start(f32[1,2048]{1,0:T(1,128)S(1)} %add.8.a_ref), channel_id=1, source_target_pairs={{0,128},{32,160},{64,192},{96,224},{128,0},{160,32},{192,64},{224,... | collective-permute-start | bytes 24584 | tf_op jit(solution)/shard_map/ppermute | solution.py:50

commit v6 on v5

--- a/solution.py
+++ b/solution.py
@@ -251,7 +251,7 @@
 def main_kernel(*refs):
     units = refs[:N_SLOT]
     encs, hids, invs = refs[N_SLOT:N_SLOT + 4], refs[N_SLOT + 4:N_SLOT + 8], refs[N_SLOT + 8:N_SLOT + 12]
-    (map_ref, rows_ref, cot_ref, qg_oth, gain_ref, dh_enc, gp_enc,
+    (flag_ref, rows_ref, cot_ref, qg_oth, gain_ref, dh_enc, gp_enc,
      own_out, oth_out, dh_own, dh_oth, gp_ref, dkv, mean_ref) = refs[N_SLOT + 12:]
     mean_ref[...] = jnp.zeros_like(mean_ref)
 
@@ -292,7 +292,9 @@
     inv = jnp.concatenate([ref[:, :1] for ref in invs], axis=0)
     factor = inv * inv * (jnp.sum(mean_ref[...], axis=1, keepdims=True) * (1.0 / D))
 
-    @pl.when(jnp.logical_not(is_encoder(map_ref)))
+    encoder = jnp.max(flag_ref[...]) > 0.5
+
+    @pl.when(jnp.logical_not(encoder))
     def _():
         for block in range(N_SLOT // 2):
             w = jnp.concatenate([units[2 * block][...], units[2 * block + 1][...]], axis=0)
@@ -310,7 +312,7 @@
                     total = total + jnp.sum(scaled * hidden, axis=0, keepdims=True)
                 gp_ref[:, cols] = total
 
-    @pl.when(is_encoder(map_ref))
+    @pl.when(encoder)
     def _():
         dh_oth[...] = jnp.zeros_like(dh_oth)
         dh_own[...] = dh_enc[...]
@@ -334,7 +336,7 @@
     whole = jax.ShapeDtypeStruct((LEN, D), bf16)
     return pl.pallas_call(
         main_kernel,
-        in_specs=[VMEM] * (N_SLOT + 12) + [SMEM] + [VMEM] * 6,
+        in_specs=[VMEM] * (N_SLOT + 19),
         out_specs=[VMEM] * 5,
         out_shape=[
             whole, whole, whole, jax.ShapeDtypeStruct((LEN + 16, D), bf16), jax.ShapeDtypeStruct((1, D), f32)
@@ -532,7 +534,7 @@
     )
     pieces = (enc_0, enc_1, enc_2, enc_3, own_a, own_b, oth_a, oth_b, inv_0, inv_1, inv_2, inv_3)
     own_out, oth_out, dh_own, dh_oth, gp = attend(
-        units, pieces, section_map, rows, cot, qg_oth, gain, dh_enc, gp_enc
+        units, pieces, flag, rows, cot, qg_oth, gain, dh_enc, gp_enc
     )
 
     def add_from(part, *moves):

time: 149 us -> 148 us (level)
  transfers between devices with their start and end apart: 42 -> 42, of which waited for: 21 -> 21; matrix products, arithmetic and copies ran while one was open for 0% -> 0% of each run, Pallas kernels for 3% -> 4%
where the time goes in v6:
time: 148 us
  waiting for transfers between devices  68.6 us (46%)
  starting transfers between devices  54.5 us (37%)
  Pallas kernels  21.8 us (15%)
  local copies, waits for them, and re-layouts  2.36 us (2%)
    ppermute x26, waiting for transfers between devices, dp_swap(): return lax.ppermute(x, 'dp', pairs)  46.2 us
    ppermute x16, starting transfers between devices, section_swap(): return lax.ppermute(x, 'section', pairs)  28.8 us
    ppermute x26, starting transfers between devices, dp_swap(): return lax.ppermute(x, 'dp', pairs)  25.7 us
    ppermute x16, waiting for transfers between devices, section_swap(): return lax.ppermute(x, 'section', pairs)  22.4 us
    pallas_call x1, Pallas kernels, attend(): pl.pallas_call(main_kernel, in_specs=[VMEM] * (N_SLOT + 19), out_specs=[V...  14.2 us
    pallas_call x16, Pallas kernels, small_call(): pl.pallas_call(kernel, in_specs=[SMEM] * len(first) + [VMEM] * len(args),...  4.99 us
  transfers between devices with their start and end apart: 42, of which 21 were waited for; matrix products, arithmetic and copies ran while one was open for 0% of the time, Pallas kernels for 4%

profile of v6, /device:TPU:6, one launch (start us, length us, event | category | flops | bytes accessed | tf_op | source)
XLA Modules:
  0.0 148.3 jit_solution(9143011485740693203)
XLA Ops:
  0.6 1.1 copy-done.3
  1.8 0.1 columns.1
  2.0 1.5 %collective-permute-done.1.got_ref = bf16[64,2048]{1,0:T(8,128)(2,1)S(1)} collective-permute-done((bf16[64,2048]{1,0:T(8,128)(2,1)S(1)}, bf16[64,2048]{1,0:T(8,128)(2,1)S(1)}, u32[]{:S(2)}, u32[]{:S(2)}) %collective-permute-start.1) | collective-permute-done | bytes 262176 | tf_op jit(solution)/shard_map/ppermute | solution.py:42
  3.6 1.2 copy-done.1
  5.0 0.2 collective-permute-start.4
  5.2 5.9 %collective-permute-start.3 = (bf16[128,2048]{1,0:T(8,128)(2,1)S(1)}, bf16[128,2048]{1,0:T(8,128)(2,1)S(1)}, u32[]{:S(2)}, u32[]{:S(2)}) collective-permute-start(bf16[128,2048]{1,0:T(8,128)(2,1)S(1)} %unit.1.token_ref.refs_0_), channel_id=1, source_target_pairs={{0,14},{1,15},{2,0},{3,1},{4,2},{5,3},{6,4},{7,5},{8,6},{9,7},{10,... | collective-permute-start | bytes 1572872 | tf_op jit(solution)/shard_map/ppermute | solution.py:42
  11.1 3.3 %collective-permute-start = (bf16[128,2048]{1,0:T(8,128)(2,1)S(1)}, bf16[128,2048]{1,0:T(8,128)(2,1)S(1)}, u32[]{:S(2)}, u32[]{:S(2)}) collective-permute-start(bf16[128,2048]{1,0:T(8,128)(2,1)S(1)} %half.1), channel_id=1, source_target_pairs={{0,64},{32,96},{64,0},{96,32},{128,192},{160,224},{192,128},{224,1... | collective-permute-start | bytes 1572872 | tf_op jit(solution)/shard_map/ppermute | solution.py:50
  14.4 0.8 collective-permute-start.6
  15.2 7.5 %collective-permute-done.3.refs_0_ = bf16[128,2048]{1,0:T(8,128)(2,1)S(1)} collective-permute-done((bf16[128,2048]{1,0:T(8,128)(2,1)S(1)}, bf16[128,2048]{1,0:T(8,128)(2,1)S(1)}, u32[]{:S(2)}, u32[]{:S(2)}) %collective-permute-start.3) | collective-permute-done | bytes 524320 | tf_op jit(solution)/shard_map/ppermute | solution.py:42
  22.8 3.7 %collective-permute-start.10 = (bf16[128,2048]{1,0:T(8,128)(2,1)S(1)}, bf16[128,2048]{1,0:T(8,128)(2,1)S(1)}, u32[]{:S(2)}, u32[]{:S(2)}) collective-permute-start(bf16[128,2048]{1,0:T(8,128)(2,1)S(1)} %get-tuple-element.97.refs_1_), channel_id=1, source_target_pairs={{0,14},{1,15},{2,0},{3,1},{4,2},{5,3},{6,4},{7,5},{8,6},{9,7},{10,... | collective-permute-start | bytes 1572872 | tf_op jit(solution)/shard_map/ppermute | solution.py:42
  26.5 0.1 collective-permute-done.refs_0_
  26.6 0.6 select.3
  27.2 1.7 %collective-permute-start.5 = (bf16[64,2048]{1,0:T(8,128)(2,1)S(1)}, bf16[64,2048]{1,0:T(8,128)(2,1)S(1)}, u32[]{:S(2)}, u32[]{:S(2)}) collective-permute-start(bf16[64,2048]{1,0:T(8,128)(2,1)S(1)} %get-tuple-element.93), channel_id=1, source_target_pairs={{0,32},{32,0},{64,96},{96,64},{128,160},{160,128},{192,224},{224,1... | collective-permute-start | bytes 786440 | tf_op jit(solution)/shard_map/ppermute | solution.py:50
  28.9 0.8 collective-permute-start.8
  29.7 5.0 %collective-permute-done.5.refs_0_ = bf16[64,2048]{1,0:T(8,128)(2,1)S(1)} collective-permute-done((bf16[64,2048]{1,0:T(8,128)(2,1)S(1)}, bf16[64,2048]{1,0:T(8,128)(2,1)S(1)}, u32[]{:S(2)}, u32[]{:S(2)}) %collective-permute-start.5) | collective-permute-done | bytes 262176 | tf_op jit(solution)/shard_map/ppermute | solution.py:50
  34.8 2.6 %collective-permute-done.10.refs_0_ = bf16[128,2048]{1,0:T(8,128)(2,1)S(1)} collective-permute-done((bf16[128,2048]{1,0:T(8,128)(2,1)S(1)}, bf16[128,2048]{1,0:T(8,128)(2,1)S(1)}, u32[]{:S(2)}, u32[]{:S(2)}) %collective-permute-start.10) | collective-permute-done | bytes 524320 | tf_op jit(solution)/shard_map/ppermute | solution.py:42
  37.4 3.7 %collective-permute-start.14 = (bf16[128,2048]{1,0:T(8,128)(2,1)S(1)}, bf16[128,2048]{1,0:T(8,128)(2,1)S(1)}, u32[]{:S(2)}, u32[]{:S(2)}) collective-permute-start(bf16[128,2048]{1,0:T(8,128)(2,1)S(1)} %get-tuple-element.105.refs_4_), channel_id=1, source_target_pairs={{0,14},{1,15},{2,0},{3,1},{4,2},{5,3},{6,4},{7,5},{8,6},{9,7},{10,... | collective-permute-start | bytes 1572872 | tf_op jit(solution)/shard_map/ppermute | solution.py:42
  41.1 0.6 select.4.own_ref
  41.7 1.5 %collective-permute-start.7 = (bf16[64,2048]{1,0:T(8,128)(2,1)S(1)}, bf16[64,2048]{1,0:T(8,128)(2,1)S(1)}, u32[]{:S(2)}, u32[]{:S(2)}) collective-permute-start(bf16[64,2048]{1,0:T(8,128)(2,1)S(1)} %select.4.own_ref), channel_id=1, source_target_pairs={{0,128},{32,160},{64,192},{96,224},{128,0},{160,32},{192,64},{224,... | collective-permute-start | bytes 786440 | tf_op jit(solution)/shard_map/ppermute | solution.py:50
  43.2 9.3 %collective-permute-done.7.refs_0_ = bf16[64,2048]{1,0:T(8,128)(2,1)S(1)} collective-permute-done((bf16[64,2048]{1,0:T(8,128)(2,1)S(1)}, bf16[64,2048]{1,0:T(8,128)(2,1)S(1)}, u32[]{:S(2)}, u32[]{:S(2)}) %collective-permute-start.7) | collective-permute-done | bytes 262176 | tf_op jit(solution)/shard_map/ppermute | solution.py:50
  52.5 0.6 select.5.refs_0_
  53.1 1.7 %collective-permute-start.11 = (bf16[64,2048]{1,0:T(8,128)(2,1)S(1)}, bf16[64,2048]{1,0:T(8,128)(2,1)S(1)}, u32[]{:S(2)}, u32[]{:S(2)}) collective-permute-start(bf16[64,2048]{1,0:T(8,128)(2,1)S(1)} %select.5.refs_0_), channel_id=1, source_target_pairs={{0,32},{32,0},{64,96},{96,64},{128,160},{160,128},{192,224},{224,1... | collective-permute-start | bytes 786440 | tf_op jit(solution)/shard_map/ppermute | solution.py:50
  54.8 3.3 %collective-permute-start.17 = (bf16[128,2048]{1,0:T(8,128)(2,1)S(1)}, bf16[128,2048]{1,0:T(8,128)(2,1)S(1)}, u32[]{:S(2)}, u32[]{:S(2)}) collective-permute-start(bf16[128,2048]{1,0:T(8,128)(2,1)S(1)} %get-tuple-element.112.refs_6_), channel_id=1, source_target_pairs={{0,14},{1,15},{2,0},{3,1},{4,2},{5,3},{6,4},{7,5},{8,6},{9,7},{10,... | collective-permute-start | bytes 1572872 | tf_op jit(solution)/shard_map/ppermute | solution.py:42
  58.2 0.8 collective-permute-start.16
  59.0 2.2 %collective-permute-done.12.refs_0_ = bf16[128,2048]{1,0:T(8,128)(2,1)S(1)} collective-permute-done((bf16[128,2048]{1,0:T(8,128)(2,1)S(1)}, bf16[128,2048]{1,0:T(8,128)(2,1)S(1)}, u32[]{:S(2)}, u32[]{:S(2)}) %collective-permute-start.12) | collective-permute-done | bytes 524320 | tf_op jit(solution)/shard_map/ppermute | solution.py:42
  61.2 3.3 %collective-permute-start.15 = (bf16[128,2048]{1,0:T(8,128)(2,1)S(1)}, bf16[128,2048]{1,0:T(8,128)(2,1)S(1)}, u32[]{:S(2)}, u32[]{:S(2)}) collective-permute-start(bf16[128,2048]{1,0:T(8,128)(2,1)S(1)} %stack.1.a_ref.refs_0_.refs_20_), channel_id=1, source_target_pairs={{0,64},{32,96},{64,0},{96,32},{128,192},{160,224},{192,128},{224,1... | collective-permute-start | bytes 1572872 | tf_op jit(solution)/shard_map/ppermute | solution.py:50
  64.5 6.2 %collective-permute-done.18.refs_0_ = bf16[128,2048]{1,0:T(8,128)(2,1)S(1)} collective-permute-done((bf16[128,2048]{1,0:T(8,128)(2,1)S(1)}, bf16[128,2048]{1,0:T(8,128)(2,1)S(1)}, u32[]{:S(2)}, u32[]{:S(2)}) %collective-permute-start.18) | collective-permute-done | bytes 524320 | tf_op jit(solution)/shard_map/ppermute | solution.py:42
  70.8 2.2 %collective-permute-done.16.refs_0_ = bf16[128,2048]{1,0:T(8,128)(2,1)S(1)} collective-permute-done((bf16[128,2048]{1,0:T(8,128)(2,1)S(1)}, bf16[128,2048]{1,0:T(8,128)(2,1)S(1)}, u32[]{:S(2)}, u32[]{:S(2)}) %collective-permute-start.16) | collective-permute-done | bytes 524320 | tf_op jit(solution)/shard_map/ppermute | solution.py:42
  73.0 0.2 collective-permute-done.15.refs_0_
  73.4 0.5 collective-permute-start.23
  73.9 0.7 norm.2
  74.6 0.6 encoder.1
  75.2 4.8 %collective-permute-done.19.refs_0_ = bf16[128,2048]{1,0:T(8,128)(2,1)S(1)} collective-permute-done((bf16[128,2048]{1,0:T(8,128)(2,1)S(1)}, bf16[128,2048]{1,0:T(8,128)(2,1)S(1)}, u32[]{:S(2)}, u32[]{:S(2)}) %collective-permute-start.19) | collective-permute-done | bytes 524320 | tf_op jit(solution)/shard_map/ppermute | solution.py:42
  80.0 1.4 collective-permute-done.21.refs_0_
  81.4 0.7 norm.3
  82.1 14.2 %attend.1 = (bf16[256,2048]{1,0:T(8,128)(2,1)S(1)}, bf16[256,2048]{1,0:T(8,128)(2,1)S(1)}, bf16[256,2048]{1,0:T(8,128)(2,1)S(1)}, bf16[272,2048]{1,0:T(8,128)(2,1)S(1)}, f32[1,2048]{1,0:T(1,128)S(1)}) custom-call(bf16[128,2048]{1,0:T(8,128)(2,1)S(1)} %unit.1.token_ref.refs_0_, bf16[128,2048]{1,0:T(8,128)(2,1)S(1)} %get-tuple-element.97.refs_1_, ...), custom_call_target="tpu_custom_call" | custom-call | flops 10000000000 | bytes 20000000 | tf_op jit(solution)/shard_map/attend/pallas_call | solution.py:337
  96.3 0.3 collective-permute-start.24
  96.6 0.5 collective-permute-start.25
  97.1 2.2 %collective-permute-done.24.got_ref = bf16[272,2048]{1,0:T(8,128)(2,1)S(1)} collective-permute-done((bf16[272,2048]{1,0:T(8,128)(2,1)S(1)}, bf16[272,2048]{1,0:T(8,128)(2,1)S(1)}, u32[]{:S(2)}, u32[]{:S(2)}) %collective-permute-start.24) | collective-permute-done | bytes 1114144 | tf_op jit(solution)/shard_map/ppermute | solution.py:42
  99.3 0.3 split.1
  99.7 1.7 %collective-permute-start.26 = (bf16[64,2048]{1,0:T(8,128)(2,1)S(1)}, bf16[64,2048]{1,0:T(8,128)(2,1)S(1)}, u32[]{:S(2)}, u32[]{:S(2)}) collective-permute-start(bf16[64,2048]{1,0:T(8,128)(2,1)S(1)} %get-tuple-element.155), channel_id=1, source_target_pairs={{0,32},{32,0},{64,96},{96,64},{128,160},{160,128},{192,224},{224,1... | collective-permute-start | bytes 786440 | tf_op jit(solution)/shard_map/ppermute | solution.py:50
  101.3 2.9 %collective-permute-start.27 = (bf16[64,2048]{1,0:T(8,128)(2,1)S(1)}, bf16[64,2048]{1,0:T(8,128)(2,1)S(1)}, u32[]{:S(2)}, u32[]{:S(2)}) collective-permute-start(bf16[64,2048]{1,0:T(8,128)(2,1)S(1)} %get-tuple-element.156), channel_id=1, source_target_pairs={{0,64},{32,96},{64,0},{96,32},{128,192},{160,224},{192,128},{224,1... | collective-permute-start | bytes 786440 | tf_op jit(solution)/shard_map/ppermute | solution.py:50
  104.2 0.2 collective-permute-start.28
  104.4 2.3 %collective-permute-start.31 = (f32[1,2048]{1,0:T(1,128)S(1)}, f32[1,2048]{1,0:T(1,128)S(1)}, u32[]{:S(2)}, u32[]{:S(2)}) collective-permute-start(f32[1,2048]{1,0:T(1,128)S(1)} %get-tuple-element.158.a_ref), channel_id=1, source_target_pairs={{0,6},{1,7},{2,4},{3,5},{4,2},{5,3},{6,0},{7,1},{8,14},{9,15},{10,... | collective-permute-start | bytes 24584 | tf_op jit(solution)/shard_map/ppermute | solution.py:42
  106.8 3.1 %collective-permute-done.31.d_ref = f32[1,2048]{1,0:T(1,128)S(1)} collective-permute-done((f32[1,2048]{1,0:T(1,128)S(1)}, f32[1,2048]{1,0:T(1,128)S(1)}, u32[]{:S(2)}, u32[]{:S(2)}) %collective-permute-start.31) | collective-permute-done | bytes 8224 | tf_op jit(solution)/shard_map/ppermute | solution.py:42
  109.9 1.4 collective-permute-done.30.c_ref
  111.3 2.2 %collective-permute-done.29.b_ref = f32[1,2048]{1,0:T(1,128)S(1)} collective-permute-done((f32[1,2048]{1,0:T(1,128)S(1)}, f32[1,2048]{1,0:T(1,128)S(1)}, u32[]{:S(2)}, u32[]{:S(2)}) %collective-permute-start.29) | collective-permute-done | bytes 8224 | tf_op jit(solution)/shard_map/ppermute | solution.py:42
  113.6 2.4 %collective-permute-start.32 = (f32[1,2048]{1,0:T(1,128)S(1)}, f32[1,2048]{1,0:T(1,128)S(1)}, u32[]{:S(2)}, u32[]{:S(2)}) collective-permute-start(f32[1,2048]{1,0:T(1,128)S(1)} %add.5.a_ref), channel_id=1, source_target_pairs={{0,8},{1,9},{2,10},{3,11},{4,12},{5,13},{6,14},{7,15},{8,0},{9,1},... | collective-permute-start | bytes 24584 | tf_op jit(solution)/shard_map/ppermute | solution.py:42
  116.0 5.1 %collective-permute-done.32.b_ref = f32[1,2048]{1,0:T(1,128)S(1)} collective-permute-done((f32[1,2048]{1,0:T(1,128)S(1)}, f32[1,2048]{1,0:T(1,128)S(1)}, u32[]{:S(2)}, u32[]{:S(2)}) %collective-permute-start.32) | collective-permute-done | bytes 8224 | tf_op jit(solution)/shard_map/ppermute | solution.py:42
  121.2 0.1 sum.1
  121.3 3.7 %collective-permute-start.33 = (bf16[64,2048]{1,0:T(8,128)(2,1)S(1)}, bf16[64,2048]{1,0:T(8,128)(2,1)S(1)}, u32[]{:S(2)}, u32[]{:S(2)}) collective-permute-start(bf16[64,2048]{1,0:T(8,128)(2,1)S(1)} %get-tuple-element.165), channel_id=1, source_target_pairs={{0,128},{32,160},{64,192},{96,224},{128,0},{160,32},{192,64},{224,... | collective-permute-start | bytes 786440 | tf_op jit(solution)/shard_map/ppermute | solution.py:50
  125.0 3.0 %collective-permute-start.36 = (f32[1,2048]{1,0:T(1,128)S(1)}, f32[1,2048]{1,0:T(1,128)S(1)}, u32[]{:S(2)}, u32[]{:S(2)}) collective-permute-start(f32[1,2048]{1,0:T(1,128)S(1)} %get-tuple-element.166.a_ref), channel_id=1, source_target_pairs={{0,96},{32,64},{64,32},{96,0},{128,224},{160,192},{192,160},{224,1... | collective-permute-start | bytes 24584 | tf_op jit(solution)/shard_map/ppermute | solution.py:50
  128.0 1.1 collective-permute-start.34
  129.1 0.8 collective-permute-done.36.d_ref
  129.9 3.5 %collective-permute-done.35.c_ref = f32[1,2048]{1,0:T(1,128)S(1)} collective-permute-done((f32[1,2048]{1,0:T(1,128)S(1)}, f32[1,2048]{1,0:T(1,128)S(1)}, u32[]{:S(2)}, u32[]{:S(2)}) %collective-permute-start.35) | collective-permute-done | bytes 8224 | tf_op jit(solution)/shard_map/ppermute | solution.py:50
  133.4 0.8 collective-permute-start.39
  134.2 1.4 collective-permute-start.38
  135.5 2.1 %collective-permute-start.37 = (bf16[64,2048]{1,0:T(8,128)(2,1)S(1)}, bf16[64,2048]{1,0:T(8,128)(2,1)S(1)}, u32[]{:S(2)}, u32[]{:S(2)}) collective-permute-start(bf16[64,2048]{1,0:T(8,128)(2,1)S(1)} %get-tuple-element.167.refs_0_), channel_id=1, source_target_pairs={{0,32},{32,0},{64,96},{96,64},{128,160},{160,128},{192,224},{224,1... | collective-permute-start | bytes 786440 | tf_op jit(solution)/shard_map/ppermute | solution.py:50
  137.6 3.6 %collective-permute-done.40.b_ref = f32[1,2048]{1,0:T(1,128)S(1)} collective-permute-done((f32[1,2048]{1,0:T(1,128)S(1)}, f32[1,2048]{1,0:T(1,128)S(1)}, u32[]{:S(2)}, u32[]{:S(2)}) %collective-permute-start.40) | collective-permute-done | bytes 8224 | tf_op jit(solution)/shard_map/ppermute | solution.py:42
  141.3 0.6 collective-permute-start.41
  141.9 1.1 rows.1
  143.0 3.4 %collective-permute-done.41.b_ref = f32[1,2048]{1,0:T(1,128)S(1)} collective-permute-done((f32[1,2048]{1,0:T(1,128)S(1)}, f32[1,2048]{1,0:T(1,128)S(1)}, u32[]{:S(2)}, u32[]{:S(2)}) %collective-permute-start.41) | collective-permute-done | bytes 8224 | tf_op jit(solution)/shard_map/ppermute | solution.py:50
  146.4 0.6 add.9
  147.0 1.1 grads.1
  (78 shorter events, 0.8 us)
Async XLA Ops:
  0.6 3.0 %copy-start = (bf16[1,256,2048]{2,1,0:T(8,128)(2,1)S(1)}, bf16[1,256,2048]{2,1,0:T(8,128)(2,1)}, u32[]{:S(2)}) copy-start(bf16[1,256,2048]{2,1,0:T(8,128)(2,1)} %param.5) | copy-start | bytes 3145732
  0.6 1.1 copy-start.3
  1.9 1.6 %collective-permute-start.1 = (bf16[64,2048]{1,0:T(8,128)(2,1)S(1)}, bf16[64,2048]{1,0:T(8,128)(2,1)S(1)}, u32[]{:S(2)}, u32[]{:S(2)}) collective-permute-start(bf16[64,2048]{1,0:T(8,128)(2,1)S(1)} %get-tuple-element.87), channel_id=1, source_target_pairs={{0,1},{1,0},{2,3},{3,2},{4,5},{5,4},{6,7},{7,6},{8,9},{9,8},{10,11... | collective-permute-start | bytes 786440 | tf_op jit(solution)/shard_map/ppermute | solution.py:42
  3.6 1.2 copy-start.1
  5.0 17.8 %collective-permute-start.4 = (bf16[256,2048]{1,0:T(8,128)(2,1)S(1)}, bf16[256,2048]{1,0:T(8,128)(2,1)S(1)}, u32[]{:S(2)}, u32[]{:S(2)}) collective-permute-start(bf16[256,2048]{1,0:T(8,128)(2,1)S(1)} %give.1), channel_id=1, source_target_pairs={{0,1},{1,0},{2,3},{3,2},{4,5},{5,4},{6,7},{7,6},{8,9},{9,8},{10,11... | collective-permute-start | bytes 3145736 | tf_op jit(solution)/shard_map/ppermute | solution.py:42
  5.2 17.6 %collective-permute-start.3 = (bf16[128,2048]{1,0:T(8,128)(2,1)S(1)}, bf16[128,2048]{1,0:T(8,128)(2,1)S(1)}, u32[]{:S(2)}, u32[]{:S(2)}) collective-permute-start(bf16[128,2048]{1,0:T(8,128)(2,1)S(1)} %unit.1.token_ref.refs_0_), channel_id=1, source_target_pairs={{0,14},{1,15},{2,0},{3,1},{4,2},{5,3},{6,4},{7,5},{8,6},{9,7},{10,... | collective-permute-start | bytes 1572872 | tf_op jit(solution)/shard_map/ppermute | solution.py:42
  11.0 15.4 %collective-permute-start.2 = (bf16[128,2048]{1,0:T(8,128)(2,1)S(1)}, bf16[128,2048]{1,0:T(8,128)(2,1)S(1)}, u32[]{:S(2)}, u32[]{:S(2)}) collective-permute-start(bf16[128,2048]{1,0:T(8,128)(2,1)S(1)} %unit.1.token_ref.refs_0_), channel_id=1, source_target_pairs={{0,2},{1,3},{2,4},{3,5},{4,6},{5,7},{6,8},{7,9},{8,10},{9,11},{10,... | collective-permute-start | bytes 1572872 | tf_op jit(solution)/shard_map/ppermute | solution.py:42
  11.1 15.5 %collective-permute-start = (bf16[128,2048]{1,0:T(8,128)(2,1)S(1)}, bf16[128,2048]{1,0:T(8,128)(2,1)S(1)}, u32[]{:S(2)}, u32[]{:S(2)}) collective-permute-start(bf16[128,2048]{1,0:T(8,128)(2,1)S(1)} %half.1), channel_id=1, source_target_pairs={{0,64},{32,96},{64,0},{96,32},{128,192},{160,224},{192,128},{224,1... | collective-permute-start | bytes 1572872 | tf_op jit(solution)/shard_map/ppermute | solution.py:50
  14.4 15.4 %collective-permute-start.6 = (bf16[128,2048]{1,0:T(8,128)(2,1)S(1)}, bf16[128,2048]{1,0:T(8,128)(2,1)S(1)}, u32[]{:S(2)}, u32[]{:S(2)}) collective-permute-start(bf16[128,2048]{1,0:T(8,128)(2,1)S(1)} %unit.1.token_ref.refs_0_), channel_id=1, source_target_pairs={{0,16},{1,17},{2,18},{3,19},{4,20},{5,21},{6,22},{7,23},{8,24},{9,... | collective-permute-start | bytes 1572872 | tf_op jit(solution)/shard_map/ppermute | solution.py:42
  22.8 3.9 %copy-start.5 = (s32[8]{0:T(128)S(1)}, s32[8]{0:T(128)}, u32[]{:S(2)}) copy-start(s32[8]{0:T(128)} %map_ref.7) | copy-start | bytes 100
  22.8 14.6 %collective-permute-start.10 = (bf16[128,2048]{1,0:T(8,128)(2,1)S(1)}, bf16[128,2048]{1,0:T(8,128)(2,1)S(1)}, u32[]{:S(2)}, u32[]{:S(2)}) collective-permute-start(bf16[128,2048]{1,0:T(8,128)(2,1)S(1)} %get-tuple-element.97.refs_1_), channel_id=1, source_target_pairs={{0,14},{1,15},{2,0},{3,1},{4,2},{5,3},{6,4},{7,5},{8,6},{9,7},{10,... | collective-permute-start | bytes 1572872 | tf_op jit(solution)/shard_map/ppermute | solution.py:42
  26.5 14.6 %collective-permute-start.9 = (bf16[128,2048]{1,0:T(8,128)(2,1)S(1)}, bf16[128,2048]{1,0:T(8,128)(2,1)S(1)}, u32[]{:S(2)}, u32[]{:S(2)}) collective-permute-start(bf16[128,2048]{1,0:T(8,128)(2,1)S(1)} %get-tuple-element.98.refs_2_), channel_id=1, source_target_pairs={{0,2},{1,3},{2,4},{3,5},{4,6},{5,7},{6,8},{7,9},{8,10},{9,11},{10,... | collective-permute-start | bytes 1572872 | tf_op jit(solution)/shard_map/ppermute | solution.py:42
  27.2 7.5 %collective-permute-start.5 = (bf16[64,2048]{1,0:T(8,128)(2,1)S(1)}, bf16[64,2048]{1,0:T(8,128)(2,1)S(1)}, u32[]{:S(2)}, u32[]{:S(2)}) collective-permute-start(bf16[64,2048]{1,0:T(8,128)(2,1)S(1)} %get-tuple-element.93), channel_id=1, source_target_pairs={{0,32},{32,0},{64,96},{96,64},{128,160},{160,128},{192,224},{224,1... | collective-permute-start | bytes 786440 | tf_op jit(solution)/shard_map/ppermute | solution.py:50
  28.9 14.2 %collective-permute-start.8 = (bf16[128,2048]{1,0:T(8,128)(2,1)S(1)}, bf16[128,2048]{1,0:T(8,128)(2,1)S(1)}, u32[]{:S(2)}, u32[]{:S(2)}) collective-permute-start(bf16[128,2048]{1,0:T(8,128)(2,1)S(1)} %get-tuple-element.97.refs_1_), channel_id=1, source_target_pairs={{0,16},{1,17},{2,18},{3,19},{4,20},{5,21},{6,22},{7,23},{8,24},{9,... | collective-permute-start | bytes 1572872 | tf_op jit(solution)/shard_map/ppermute | solution.py:42
  37.4 17.4 %collective-permute-start.14 = (bf16[128,2048]{1,0:T(8,128)(2,1)S(1)}, bf16[128,2048]{1,0:T(8,128)(2,1)S(1)}, u32[]{:S(2)}, u32[]{:S(2)}) collective-permute-start(bf16[128,2048]{1,0:T(8,128)(2,1)S(1)} %get-tuple-element.105.refs_4_), channel_id=1, source_target_pairs={{0,14},{1,15},{2,0},{3,1},{4,2},{5,3},{6,4},{7,5},{8,6},{9,7},{10,... | collective-permute-start | bytes 1572872 | tf_op jit(solution)/shard_map/ppermute | solution.py:42
  41.1 13.7 %collective-permute-start.13 = (bf16[128,2048]{1,0:T(8,128)(2,1)S(1)}, bf16[128,2048]{1,0:T(8,128)(2,1)S(1)}, u32[]{:S(2)}, u32[]{:S(2)}) collective-permute-start(bf16[128,2048]{1,0:T(8,128)(2,1)S(1)} %get-tuple-element.104.refs_5_), channel_id=1, source_target_pairs={{0,2},{1,3},{2,4},{3,5},{4,6},{5,7},{6,8},{7,9},{8,10},{9,11},{10,... | collective-permute-start | bytes 1572872 | tf_op jit(solution)/shard_map/ppermute | solution.py:42
  41.7 10.8 %collective-permute-start.7 = (bf16[64,2048]{1,0:T(8,128)(2,1)S(1)}, bf16[64,2048]{1,0:T(8,128)(2,1)S(1)}, u32[]{:S(2)}, u32[]{:S(2)}) collective-permute-start(bf16[64,2048]{1,0:T(8,128)(2,1)S(1)} %select.4.own_ref), channel_id=1, source_target_pairs={{0,128},{32,160},{64,192},{96,224},{128,0},{160,32},{192,64},{224,... | collective-permute-start | bytes 786440 | tf_op jit(solution)/shard_map/ppermute | solution.py:50
  43.1 18.0 %collective-permute-start.12 = (bf16[128,2048]{1,0:T(8,128)(2,1)S(1)}, bf16[128,2048]{1,0:T(8,128)(2,1)S(1)}, u32[]{:S(2)}, u32[]{:S(2)}) collective-permute-start(bf16[128,2048]{1,0:T(8,128)(2,1)S(1)} %get-tuple-element.104.refs_5_), channel_id=1, source_target_pairs={{0,16},{1,17},{2,18},{3,19},{4,20},{5,21},{6,22},{7,23},{8,24},{9,... | collective-permute-start | bytes 1572872 | tf_op jit(solution)/shard_map/ppermute | solution.py:42
  53.1 8.1 %collective-permute-start.11 = (bf16[64,2048]{1,0:T(8,128)(2,1)S(1)}, bf16[64,2048]{1,0:T(8,128)(2,1)S(1)}, u32[]{:S(2)}, u32[]{:S(2)}) collective-permute-start(bf16[64,2048]{1,0:T(8,128)(2,1)S(1)} %select.5.refs_0_), channel_id=1, source_target_pairs={{0,32},{32,0},{64,96},{96,64},{128,160},{160,128},{192,224},{224,1... | collective-permute-start | bytes 786440 | tf_op jit(solution)/shard_map/ppermute | solution.py:50
  54.8 15.9 %collective-permute-start.18 = (bf16[128,2048]{1,0:T(8,128)(2,1)S(1)}, bf16[128,2048]{1,0:T(8,128)(2,1)S(1)}, u32[]{:S(2)}, u32[]{:S(2)}) collective-permute-start(bf16[128,2048]{1,0:T(8,128)(2,1)S(1)} %get-tuple-element.111.refs_8_), channel_id=1, source_target_pairs={{0,2},{1,3},{2,4},{3,5},{4,6},{5,7},{6,8},{7,9},{8,10},{9,11},{10,... | collective-permute-start | bytes 1572872 | tf_op jit(solution)/shard_map/ppermute | solution.py:42
  54.8 15.8 %collective-permute-start.17 = (bf16[128,2048]{1,0:T(8,128)(2,1)S(1)}, bf16[128,2048]{1,0:T(8,128)(2,1)S(1)}, u32[]{:S(2)}, u32[]{:S(2)}) collective-permute-start(bf16[128,2048]{1,0:T(8,128)(2,1)S(1)} %get-tuple-element.112.refs_6_), channel_id=1, source_target_pairs={{0,14},{1,15},{2,0},{3,1},{4,2},{5,3},{6,4},{7,5},{8,6},{9,7},{10,... | collective-permute-start | bytes 1572872 | tf_op jit(solution)/shard_map/ppermute | solution.py:42
  58.2 14.9 %collective-permute-start.16 = (bf16[128,2048]{1,0:T(8,128)(2,1)S(1)}, bf16[128,2048]{1,0:T(8,128)(2,1)S(1)}, u32[]{:S(2)}, u32[]{:S(2)}) collective-permute-start(bf16[128,2048]{1,0:T(8,128)(2,1)S(1)} %get-tuple-element.111.refs_8_), channel_id=1, source_target_pairs={{0,16},{1,17},{2,18},{3,19},{4,20},{5,21},{6,22},{7,23},{8,24},{9,... | collective-permute-start | bytes 1572872 | tf_op jit(solution)/shard_map/ppermute | solution.py:42
  61.2 12.0 %collective-permute-start.15 = (bf16[128,2048]{1,0:T(8,128)(2,1)S(1)}, bf16[128,2048]{1,0:T(8,128)(2,1)S(1)}, u32[]{:S(2)}, u32[]{:S(2)}) collective-permute-start(bf16[128,2048]{1,0:T(8,128)(2,1)S(1)} %stack.1.a_ref.refs_0_.refs_20_), channel_id=1, source_target_pairs={{0,64},{32,96},{64,0},{96,32},{128,192},{160,224},{192,128},{224,1... | collective-permute-start | bytes 1572872 | tf_op jit(solution)/shard_map/ppermute | solution.py:50
  64.5 15.5 %collective-permute-start.20 = (bf16[128,2048]{1,0:T(8,128)(2,1)S(1)}, bf16[128,2048]{1,0:T(8,128)(2,1)S(1)}, u32[]{:S(2)}, u32[]{:S(2)}) collective-permute-start(bf16[128,2048]{1,0:T(8,128)(2,1)S(1)} %get-tuple-element.119.refs_3_), channel_id=1, source_target_pairs={{0,2},{1,3},{2,4},{3,5},{4,6},{5,7},{6,8},{7,9},{8,10},{9,11},{10,... | collective-permute-start | bytes 1572872 | tf_op jit(solution)/shard_map/ppermute | solution.py:42
  70.7 10.7 %collective-permute-start.21 = (bf16[128,2048]{1,0:T(8,128)(2,1)S(1)}, bf16[128,2048]{1,0:T(8,128)(2,1)S(1)}, u32[]{:S(2)}, u32[]{:S(2)}) collective-permute-start(bf16[128,2048]{1,0:T(8,128)(2,1)S(1)} %get-tuple-element.122.refs_10_), channel_id=1, source_target_pairs={{0,16},{1,17},{2,18},{3,19},{4,20},{5,21},{6,22},{7,23},{8,24},{9,... | collective-permute-start | bytes 1572872 | tf_op jit(solution)/shard_map/ppermute | solution.py:42
  70.7 3.2 %copy-start.4 = (f32[2048]{0:T(1024)S(1)}, f32[2048]{0:T(1024)}, u32[]{:S(2)}) copy-start(f32[2048]{0:T(1024)} %param.8) | copy-start | bytes 24580
  70.7 9.3 %collective-permute-start.19 = (bf16[128,2048]{1,0:T(8,128)(2,1)S(1)}, bf16[128,2048]{1,0:T(8,128)(2,1)S(1)}, u32[]{:S(2)}, u32[]{:S(2)}) collective-permute-start(bf16[128,2048]{1,0:T(8,128)(2,1)S(1)} %get-tuple-element.123.refs_11_), channel_id=1, source_target_pairs={{0,14},{1,15},{2,0},{3,1},{4,2},{5,3},{6,4},{7,5},{8,6},{9,7},{10,... | collective-permute-start | bytes 1572872 | tf_op jit(solution)/shard_map/ppermute | solution.py:42
  73.2 1.4 copy-start.2
  73.3 8.1 %collective-permute-start.22 = (bf16[128,2048]{1,0:T(8,128)(2,1)S(1)}, bf16[128,2048]{1,0:T(8,128)(2,1)S(1)}, u32[]{:S(2)}, u32[]{:S(2)}) collective-permute-start(bf16[128,2048]{1,0:T(8,128)(2,1)S(1)} %late.1), channel_id=1, source_target_pairs={{0,1},{1,0},{2,3},{3,2},{4,5},{5,4},{6,7},{7,6},{8,9},{9,8},{10,11... | collective-permute-start | bytes 1572872 | tf_op jit(solution)/shard_map/ppermute | solution.py:42
  73.4 8.0 %collective-permute-start.23 = (bf16[128,2048]{1,0:T(8,128)(2,1)S(1)}, bf16[128,2048]{1,0:T(8,128)(2,1)S(1)}, u32[]{:S(2)}, u32[]{:S(2)}) collective-permute-start(bf16[128,2048]{1,0:T(8,128)(2,1)S(1)} %get-tuple-element.117.b_ref.refs_1_.refs_21_), channel_id=1, source_target_pairs={{0,1},{1,0},{2,3},{3,2},{4,5},{5,4},{6,7},{7,6},{8,9},{9,8},{10,11... | collective-permute-start | bytes 1572872 | tf_op jit(solution)/shard_map/ppermute | solution.py:42
  96.3 3.1 %collective-permute-start.24 = (bf16[272,2048]{1,0:T(8,128)(2,1)S(1)}, bf16[272,2048]{1,0:T(8,128)(2,1)S(1)}, u32[]{:S(2)}, u32[]{:S(2)}) collective-permute-start(bf16[272,2048]{1,0:T(8,128)(2,1)S(1)} %get-tuple-element.148), channel_id=1, source_target_pairs={{0,1},{1,0},{2,3},{3,2},{4,5},{5,4},{6,7},{7,6},{8,9},{9,8},{10,11... | collective-permute-start | bytes 3342344 | tf_op jit(solution)/shard_map/ppermute | solution.py:42
  96.6 7.8 %collective-permute-start.25 = (bf16[256,2048]{1,0:T(8,128)(2,1)S(1)}, bf16[256,2048]{1,0:T(8,128)(2,1)S(1)}, u32[]{:S(2)}, u32[]{:S(2)}) collective-permute-start(bf16[256,2048]{1,0:T(8,128)(2,1)S(1)} %get-tuple-element.150), channel_id=1, source_target_pairs={{0,1},{1,0},{2,3},{3,2},{4,5},{5,4},{6,7},{7,6},{8,9},{9,8},{10,11... | collective-permute-start | bytes 3145736 | tf_op jit(solution)/shard_map/ppermute | solution.py:42
  99.7 21.5 %collective-permute-start.26 = (bf16[64,2048]{1,0:T(8,128)(2,1)S(1)}, bf16[64,2048]{1,0:T(8,128)(2,1)S(1)}, u32[]{:S(2)}, u32[]{:S(2)}) collective-permute-start(bf16[64,2048]{1,0:T(8,128)(2,1)S(1)} %get-tuple-element.155), channel_id=1, source_target_pairs={{0,32},{32,0},{64,96},{96,64},{128,160},{160,128},{192,224},{224,1... | collective-permute-start | bytes 786440 | tf_op jit(solution)/shard_map/ppermute | solution.py:50
  101.3 19.8 %collective-permute-start.27 = (bf16[64,2048]{1,0:T(8,128)(2,1)S(1)}, bf16[64,2048]{1,0:T(8,128)(2,1)S(1)}, u32[]{:S(2)}, u32[]{:S(2)}) collective-permute-start(bf16[64,2048]{1,0:T(8,128)(2,1)S(1)} %get-tuple-element.156), channel_id=1, source_target_pairs={{0,64},{32,96},{64,0},{96,32},{128,192},{160,224},{192,128},{224,1... | collective-permute-start | bytes 786440 | tf_op jit(solution)/shard_map/ppermute | solution.py:50
  104.2 16.9 %collective-permute-start.28 = (bf16[64,2048]{1,0:T(8,128)(2,1)S(1)}, bf16[64,2048]{1,0:T(8,128)(2,1)S(1)}, u32[]{:S(2)}, u32[]{:S(2)}) collective-permute-start(bf16[64,2048]{1,0:T(8,128)(2,1)S(1)} %get-tuple-element.157), channel_id=1, source_target_pairs={{0,96},{32,64},{64,32},{96,0},{128,224},{160,192},{192,160},{224,1... | collective-permute-start | bytes 786440 | tf_op jit(solution)/shard_map/ppermute | solution.py:50
  104.4 5.4 %collective-permute-start.31 = (f32[1,2048]{1,0:T(1,128)S(1)}, f32[1,2048]{1,0:T(1,128)S(1)}, u32[]{:S(2)}, u32[]{:S(2)}) collective-permute-start(f32[1,2048]{1,0:T(1,128)S(1)} %get-tuple-element.158.a_ref), channel_id=1, source_target_pairs={{0,6},{1,7},{2,4},{3,5},{4,2},{5,3},{6,0},{7,1},{8,14},{9,15},{10,... | collective-permute-start | bytes 24584 | tf_op jit(solution)/shard_map/ppermute | solution.py:42
  106.8 4.5 %collective-permute-start.30 = (f32[1,2048]{1,0:T(1,128)S(1)}, f32[1,2048]{1,0:T(1,128)S(1)}, u32[]{:S(2)}, u32[]{:S(2)}) collective-permute-start(f32[1,2048]{1,0:T(1,128)S(1)} %get-tuple-element.158.a_ref), channel_id=1, source_target_pairs={{0,4},{1,5},{2,6},{3,7},{4,0},{5,1},{6,2},{7,3},{8,12},{9,13},{10,... | collective-permute-start | bytes 24584 | tf_op jit(solution)/shard_map/ppermute | solution.py:42
  109.9 3.7 %collective-permute-start.29 = (f32[1,2048]{1,0:T(1,128)S(1)}, f32[1,2048]{1,0:T(1,128)S(1)}, u32[]{:S(2)}, u32[]{:S(2)}) collective-permute-start(f32[1,2048]{1,0:T(1,128)S(1)} %get-tuple-element.158.a_ref), channel_id=1, source_target_pairs={{0,2},{1,3},{2,0},{3,1},{4,6},{5,7},{6,4},{7,5},{8,10},{9,11},{10,... | collective-permute-start | bytes 24584 | tf_op jit(solution)/shard_map/ppermute | solution.py:42
  113.6 7.6 %collective-permute-start.32 = (f32[1,2048]{1,0:T(1,128)S(1)}, f32[1,2048]{1,0:T(1,128)S(1)}, u32[]{:S(2)}, u32[]{:S(2)}) collective-permute-start(f32[1,2048]{1,0:T(1,128)S(1)} %add.5.a_ref), channel_id=1, source_target_pairs={{0,8},{1,9},{2,10},{3,11},{4,12},{5,13},{6,14},{7,15},{8,0},{9,1},... | collective-permute-start | bytes 24584 | tf_op jit(solution)/shard_map/ppermute | solution.py:42
  121.3 12.1 %collective-permute-start.33 = (bf16[64,2048]{1,0:T(8,128)(2,1)S(1)}, bf16[64,2048]{1,0:T(8,128)(2,1)S(1)}, u32[]{:S(2)}, u32[]{:S(2)}) collective-permute-start(bf16[64,2048]{1,0:T(8,128)(2,1)S(1)} %get-tuple-element.165), channel_id=1, source_target_pairs={{0,128},{32,160},{64,192},{96,224},{128,0},{160,32},{192,64},{224,... | collective-permute-start | bytes 786440 | tf_op jit(solution)/shard_map/ppermute | solution.py:50
  125.0 4.9 %collective-permute-start.36 = (f32[1,2048]{1,0:T(1,128)S(1)}, f32[1,2048]{1,0:T(1,128)S(1)}, u32[]{:S(2)}, u32[]{:S(2)}) collective-permute-start(f32[1,2048]{1,0:T(1,128)S(1)} %get-tuple-element.166.a_ref), channel_id=1, source_target_pairs={{0,96},{32,64},{64,32},{96,0},{128,224},{160,192},{192,160},{224,1... | collective-permute-start | bytes 24584 | tf_op jit(solution)/shard_map/ppermute | solution.py:50
  128.0 5.3 %collective-permute-start.35 = (f32[1,2048]{1,0:T(1,128)S(1)}, f32[1,2048]{1,0:T(1,128)S(1)}, u32[]{:S(2)}, u32[]{:S(2)}) collective-permute-start(f32[1,2048]{1,0:T(1,128)S(1)} %get-tuple-element.166.a_ref), channel_id=1, source_target_pairs={{0,64},{32,96},{64,0},{96,32},{128,192},{160,224},{192,128},{224,1... | collective-permute-start | bytes 24584 | tf_op jit(solution)/shard_map/ppermute | solution.py:50
  128.0 5.3 %collective-permute-start.34 = (f32[1,2048]{1,0:T(1,128)S(1)}, f32[1,2048]{1,0:T(1,128)S(1)}, u32[]{:S(2)}, u32[]{:S(2)}) collective-permute-start(f32[1,2048]{1,0:T(1,128)S(1)} %get-tuple-element.166.a_ref), channel_id=1, source_target_pairs={{0,32},{32,0},{64,96},{96,64},{128,160},{160,128},{192,224},{224,1... | collective-permute-start | bytes 24584 | tf_op jit(solution)/shard_map/ppermute | solution.py:50
  133.4 13.6 %collective-permute-start.39 = (bf16[64,2048]{1,0:T(8,128)(2,1)S(1)}, bf16[64,2048]{1,0:T(8,128)(2,1)S(1)}, u32[]{:S(2)}, u32[]{:S(2)}) collective-permute-start(bf16[64,2048]{1,0:T(8,128)(2,1)S(1)} %get-tuple-element.167.refs_0_), channel_id=1, source_target_pairs={{0,96},{32,64},{64,32},{96,0},{128,224},{160,192},{192,160},{224,1... | collective-permute-start | bytes 786440 | tf_op jit(solution)/shard_map/ppermute | solution.py:50
  134.2 12.8 %collective-permute-start.38 = (bf16[64,2048]{1,0:T(8,128)(2,1)S(1)}, bf16[64,2048]{1,0:T(8,128)(2,1)S(1)}, u32[]{:S(2)}, u32[]{:S(2)}) collective-permute-start(bf16[64,2048]{1,0:T(8,128)(2,1)S(1)} %get-tuple-element.167.refs_0_), channel_id=1, source_target_pairs={{0,64},{32,96},{64,0},{96,32},{128,192},{160,224},{192,128},{224,1... | collective-permute-start | bytes 786440 | tf_op jit(solution)/shard_map/ppermute | solution.py:50
  135.5 11.5 %collective-permute-start.37 = (bf16[64,2048]{1,0:T(8,128)(2,1)S(1)}, bf16[64,2048]{1,0:T(8,128)(2,1)S(1)}, u32[]{:S(2)}, u32[]{:S(2)}) collective-permute-start(bf16[64,2048]{1,0:T(8,128)(2,1)S(1)} %get-tuple-element.167.refs_0_), channel_id=1, source_target_pairs={{0,32},{32,0},{64,96},{96,64},{128,160},{160,128},{192,224},{224,1... | collective-permute-start | bytes 786440 | tf_op jit(solution)/shard_map/ppermute | solution.py:50
  137.6 3.7 %collective-permute-start.40 = (f32[1,2048]{1,0:T(1,128)S(1)}, f32[1,2048]{1,0:T(1,128)S(1)}, u32[]{:S(2)}, u32[]{:S(2)}) collective-permute-start(f32[1,2048]{1,0:T(1,128)S(1)} %get-tuple-element.168.a_ref), channel_id=1, source_target_pairs={{0,16},{1,17},{2,18},{3,19},{4,20},{5,21},{6,22},{7,23},{8,24},{9,... | collective-permute-start | bytes 24584 | tf_op jit(solution)/shard_map/ppermute | solution.py:42
  141.3 5.2 %collective-permute-start.41 = (f32[1,2048]{1,0:T(1,128)S(1)}, f32[1,2048]{1,0:T(1,128)S(1)}, u32[]{:S(2)}, u32[]{:S(2)}) collective-permute-start(f32[1,2048]{1,0:T(1,128)S(1)} %add.8.a_ref), channel_id=1, source_target_pairs={{0,128},{32,160},{64,192},{96,224},{128,0},{160,32},{192,64},{224,... | collective-permute-start | bytes 24584 | tf_op jit(solution)/shard_map/ppermute | solution.py:50
